TPU v7x, 128 devices: a whole 4x4x4 slice. The times are simulated.
128 devices in a mesh: dp: 32 (over x, z, y_hi), tensor: 4 (over y_lo, core).
Axes of the slice: x: 4, y: 4 (y_hi: 2, y_lo: 2; y = y_hi * 2 + y_lo), z: 4, core: 2. Of those that a mesh axis runs over, the one named last changes fastest.
Arguments:
- tokens: bfloat16 [16384, 2048], P(('dp', 'tensor')), may hold values from -6 to 6
- group_length: int32 [32], P('dp'), may hold values from 385 to 512, as said below
- forget_rate: float32 [8], P('tensor'), may hold values from 0.00048828125 to 0.05
- mixer_gain: float32 [2048], replicated, may hold values from 0.1 to 1.9
- feed_gain: float32 [2048], replicated, may hold values from 0.1 to 1.9
- group_gain: float32 [3456], P('tensor'), may hold values from 0.1 to 1.9
- w_query: bfloat16 [2048, 2048], P('dp', 'tensor'), may hold values from -0.125 to 0.125
- w_key: bfloat16 [2048, 2048], P('dp', 'tensor'), may hold values from -0.125 to 0.125
- w_value: bfloat16 [2048, 3456], P('dp', 'tensor'), may hold values from -0.125 to 0.125
- w_swish: bfloat16 [2048, 3456], P('dp', 'tensor'), may hold values from -0.125 to 0.125
- w_output: bfloat16 [3456, 2048], P('tensor', 'dp'), may hold values from -0.109375 to 0.109375
- w_gelu: bfloat16 [2048, 3456], P('dp', 'tensor'), may hold values from -0.125 to 0.125
- w_linear: bfloat16 [2048, 3456], P('dp', 'tensor'), may hold values from -0.125 to 0.125
- w_down: bfloat16 [3456, 2048], P('tensor', 'dp'), may hold values from -0.109375 to 0.109375
- cotangent: bfloat16 [16384, 2048], P(('dp', 'tensor')), may hold values from -6 to 6
Outputs:
- result: bfloat16 [16384, 2048], P(('dp', 'tensor'))
- grad_tokens: bfloat16 [16384, 2048], P(('dp', 'tensor'))
- grad_mixer_gain: float32 [2048], replicated
- grad_feed_gain: float32 [2048], replicated
- grad_group_gain: float32 [3456], P('tensor')
- grad_query: float32 [2048, 2048], P('dp', 'tensor')
- grad_key: float32 [2048, 2048], P('dp', 'tensor')
- grad_value: float32 [2048, 3456], P('dp', 'tensor')
- grad_swish: float32 [2048, 3456], P('dp', 'tensor')
- grad_output: float32 [3456, 2048], P('tensor', 'dp')
- grad_gelu: float32 [2048, 3456], P('dp', 'tensor')
- grad_linear: float32 [2048, 3456], P('dp', 'tensor')
- grad_down: float32 [3456, 2048], P('tensor', 'dp')
Inputs may be any that keep to these rules, and one draw needn't show every extreme that they name: The first group_length[g] rows of data group g form one sequence, the other rows are padding; some group fills all 512 rows.
All inputs are finite; a program needn't handle non-finite values.
Results may differ from a plain program's by a relative error of at most 0.03.
Values may be sent and summed in bfloat16 or wider, within the bound.
No kernel may reach another device: no remote copies, remote signals or barrier semaphores. Data moves between devices by JAX's collectives and lax.ppermute only.
A program may use at most 192 MiB of HBM per device.

v0:
```python
import jax
import jax.numpy as jnp
from jax import lax
from jax.sharding import PartitionSpec as P

norm_eps = 1e-05
group_eps = 1.0
contract_rows = (((0,), (0,)), ((), ()))
contract_cols = (((1,), (1,)), ((), ()))


def rms_scale(row_data, gain_vec):
    return (
        row_data
        * lax.rsqrt(jnp.mean(row_data * row_data, axis=-1, keepdims=True) + norm_eps)
        * gain_vec
    )


def group_gate(retained, gate_pre, gain_vec):
    center = retained - jnp.mean(retained, axis=-1, keepdims=True)
    spread = jnp.mean(center * center, axis=-1, keepdims=True)
    normed = (center * lax.rsqrt(spread + group_eps)).reshape(gate_pre.shape)
    return jax.nn.silu(gate_pre) * normed * gain_vec


def gelu_mix(left_in, right_in):
    return jax.nn.gelu(left_in, approximate=False) * right_in


def decay_mask(log_keep, first_row, query_rows, key_count):
    row_ids = first_row + lax.broadcasted_iota(jnp.int32, (query_rows, key_count), 0)
    col_ids = lax.broadcasted_iota(jnp.int32, (query_rows, key_count), 1)
    offset_rows = row_ids - col_ids
    distance = jnp.maximum(offset_rows, 0).astype(jnp.float32)
    return jnp.where(offset_rows[None] >= 0, jnp.exp(distance[None] * log_keep[:, None, None]), 0.0)


def block_weights(query_block, key_rows, log_keep, first_row, score_scale):
    raw_scores = jnp.einsum(
        "ihd,jhd->hij", query_block, key_rows, preferred_element_type=jnp.float32
    )
    weighting = decay_mask(log_keep, first_row, query_block.shape[0], key_rows.shape[0])
    return (raw_scores * score_scale * weighting, weighting)


def retention_forward(queries, key_rows, values, log_keep, block_rows, score_scale):
    row_total = queries.shape[0]
    block_count = row_total // block_rows
    blocks = queries.reshape((block_count, block_rows) + queries.shape[1:])
    starts = jnp.arange(block_count, dtype=jnp.int32) * block_rows

    def one_block(carried, item_pair):
        query_block, first_row = item_pair
        weights, weighting = block_weights(query_block, key_rows, log_keep, first_row, score_scale)
        block_out = jnp.einsum(
            "hij,jhe->ihe", weights.astype(jnp.bfloat16), values, preferred_element_type=jnp.float32
        )
        return (carried, block_out)

    unused, outputs = lax.scan(one_block, 0, (blocks, starts))
    return outputs.reshape((row_total,) + outputs.shape[2:])


def retention_backward(queries, key_rows, values, grad_out, log_keep, block_rows, score_scale):
    row_total = queries.shape[0]
    block_count = row_total // block_rows
    blocks = queries.reshape((block_count, block_rows) + queries.shape[1:])
    grad_blocks = grad_out.reshape((block_count, block_rows) + grad_out.shape[1:])
    starts = jnp.arange(block_count, dtype=jnp.int32) * block_rows

    def one_block(carried, item_triple):
        grad_keys, grad_values = carried
        query_block, grad_block, first_row = item_triple
        weights, weighting = block_weights(query_block, key_rows, log_keep, first_row, score_scale)
        grad_weights = jnp.einsum(
            "ihe,jhe->hij", grad_block, values, preferred_element_type=jnp.float32
        )
        grad_scores = (grad_weights * score_scale * weighting).astype(jnp.bfloat16)
        grad_query_block = jnp.einsum(
            "hij,jhd->ihd", grad_scores, key_rows, preferred_element_type=jnp.float32
        )
        grad_keys = grad_keys + jnp.einsum(
            "hij,ihd->jhd", grad_scores, query_block, preferred_element_type=jnp.float32
        )
        grad_values = grad_values + jnp.einsum(
            "hij,ihe->jhe",
            weights.astype(jnp.bfloat16),
            grad_block,
            preferred_element_type=jnp.float32,
        )
        return ((grad_keys, grad_values), grad_query_block)

    initial = (jnp.zeros(key_rows.shape, jnp.float32), jnp.zeros(values.shape, jnp.float32))
    (grad_keys, grad_values), grad_queries = lax.scan(
        one_block, initial, (blocks, grad_blocks, starts)
    )
    return (grad_queries.reshape(queries.shape), grad_keys, grad_values)


def shards(
    tokens,
    group_length,
    forget_rate,
    mixer_gain,
    feed_gain,
    group_gain,
    w_query,
    w_key,
    w_value,
    w_swish,
    w_output,
    w_gelu,
    w_linear,
    w_down,
    cotangent,
):
    tensor_size = lax.axis_size("tensor")
    local_rows = tokens.shape[0]
    group_rows = local_rows * tensor_size
    local_heads = forget_rate.shape[0]
    key_width = w_query.shape[1] // local_heads
    value_width = w_value.shape[1] // local_heads
    value_local = w_value.shape[1]
    block_rows = min(512, group_rows)
    score_scale = key_width ** (-0.5)
    log_keep = jnp.log1p(-forget_rate)
    position = lax.axis_index("tensor") * local_rows + lax.broadcasted_iota(
        jnp.int32, (local_rows, 1), 0
    )
    valid_rows = (position < group_length[0]).astype(jnp.float32)
    query_full, key_full, value_full, swish_full, output_full, gelu_full, linear_full, down_full = (
        lax.all_gather(w_query, "dp", axis=0, tiled=True),
        lax.all_gather(w_key, "dp", axis=0, tiled=True),
        lax.all_gather(w_value, "dp", axis=0, tiled=True),
        lax.all_gather(w_swish, "dp", axis=0, tiled=True),
        lax.all_gather(w_output, "dp", axis=1, tiled=True),
        lax.all_gather(w_gelu, "dp", axis=0, tiled=True),
        lax.all_gather(w_linear, "dp", axis=0, tiled=True),
        lax.all_gather(w_down, "dp", axis=1, tiled=True),
    )
    token_float = tokens.astype(jnp.float32)
    normed_in = rms_scale(token_float, mixer_gain).astype(jnp.bfloat16)
    normed_group = lax.all_gather(normed_in, "tensor", axis=0, tiled=True)
    queries = (
        jnp.dot(normed_group, query_full, preferred_element_type=jnp.float32)
        .astype(jnp.bfloat16)
        .reshape(group_rows, local_heads, key_width)
    )
    key_rows = (
        jnp.dot(normed_group, key_full, preferred_element_type=jnp.float32)
        .astype(jnp.bfloat16)
        .reshape(group_rows, local_heads, key_width)
    )
    values = (
        jnp.dot(normed_group, value_full, preferred_element_type=jnp.float32)
        .astype(jnp.bfloat16)
        .reshape(group_rows, local_heads, value_width)
    )
    gate_pre = jnp.dot(normed_group, swish_full, preferred_element_type=jnp.float32)
    retained = retention_forward(queries, key_rows, values, log_keep, block_rows, score_scale)
    mixed_low = group_gate(retained, gate_pre, group_gain).astype(jnp.bfloat16)
    mixer_out = lax.psum_scatter(
        jnp.dot(mixed_low, output_full, preferred_element_type=jnp.float32).astype(jnp.bfloat16),
        "tensor",
        scatter_dimension=0,
        tiled=True,
    ).astype(jnp.float32)
    middle = token_float + valid_rows * mixer_out
    normed_mid = rms_scale(middle, feed_gain).astype(jnp.bfloat16)
    mid_group = lax.all_gather(normed_mid, "tensor", axis=0, tiled=True)
    gelu_in = jnp.dot(mid_group, gelu_full, preferred_element_type=jnp.float32)
    linear_in = jnp.dot(mid_group, linear_full, preferred_element_type=jnp.float32)
    hidden = gelu_mix(gelu_in, linear_in).astype(jnp.bfloat16)
    feed_out = lax.psum_scatter(
        jnp.dot(hidden, down_full, preferred_element_type=jnp.float32).astype(jnp.bfloat16),
        "tensor",
        scatter_dimension=0,
        tiled=True,
    ).astype(jnp.float32)
    result = (middle + valid_rows * feed_out).astype(jnp.bfloat16)
    query_back, key_back, value_back, swish_back, output_back, gelu_back, linear_back, down_back = (
        lax.all_gather(w_query, "dp", axis=0, tiled=True),
        lax.all_gather(w_key, "dp", axis=0, tiled=True),
        lax.all_gather(w_value, "dp", axis=0, tiled=True),
        lax.all_gather(w_swish, "dp", axis=0, tiled=True),
        lax.all_gather(w_output, "dp", axis=1, tiled=True),
        lax.all_gather(w_gelu, "dp", axis=0, tiled=True),
        lax.all_gather(w_linear, "dp", axis=0, tiled=True),
        lax.all_gather(w_down, "dp", axis=1, tiled=True),
    )
    grad_result = cotangent.astype(jnp.float32)
    grad_feed_out = (valid_rows * grad_result).astype(jnp.bfloat16)
    grad_feed_group = lax.all_gather(grad_feed_out, "tensor", axis=0, tiled=True)
    grad_hidden = lax.dot_general(
        grad_feed_group, down_back, contract_cols, preferred_element_type=jnp.float32
    )
    grad_down = lax.dot_general(
        hidden, grad_feed_group, contract_rows, preferred_element_type=jnp.float32
    )
    unused, gelu_pull = jax.vjp(gelu_mix, gelu_in, linear_in)
    grad_gelu_in, grad_linear_in = gelu_pull(grad_hidden)
    grad_gelu_in = grad_gelu_in.astype(jnp.bfloat16)
    grad_linear_in = grad_linear_in.astype(jnp.bfloat16)
    grad_gelu = lax.dot_general(
        mid_group, grad_gelu_in, contract_rows, preferred_element_type=jnp.float32
    )
    grad_linear = lax.dot_general(
        mid_group, grad_linear_in, contract_rows, preferred_element_type=jnp.float32
    )
    feed_sums = (grad_gelu, grad_linear, grad_down)
    grad_normed_mid = lax.psum_scatter(
        (
            lax.dot_general(
                grad_gelu_in, gelu_back, contract_cols, preferred_element_type=jnp.float32
            )
            + lax.dot_general(
                grad_linear_in, linear_back, contract_cols, preferred_element_type=jnp.float32
            )
        ).astype(jnp.bfloat16),
        "tensor",
        scatter_dimension=0,
        tiled=True,
    ).astype(jnp.float32)
    unused, mid_pull = jax.vjp(rms_scale, middle, feed_gain)
    grad_mid_part, grad_feed_gain = mid_pull(grad_normed_mid)
    grad_middle = grad_result + grad_mid_part
    grad_mixer_out = (valid_rows * grad_middle).astype(jnp.bfloat16)
    grad_mixer_group = lax.all_gather(grad_mixer_out, "tensor", axis=0, tiled=True)
    grad_mixed = lax.dot_general(
        grad_mixer_group, output_back, contract_cols, preferred_element_type=jnp.float32
    )
    grad_output = lax.dot_general(
        mixed_low, grad_mixer_group, contract_rows, preferred_element_type=jnp.float32
    )
    unused, gate_pull = jax.vjp(group_gate, retained, gate_pre, group_gain)
    grad_retained, grad_gate_pre, grad_group_part = gate_pull(grad_mixed)
    grad_retained = grad_retained.astype(jnp.bfloat16)
    grad_gate_pre = grad_gate_pre.astype(jnp.bfloat16)
    grad_queries, grad_keys, grad_values = retention_backward(
        queries, key_rows, values, grad_retained, log_keep, block_rows, score_scale
    )
    grad_queries = grad_queries.astype(jnp.bfloat16).reshape(group_rows, local_heads * key_width)
    grad_keys = grad_keys.astype(jnp.bfloat16).reshape(group_rows, local_heads * key_width)
    grad_values = grad_values.astype(jnp.bfloat16).reshape(group_rows, value_local)
    grad_query = lax.dot_general(
        normed_group, grad_queries, contract_rows, preferred_element_type=jnp.float32
    )
    grad_key = lax.dot_general(
        normed_group, grad_keys, contract_rows, preferred_element_type=jnp.float32
    )
    grad_value = lax.dot_general(
        normed_group, grad_values, contract_rows, preferred_element_type=jnp.float32
    )
    grad_swish = lax.dot_general(
        normed_group, grad_gate_pre, contract_rows, preferred_element_type=jnp.float32
    )
    summed = lax.dot_general(
        grad_queries, query_back, contract_cols, preferred_element_type=jnp.float32
    )
    summed = summed + lax.dot_general(
        grad_keys, key_back, contract_cols, preferred_element_type=jnp.float32
    )
    summed = summed + lax.dot_general(
        grad_values, value_back, contract_cols, preferred_element_type=jnp.float32
    )
    grad_normed_in = lax.psum_scatter(
        (
            summed
            + lax.dot_general(
                grad_gate_pre, swish_back, contract_cols, preferred_element_type=jnp.float32
            )
        ).astype(jnp.bfloat16),
        "tensor",
        scatter_dimension=0,
        tiled=True,
    ).astype(jnp.float32)
    unused, token_pull = jax.vjp(rms_scale, token_float, mixer_gain)
    grad_token_part, grad_mixer_gain = token_pull(grad_normed_in)
    grad_tokens = (grad_middle + grad_token_part).astype(jnp.bfloat16)
    group_place = lax.axis_index("tensor") * value_local
    group_full = lax.dynamic_update_slice(
        jnp.zeros((value_local * tensor_size,), jnp.float32), grad_group_part, (group_place,)
    )
    mixer_sum, feed_sum, group_sum = lax.psum(
        (grad_mixer_gain, grad_feed_gain, group_full), ("dp", "tensor")
    )
    group_own = lax.dynamic_slice_in_dim(group_sum, group_place, value_local, 0)
    summed_all = (
        lax.psum_scatter(
            grad_query.astype(jnp.bfloat16), "dp", scatter_dimension=0, tiled=True
        ).astype(jnp.float32),
        lax.psum_scatter(
            grad_key.astype(jnp.bfloat16), "dp", scatter_dimension=0, tiled=True
        ).astype(jnp.float32),
        lax.psum_scatter(
            grad_value.astype(jnp.bfloat16), "dp", scatter_dimension=0, tiled=True
        ).astype(jnp.float32),
        lax.psum_scatter(
            grad_swish.astype(jnp.bfloat16), "dp", scatter_dimension=0, tiled=True
        ).astype(jnp.float32),
        lax.psum_scatter(
            grad_output.astype(jnp.bfloat16), "dp", scatter_dimension=1, tiled=True
        ).astype(jnp.float32),
        lax.psum_scatter(
            feed_sums[0].astype(jnp.bfloat16), "dp", scatter_dimension=0, tiled=True
        ).astype(jnp.float32),
        lax.psum_scatter(
            feed_sums[1].astype(jnp.bfloat16), "dp", scatter_dimension=0, tiled=True
        ).astype(jnp.float32),
        lax.psum_scatter(
            feed_sums[2].astype(jnp.bfloat16), "dp", scatter_dimension=1, tiled=True
        ).astype(jnp.float32),
    )
    return (
        result,
        grad_tokens,
        mixer_sum,
        feed_sum,
        group_own,
        summed_all[0],
        summed_all[1],
        summed_all[2],
        summed_all[3],
        summed_all[4],
        summed_all[5],
        summed_all[6],
        summed_all[7],
    )


def solution(mesh):
    return jax.shard_map(
        shards,
        mesh=mesh,
        in_specs=(
            P(("dp", "tensor"), None),
            P("dp"),
            P("tensor"),
            P(),
            P(),
            P("tensor"),
            P("dp", "tensor"),
            P("dp", "tensor"),
            P("dp", "tensor"),
            P("dp", "tensor"),
            P("tensor", "dp"),
            P("dp", "tensor"),
            P("dp", "tensor"),
            P("tensor", "dp"),
            P(("dp", "tensor"), None),
        ),
        out_specs=(
            P(("dp", "tensor"), None),
            P(("dp", "tensor"), None),
            P(),
            P(),
            P("tensor"),
            P("dp", "tensor"),
            P("dp", "tensor"),
            P("dp", "tensor"),
            P("dp", "tensor"),
            P("tensor", "dp"),
            P("dp", "tensor"),
            P("dp", "tensor"),
            P("tensor", "dp"),
        ),
        check_vma=False,
    )
```

profile of v0, /device:TPU:0, one launch (start us, length us, event | category | flops | bytes accessed | tf_op | source)
XLA Modules:
  0.0 2405.8 jit_solution(8086462261223123439)
XLA Ops:
  14.1 28.0 %all-gather.13.cloned.1.call-done = bf16[512,2048]{1,0:T(8,128)(2,1)} async-done(((bf16[128,2048]{1,0:T(8,128)(2,1)}), bf16[512,2048]{1,0:T(8,128)(2,1)}) %all-gather.13.cloned.1.call-update) | async-done | bytes 2097168 | tf_op jit(solution)/shard_map/all_gather | solution.py:144
  42.1 75.0 %all-gather.19.cloned.1.call-done = bf16[2048,512]{1,0:T(8,128)(2,1)} async-done(((bf16[64,512]{1,0:T(8,128)(2,1)}), bf16[2048,512]{1,0:T(8,128)(2,1)}) %all-gather.19.cloned.1.call-update) | async-done | bytes 2097168 | tf_op jit(solution)/shard_map/all_gather | solution.py:133
  120.6 67.2 %all-gather.21.cloned.1.call-done = bf16[2048,512]{1,0:T(8,128)(2,1)} async-done(((bf16[64,512]{1,0:T(8,128)(2,1)}), bf16[2048,512]{1,0:T(8,128)(2,1)}) %all-gather.21.cloned.1.call-update) | async-done | bytes 2097168 | tf_op jit(solution)/shard_map/all_gather | solution.py:134
  192.9 71.9 %all-gather.17.cloned.1.call-done = bf16[2048,864]{1,0:T(8,128)(2,1)} async-done(((bf16[64,864]{1,0:T(8,128)(2,1)}), bf16[2048,864]{1,0:T(8,128)(2,1)}) %all-gather.17.cloned.1.call-update) | async-done | bytes 3538960 | tf_op jit(solution)/shard_map/all_gather | solution.py:135
  272.2 70.7 %all-gather.15.cloned.1.call-done = bf16[2048,864]{1,0:T(8,128)(2,1)} async-done(((bf16[64,864]{1,0:T(8,128)(2,1)}), bf16[2048,864]{1,0:T(8,128)(2,1)}) %all-gather.15.cloned.1.call-update) | async-done | bytes 3538960 | tf_op jit(solution)/shard_map/all_gather | solution.py:136
  350.1 70.8 %all-gather.23.cloned.1.call-done = bf16[864,2048]{0,1:T(8,128)(2,1)} async-done(((bf16[864,64]{0,1:T(8,128)(2,1)}), bf16[864,2048]{0,1:T(8,128)(2,1)}) %all-gather.23.cloned.1.call-update) | async-done | bytes 3538960 | tf_op jit(solution)/shard_map/all_gather | solution.py:137
  429.0 24.6 %reduce-scatter.13.cloned.1.call-done = bf16[128,2048]{1,0:T(8,128)(2,1)} async-done(((bf16[512,2048]{1,0:T(8,128)(2,1)}), bf16[128,2048]{1,0:T(8,128)(2,1)}) %reduce-scatter.13.cloned.1.call-update) | async-done | bytes 524304 | tf_op jit(solution)/shard_map/reduce_scatter | solution.py:163
  459.8 75.7 %all-gather.27.cloned.1.call-done = bf16[2048,864]{1,0:T(8,128)(2,1)} async-done(((bf16[64,864]{1,0:T(8,128)(2,1)}), bf16[2048,864]{1,0:T(8,128)(2,1)}) %all-gather.27.cloned.1.call-update) | async-done | bytes 3538960 | tf_op jit(solution)/shard_map/all_gather | solution.py:138
  535.5 29.0 %all-gather.25.cloned.1.call-done = bf16[512,2048]{1,0:T(8,128)(2,1)} async-done(((bf16[128,2048]{1,0:T(8,128)(2,1)}), bf16[512,2048]{1,0:T(8,128)(2,1)}) %all-gather.25.cloned.1.call-update) | async-done | bytes 2097168 | tf_op jit(solution)/shard_map/all_gather | solution.py:171
  570.5 75.9 %all-gather.31.cloned.1.call-done = bf16[864,2048]{0,1:T(8,128)(2,1)} async-done(((bf16[864,64]{0,1:T(8,128)(2,1)}), bf16[864,2048]{0,1:T(8,128)(2,1)}) %all-gather.31.cloned.1.call-update) | async-done | bytes 3538960 | tf_op jit(solution)/shard_map/all_gather | solution.py:140
  646.4 29.0 %all-gather.33.cloned.1.call-done = bf16[512,2048]{1,0:T(8,128)(2,1)} async-done(((bf16[128,2048]{1,0:T(8,128)(2,1)}), bf16[512,2048]{1,0:T(8,128)(2,1)}) %all-gather.33.cloned.1.call-update) | async-done | bytes 2097168 | tf_op jit(solution)/shard_map/all_gather | solution.py:194
  686.2 71.0 %all-gather.29.cloned.1.call-done = bf16[2048,864]{1,0:T(8,128)(2,1)} async-done(((bf16[64,864]{1,0:T(8,128)(2,1)}), bf16[2048,864]{1,0:T(8,128)(2,1)}) %all-gather.29.cloned.1.call-update) | async-done | bytes 3538960 | tf_op jit(solution)/shard_map/all_gather | solution.py:139
  771.8 26.0 %reduce-scatter.17.cloned.1.call-done = bf16[128,2048]{1,0:T(8,128)(2,1)} async-done(((bf16[512,2048]{1,0:T(8,128)(2,1)}), bf16[128,2048]{1,0:T(8,128)(2,1)}) %reduce-scatter.17.cloned.1.call-update) | async-done | bytes 524304 | tf_op jit(solution)/shard_map/reduce_scatter | solution.py:212
  891.0 134.4 %reduce-scatter.31.cloned.1.call-done = bf16[64,864]{1,0:T(8,128)(2,1)} async-done(((bf16[2048,864]{1,0:T(8,128)(2,1)}), bf16[64,864]{1,0:T(8,128)(2,1)}) %reduce-scatter.31.cloned.1.call-update) | async-done | bytes 110608 | tf_op jit(solution)/shard_map/reduce_scatter | solution.py:305
  1027.0 186.8 %reduce-scatter.33.cloned.1.call-done = bf16[64,864]{1,0:T(8,128)(2,1)} async-done(((bf16[2048,864]{1,0:T(8,128)(2,1)}), bf16[64,864]{1,0:T(8,128)(2,1)}) %reduce-scatter.33.cloned.1.call-update) | async-done | bytes 110608 | tf_op jit(solution)/shard_map/reduce_scatter | solution.py:308
  1215.4 186.0 %reduce-scatter.35.cloned.1.call-done = bf16[864,64]{0,1:T(8,128)(2,1)} async-done(((bf16[864,2048]{0,1:T(8,128)(2,1)}), bf16[864,64]{0,1:T(8,128)(2,1)}) %reduce-scatter.35.cloned.1.call-update) | async-done | bytes 110608 | tf_op jit(solution)/shard_map/reduce_scatter | solution.py:311
  1403.2 23.3 reduce-scatter.19.cloned.1.call-done
  1428.2 69.4 %all-reduce = (f32[2048]{0:T(1024)}, f32[2048]{0:T(1024)}, f32[3456]{0:T(1024)S(1)}) all-reduce(f32[2048]{0:T(1024)S(1)} %get-tuple-element.60, f32[2048]{0:T(1024)S(1)} %get-tuple-element.49, f32[3456]{0:T(1024)S(1)} %dynamic_update_slice.9), channel_id=1, replica_groups=mesh['dp'=32,'tensor'=4] {'dp','tensor'}, use_global_device_ids=true, to_apply=%region_13.14 | all-reduce | flops 7552 | bytes 60416 | tf_op jit(solution)/shard_map/psum | solution.py:285
  1498.3 119.1 %reduce-scatter.21.cloned.1.call-done = bf16[64,512]{1,0:T(8,128)(2,1)} async-done(((bf16[2048,512]{1,0:T(8,128)(2,1)}), bf16[64,512]{1,0:T(8,128)(2,1)}) %reduce-scatter.21.cloned.1.call-update) | async-done | bytes 65552 | tf_op jit(solution)/shard_map/reduce_scatter | solution.py:290
  1618.9 182.5 %reduce-scatter.23.cloned.1.call-done = bf16[64,512]{1,0:T(8,128)(2,1)} async-done(((bf16[2048,512]{1,0:T(8,128)(2,1)}), bf16[64,512]{1,0:T(8,128)(2,1)}) %reduce-scatter.23.cloned.1.call-update) | async-done | bytes 65552 | tf_op jit(solution)/shard_map/reduce_scatter | solution.py:293
  1802.9 23.6 reduce-scatter.15.cloned.1.call-done
  1829.5 192.0 %reduce-scatter.25.cloned.1.call-done = bf16[64,864]{1,0:T(8,128)(2,1)} async-done(((bf16[2048,864]{1,0:T(8,128)(2,1)}), bf16[64,864]{1,0:T(8,128)(2,1)}) %reduce-scatter.25.cloned.1.call-update) | async-done | bytes 110608 | tf_op jit(solution)/shard_map/reduce_scatter | solution.py:296
  2023.1 186.1 %reduce-scatter.27.cloned.1.call-done = bf16[64,864]{1,0:T(8,128)(2,1)} async-done(((bf16[2048,864]{1,0:T(8,128)(2,1)}), bf16[64,864]{1,0:T(8,128)(2,1)}) %reduce-scatter.27.cloned.1.call-update) | async-done | bytes 110608 | tf_op jit(solution)/shard_map/reduce_scatter | solution.py:299
  2210.9 186.3 %reduce-scatter.29.cloned.1.call-done = bf16[864,64]{0,1:T(8,128)(2,1)} async-done(((bf16[864,2048]{0,1:T(8,128)(2,1)}), bf16[864,64]{0,1:T(8,128)(2,1)}) %reduce-scatter.29.cloned.1.call-update) | async-done | bytes 110608 | tf_op jit(solution)/shard_map/reduce_scatter | solution.py:302
  (183 shorter events, 185.4 us)
Async XLA Ops:
  7.2 34.9 %all-gather.13.cloned.1.call-start = ((), (), s32[]{:S(2)}) async-start(), calls=%async_computation.12 | async-start | bytes 2621440 | tf_op jit(solution)/shard_map/all_gather | solution.py:144
  10.5 106.5 %all-gather.19.cloned.1.call-start = ((), (), s32[]{:S(2)}) async-start(), calls=%async_computation.15 | async-start | bytes 2162688 | tf_op jit(solution)/shard_map/all_gather | solution.py:133
  11.3 176.5 %all-gather.21.cloned.1.call-start = ((), (), s32[]{:S(2)}) async-start(), calls=%async_computation.16 | async-start | bytes 2162688 | tf_op jit(solution)/shard_map/all_gather | solution.py:134
  12.0 252.8 %all-gather.17.cloned.1.call-start = ((), (), s32[]{:S(2)}) async-start(), calls=%async_computation.14 | async-start | bytes 3784704 | tf_op jit(solution)/shard_map/all_gather | solution.py:135
  12.6 330.3 %all-gather.15.cloned.1.call-start = ((), (), s32[]{:S(2)}) async-start(), calls=%async_computation.13 | async-start | bytes 3784704 | tf_op jit(solution)/shard_map/all_gather | solution.py:136
  13.2 407.8 %all-gather.23.cloned.1.call-start = ((), (), s32[]{:S(2)}) async-start(), calls=%async_computation.17 | async-start | bytes 3784704 | tf_op jit(solution)/shard_map/all_gather | solution.py:137
  13.7 439.9 %reduce-scatter.13.cloned.1.call-start = ((), (), s32[]{:S(2)}) async-start(), calls=%async_computation.18 | async-start | bytes 2621440 | tf_op jit(solution)/shard_map/reduce_scatter | solution.py:163
  427.5 108.0 %all-gather.27.cloned.1.call-start = ((), (), s32[]{:S(2)}) async-start(), calls=%async_computation.20 | async-start | bytes 3784704 | tf_op jit(solution)/shard_map/all_gather | solution.py:138
  428.3 136.2 %all-gather.25.cloned.1.call-start = ((), (), s32[]{:S(2)}) async-start(), calls=%async_computation.19 | async-start | bytes 2621440 | tf_op jit(solution)/shard_map/all_gather | solution.py:171
  457.4 189.0 %all-gather.31.cloned.1.call-start = ((), (), s32[]{:S(2)}) async-start(), calls=%async_computation.22 | async-start | bytes 3784704 | tf_op jit(solution)/shard_map/all_gather | solution.py:140
  458.0 217.4 %all-gather.33.cloned.1.call-start = ((), (), s32[]{:S(2)}) async-start(), calls=%async_computation.24 | async-start | bytes 2621440 | tf_op jit(solution)/shard_map/all_gather | solution.py:194
  458.7 298.5 %all-gather.29.cloned.1.call-start = ((), (), s32[]{:S(2)}) async-start(), calls=%async_computation.21 | async-start | bytes 3784704 | tf_op jit(solution)/shard_map/all_gather | solution.py:139
  459.3 338.5 %reduce-scatter.17.cloned.1.call-start = ((), (), s32[]{:S(2)}) async-start(), calls=%async_computation.25 | async-start | bytes 2621440 | tf_op jit(solution)/shard_map/reduce_scatter | solution.py:212
  771.7 59.2 %all-gather.35.cloned.1.call-start = ((), (), s32[]{:S(2)}) async-start(), calls=%async_computation.26 | async-start | bytes 2621440 | tf_op jit(solution)/shard_map/all_gather | solution.py:229
  800.8 224.6 %reduce-scatter.31.cloned.1.call-start = ((), (), s32[]{:S(2)}) async-start(), calls=%async_computation.33 | async-start | bytes 3784704 | tf_op jit(solution)/shard_map/reduce_scatter | solution.py:305
  806.9 406.9 %reduce-scatter.33.cloned.1.call-start = ((), (), s32[]{:S(2)}) async-start(), calls=%async_computation.34 | async-start | bytes 3784704 | tf_op jit(solution)/shard_map/reduce_scatter | solution.py:308
  813.0 588.4 %reduce-scatter.35.cloned.1.call-start = ((), (), s32[]{:S(2)}) async-start(), calls=%async_computation.35 | async-start | bytes 3784704 | tf_op jit(solution)/shard_map/reduce_scatter | solution.py:311
  819.2 607.3 %reduce-scatter.19.cloned.1.call-start = ((), (), s32[]{:S(2)}) async-start(), calls=%async_computation.27 | async-start | bytes 2621440 | tf_op jit(solution)/shard_map/reduce_scatter | solution.py:267
  855.0 762.4 %reduce-scatter.21.cloned.1.call-start = ((), (), s32[]{:S(2)}) async-start(), calls=%async_computation.28 | async-start | bytes 2162688 | tf_op jit(solution)/shard_map/reduce_scatter | solution.py:290
  859.4 942.0 %reduce-scatter.23.cloned.1.call-start = ((), (), s32[]{:S(2)}) async-start(), calls=%async_computation.29 | async-start | bytes 2162688 | tf_op jit(solution)/shard_map/reduce_scatter | solution.py:293
  863.7 962.8 %reduce-scatter.15.cloned.1.call-start = ((), (), s32[]{:S(2)}) async-start(), calls=%async_computation.23 | async-start | bytes 2621440 | tf_op jit(solution)/shard_map/reduce_scatter | solution.py:175
  870.6 1150.9 %reduce-scatter.25.cloned.1.call-start = ((), (), s32[]{:S(2)}) async-start(), calls=%async_computation.30 | async-start | bytes 3784704 | tf_op jit(solution)/shard_map/reduce_scatter | solution.py:296
  876.5 1332.8 %reduce-scatter.27.cloned.1.call-start = ((), (), s32[]{:S(2)}) async-start(), calls=%async_computation.31 | async-start | bytes 3784704 | tf_op jit(solution)/shard_map/reduce_scatter | solution.py:299
  883.5 1513.7 %reduce-scatter.29.cloned.1.call-start = ((), (), s32[]{:S(2)}) async-start(), calls=%async_computation.32 | async-start | bytes 3784704 | tf_op jit(solution)/shard_map/reduce_scatter | solution.py:302
  (34 other events, 2682.3 us)
Sparse Core Ops, SparseCore 0:
  10.6 31.3 all-gather.12
  45.1 71.9 all-gather.18
  120.0 67.6 all-gather.20
  190.7 74.1 all-gather.16
  267.8 75.0 all-gather.14
  345.8 75.0 all-gather.22
  427.7 25.9 reduce-scatter.12
  457.2 78.3 all-gather.26
  537.9 26.6 all-gather.24
  567.9 78.4 all-gather.30
  648.7 26.6 all-gather.32
  678.8 78.4 all-gather.28
  771.8 25.9 reduce-scatter.16
  801.0 29.8 all-gather.34
  833.1 192.2 reduce-scatter.30
  1027.8 186.0 reduce-scatter.32
  1216.1 185.3 reduce-scatter.34
  1403.9 22.6 reduce-scatter.18
  1428.9 188.4 reduce-scatter.20
  1619.7 181.6 reduce-scatter.22
  1803.8 22.6 reduce-scatter.14
  1829.1 192.4 reduce-scatter.24
  2024.0 185.2 reduce-scatter.26
  2211.7 185.5 reduce-scatter.28
where the time goes:
time: 2420 us; the launch traced here: 2410 us
  waiting for transfers between devices  2150 us (89%)
  matrix products  127 us (5%)
  blocking collectives  69.4 us (3%)
  other arithmetic  30.6 us (1%)
    reduce_scatter x1, waiting for transfers between devices, shards(): lax.psum_scatter(grad_value.astype(jnp.bfloat16), 'dp', scatter_dimension...  192 us
    reduce_scatter x1, waiting for transfers between devices, shards(): lax.psum_scatter(feed_sums[1].astype(jnp.bfloat16), 'dp', scatter_dimensi...  187 us
    reduce_scatter x1, waiting for transfers between devices, shards(): lax.psum_scatter(grad_output.astype(jnp.bfloat16), 'dp', scatter_dimensio...  186 us
    reduce_scatter x1, waiting for transfers between devices, shards(): lax.psum_scatter(grad_swish.astype(jnp.bfloat16), 'dp', scatter_dimension...  186 us
    reduce_scatter x1, waiting for transfers between devices, shards(): lax.psum_scatter(feed_sums[2].astype(jnp.bfloat16), 'dp', scatter_dimensi...  186 us
    reduce_scatter x1, waiting for transfers between devices, shards(): lax.psum_scatter(grad_key.astype(jnp.bfloat16), 'dp', scatter_dimension=0...  183 us
    reduce_scatter x1, waiting for transfers between devices, shards(): lax.psum_scatter(feed_sums[0].astype(jnp.bfloat16), 'dp', scatter_dimensi...  134 us
    reduce_scatter x1, waiting for transfers between devices, shards(): lax.psum_scatter(grad_query.astype(jnp.bfloat16), 'dp', scatter_dimension...  119 us
  transfers between devices with their start and end apart: 24, of which 24 were waited for; matrix products, arithmetic and copies ran while one was open for 5% of the time, Pallas kernels for 0%

commit v1 on v0

v1 whole, which is shorter than its diff:
```python
import jax
import jax.numpy as jnp
from jax import lax
from jax.sharding import PartitionSpec as P

norm_eps = 1e-05
group_eps = 1.0
AXES = ("dp", "tensor")
f32 = jnp.float32
bf16 = jnp.bfloat16
NT = (((1,), (1,)), ((), ()))
TN = (((0,), (0,)), ((), ()))


def device_index(x, z, y, c):
    return ((x * 4 + z) * 2 + y // 2) * 4 + (y % 2) * 2 + c


def xor_pairs(dx=0, dz=0, dy=0, dc=0):
    return [
        (device_index(x, z, y, c), device_index(x ^ dx, z ^ dz, y ^ dy, c ^ dc))
        for x in range(4)
        for z in range(4)
        for y in range(4)
        for c in range(2)
    ]


X1, X2, X3 = (xor_pairs(dx=d) for d in (1, 2, 3))
Z1, Z2, Z3 = (xor_pairs(dz=d) for d in (1, 2, 3))
Y1, Y2, Y3 = (xor_pairs(dy=d) for d in (1, 2, 3))
C1 = xor_pairs(dc=1)
PLANES = [
    [device_index(x, z, y, c) for x in range(4) for z in range(4)]
    for y in range(4)
    for c in range(2)
]


def move(value, pairs):
    return lax.ppermute(value, AXES, pairs)


def tie(*values):
    return lax.optimization_barrier(values)


def gather_plane(shard):
    half = shard.shape[0] // 32 * 16
    a, b = shard[:half], shard[half:]
    ha, hb = a.shape[0] // 32 * 16, b.shape[0] // 32 * 16
    a1, a3, b1, b3 = tie(move(a, X1), move(a, X3), move(b, Z1), move(b, Z3))
    a2p, a2q, b2p, b2q = tie(
        move(a3[:ha], X1), move(a1[ha:], X3), move(b3[:hb], Z1), move(b1[hb:], Z3)
    )
    a2, b2 = jnp.concatenate([a2p, a2q]), jnp.concatenate([b2p, b2q])
    sa, sb = jnp.stack([a, a1, a2, a3]), jnp.stack([b, b1, b2, b3])
    sa, sb = tie(sa, sb)
    sa1, sa3, sb1, sb3 = tie(move(sa, Z1), move(sa, Z3), move(sb, X1), move(sb, X3))
    sa2p, sa2q, sb2p, sb2q = tie(
        move(sa3[:2], Z1), move(sa1[2:], Z3), move(sb3[:2], X1), move(sb1[2:], X3)
    )
    sa2, sb2 = jnp.concatenate([sa2p, sa2q]), jnp.concatenate([sb2p, sb2q])
    va = (sa, sa1, sa2, sa3)
    vb = (sb, sb1, sb2, sb3)
    return [
        jnp.concatenate([va[dz][dx], vb[dx][dz]]) for dx in range(4) for dz in range(4)
    ]


def add_low(*terms):
    total = terms[0].astype(f32)
    for term in terms[1:]:
        total = total + term.astype(f32)
    return total.astype(bf16)


def scatter_plane(grad):
    rows = grad.shape[0]
    half = rows // 32 * 16
    blocks = [grad[:, 128 * j : 128 * j + 128] for j in range(16)]
    a = [jnp.stack([blocks[4 * dx + dz][:half] for dx in range(4)]) for dz in range(4)]
    b = [jnp.stack([blocks[4 * dx + dz][half:] for dz in range(4)]) for dx in range(4)]
    ap, aq, bp, bq = tie(
        move(a[2][:2], Z1), move(a[2][2:], Z3), move(b[2][:2], X1), move(b[2][2:], X3)
    )
    a3 = jnp.concatenate([add_low(a[3][:2], ap), a[3][2:]])
    a1 = jnp.concatenate([a[1][:2], add_low(a[1][2:], aq)])
    b3 = jnp.concatenate([add_low(b[3][:2], bp), b[3][2:]])
    b1 = jnp.concatenate([b[1][:2], add_low(b[1][2:], bq)])
    a3, a1, b3, b1 = tie(a3, a1, b3, b1)
    r3, r1, s3, s1 = tie(move(a3, Z3), move(a1, Z1), move(b3, X3), move(b1, X1))
    a, b = add_low(a[0], r3, r1), add_low(b[0], s3, s1)
    a, b = tie(a, b)
    ha, hb = a.shape[1] // 32 * 16, b.shape[1] // 32 * 16
    ap, aq, bp, bq = tie(
        move(a[2][:ha], X1), move(a[2][ha:], X3), move(b[2][:hb], Z1), move(b[2][hb:], Z3)
    )
    a3 = jnp.concatenate([add_low(a[3][:ha], ap), a[3][ha:]])
    a1 = jnp.concatenate([a[1][:ha], add_low(a[1][ha:], aq)])
    b3 = jnp.concatenate([add_low(b[3][:hb], bp), b[3][hb:]])
    b1 = jnp.concatenate([b[1][:hb], add_low(b[1][hb:], bq)])
    a3, a1, b3, b1 = tie(a3, a1, b3, b1)
    r3, r1, s3, s1 = tie(move(a3, X3), move(a1, X1), move(b3, Z3), move(b1, Z1))
    top = a[0].astype(f32) + r3.astype(f32) + r1.astype(f32)
    low = b[0].astype(f32) + s3.astype(f32) + s1.astype(f32)
    return jnp.concatenate([top, low])


def gather_line(own):
    half = own.shape[0] // 2
    r1, r3 = tie(move(own, Y1), move(own, Y3))
    mine = jnp.concatenate([own, r1])
    mine = jnp.concatenate([mine, move(mine, C1)])
    r2 = jnp.concatenate([move(r3[:half], Y1), move(r1[half:], Y3)])
    other = jnp.concatenate([r2, r3])
    other = jnp.concatenate([other, move(other, C1)])
    return mine, other


def scatter_line(mine, other):
    rows = mine.shape[0] // 4
    half = rows // 2
    o = other[: 2 * rows] + move(other[2 * rows :].astype(bf16), C1).astype(f32)
    s2 = o[:rows].astype(bf16)
    t3, t1 = tie(move(s2[:half], Y1), move(s2[half:], Y3))
    m = mine[: 2 * rows] + move(mine[2 * rows :].astype(bf16), C1).astype(f32)
    s3 = jnp.concatenate([o[rows : rows + half] + t3.astype(f32), o[rows + half :]]).astype(bf16)
    s1 = jnp.concatenate([m[rows : rows + half], m[rows + half :] + t1.astype(f32)]).astype(bf16)
    u3, u1 = tie(move(s3, Y3), move(s1, Y1))
    return m[:rows] + u3.astype(f32) + u1.astype(f32)


def shards(
    tokens,
    group_length,
    forget_rate,
    mixer_gain,
    feed_gain,
    group_gain,
    w_query,
    w_key,
    w_value,
    w_swish,
    w_output,
    w_gelu,
    w_linear,
    w_down,
    cotangent,
):
    rows, width = tokens.shape
    dp = lax.axis_index("dp")
    tensor = lax.axis_index("tensor")
    plane = dp // 2
    high = dp % 2
    is_low = high == 0
    wide = w_value.shape[1] // 2
    kwide = w_query.shape[1] // 2
    score_scale = kwide ** (-0.5)
    log_keep = jnp.log1p(-jnp.where(is_low, forget_rate[0], forget_rate[1]))
    valid_rows = (tensor * rows + lax.broadcasted_iota(jnp.int32, (rows, 1), 0) < group_length[0]).astype(f32)
    relative = jnp.bitwise_xor(plane, jnp.arange(16, dtype=jnp.int32))

    def to_relative(value):
        parts = [lax.dynamic_slice_in_dim(value, relative[j] * 128, 128, value.ndim - 1) for j in range(16)]
        return jnp.concatenate(parts, axis=-1)

    def from_relative(value):
        return to_relative(value)

    def halves(parts):
        return [
            (
                jnp.where(is_low, part[:, : part.shape[1] // 2], part[:, part.shape[1] // 2 :]),
                jnp.where(is_low, part[:, part.shape[1] // 2 :], part[:, : part.shape[1] // 2]),
            )
            for part in parts
        ]

    def padded(parts):
        return jnp.concatenate(
            [jnp.pad(p, ((0, 0), (0, -p.shape[1] % 128))) for p in parts], axis=1
        )

    def trade(parts):
        pairs = halves(parts)
        keep, send = padded([p[0] for p in pairs]), padded([p[1] for p in pairs])
        got = move(send, Y2)
        both = jnp.where(is_low, jnp.concatenate([keep, got]), jnp.concatenate([got, keep])).T
        out, place = [], 0
        for part in parts:
            size = part.shape[1] // 2
            out.append(both[place : place + size])
            place += size + (-size % 128)
        return jnp.concatenate(out)

    first = trade([w_query, w_key, w_value, w_swish])
    second = trade([w_output.T, w_gelu, w_linear, w_down.T])

    token_float = to_relative(tokens).astype(f32)
    grad_result = to_relative(cotangent).astype(f32)
    mixer_rel = to_relative(mixer_gain)
    feed_rel = to_relative(feed_gain)
    group_own = jnp.where(is_low, group_gain[:wide], group_gain[wide:])

    r1 = lax.rsqrt(jnp.mean(token_float * token_float, axis=-1, keepdims=True) + norm_eps)
    normed_in = (token_float * r1 * mixer_rel).astype(bf16)
    normed_group = jnp.concatenate(gather_line(normed_in))

    first_full = jnp.concatenate(gather_plane(first), axis=1)
    wq, wk = first_full[:kwide], first_full[kwide : 2 * kwide]
    wv, ws = first_full[2 * kwide : 2 * kwide + wide], first_full[2 * kwide + wide :]
    second_full = lax.all_gather(second, AXES, axis_index_groups=PLANES, axis=0, tiled=False)
    second_full = jnp.concatenate(
        [lax.dynamic_index_in_dim(second_full, relative[j], 0, keepdims=False) for j in range(16)],
        axis=1,
    )
    wo, wg, wl, wd = (second_full[i * wide : (i + 1) * wide] for i in range(4))

    def dot(left, right, dims=(((1,), (0,)), ((), ()))):
        return lax.dot_general(left, right, dims, preferred_element_type=f32)

    group_rows = 4 * rows
    q = dot(normed_group, wq, NT).astype(bf16).reshape(2, group_rows, kwide)
    k = dot(normed_group, wk, NT).astype(bf16).reshape(2, group_rows, kwide)
    v = dot(normed_group, wv, NT).astype(bf16).reshape(2, group_rows, wide)
    gate_pre = dot(normed_group, ws, NT)

    order = jnp.array([0, 2, 1, 3], jnp.int32)
    starts = jnp.bitwise_xor(tensor, order) * rows
    position = (starts[:, None] + jnp.arange(rows, dtype=jnp.int32)[None]).reshape(-1)
    offset = position[:, None] - position[None]
    decay = jnp.where(
        offset >= 0, jnp.exp(jnp.maximum(offset, 0).astype(f32) * log_keep) * score_scale, 0.0
    )
    scores = jnp.einsum("gid,gjd->gij", q, k, preferred_element_type=f32)
    weights = (scores * decay).astype(bf16)
    retained = jnp.einsum("gij,gje->gie", weights, v, preferred_element_type=f32).reshape(-1, wide)
    center = retained - jnp.mean(retained, axis=-1, keepdims=True)
    rstd = lax.rsqrt(jnp.mean(center * center, axis=-1, keepdims=True) + group_eps)
    normed = center * rstd
    sig = jax.nn.sigmoid(gate_pre)
    silu = gate_pre * sig
    mixed_low = (silu * normed * group_own).astype(bf16)
    mixer_part = dot(mixed_low, wo)
    mixer_out = scatter_line(mixer_part[:group_rows], mixer_part[group_rows:])
    middle = token_float + valid_rows * mixer_out
    r2 = lax.rsqrt(jnp.mean(middle * middle, axis=-1, keepdims=True) + norm_eps)
    normed_mid = (middle * r2 * feed_rel).astype(bf16)
    mid_group = jnp.concatenate(gather_line(normed_mid))
    gelu_in = dot(mid_group, wg, NT)
    linear_in = dot(mid_group, wl, NT)
    cdf = 0.5 * (1.0 + lax.erf(gelu_in * (0.5**0.5)))
    gelu = gelu_in * cdf
    gelu_slope = cdf + gelu_in * jnp.exp(-0.5 * gelu_in * gelu_in) * 0.3989422804014327
    hidden = (gelu * linear_in).astype(bf16)
    feed_part = dot(hidden, wd)

    grad_feed_out = (valid_rows * grad_result).astype(bf16)
    grad_feed_group = jnp.concatenate(gather_line(grad_feed_out))
    grad_hidden = dot(grad_feed_group, wd, NT)
    grad_gelu_in = (grad_hidden * linear_in * gelu_slope).astype(bf16)
    grad_linear_in = (grad_hidden * gelu).astype(bf16)
    mid_part = dot(grad_gelu_in, wg) + dot(grad_linear_in, wl)
    grad_normed_mid = scatter_line(mid_part[:group_rows], mid_part[group_rows:])
    grad_ffn = jnp.concatenate(
        [
            dot(grad_gelu_in, mid_group, TN).astype(bf16),
            dot(grad_linear_in, mid_group, TN).astype(bf16),
            dot(hidden, grad_feed_group, TN).astype(bf16),
        ]
    )
    feed_out = scatter_line(feed_part[:group_rows], feed_part[group_rows:])
    result = (middle + valid_rows * feed_out).astype(bf16)

    part_feed_gain = jnp.sum(grad_normed_mid * middle * r2, axis=0)
    z2 = grad_normed_mid * feed_rel
    grad_middle = (
        grad_result + r2 * z2 - middle * (r2 * r2 * r2) * jnp.mean(z2 * middle, axis=-1, keepdims=True)
    )
    grad_mixer_out = (valid_rows * grad_middle).astype(bf16)
    grad_mixer_group = jnp.concatenate(gather_line(grad_mixer_out))
    grad_mixed = dot(grad_mixer_group, wo, NT)
    grad_output = dot(mixed_low, grad_mixer_group, TN).astype(bf16)
    grad_gate_pre = (
        grad_mixed * normed * group_own * (sig * (1.0 + gate_pre * (1.0 - sig)))
    ).astype(bf16)
    part_group_gain = jnp.sum(grad_mixed * silu * normed, axis=0)
    y = grad_mixed * silu * group_own
    grad_retained = (
        rstd * (y - jnp.mean(y, axis=-1, keepdims=True))
        - center * (rstd * rstd * rstd) * jnp.mean(y * center, axis=-1, keepdims=True)
    ).astype(bf16).reshape(2, group_rows, wide)
    grad_scores = (
        jnp.einsum("gie,gje->gij", grad_retained, v, preferred_element_type=f32) * decay
    ).astype(bf16)
    gq = jnp.einsum("gij,gjd->gid", grad_scores, k, preferred_element_type=f32).astype(bf16)
    gk = jnp.einsum("gij,gid->gjd", grad_scores, q, preferred_element_type=f32).astype(bf16)
    gv = jnp.einsum("gij,gie->gje", weights, grad_retained, preferred_element_type=f32).astype(bf16)
    gq, gk, gv = gq.reshape(-1, kwide), gk.reshape(-1, kwide), gv.reshape(-1, wide)
    in_part = dot(gq, wq) + dot(gk, wk) + dot(gv, wv) + dot(grad_gate_pre, ws)
    grad_normed_in = scatter_line(in_part[:group_rows], in_part[group_rows:])
    grad_attn = jnp.concatenate(
        [
            dot(gq, normed_group, TN).astype(bf16),
            dot(gk, normed_group, TN).astype(bf16),
            dot(gv, normed_group, TN).astype(bf16),
            dot(grad_gate_pre, normed_group, TN).astype(bf16),
        ]
    )
    part_mixer_gain = jnp.sum(grad_normed_in * token_float * r1, axis=0)
    z1 = grad_normed_in * mixer_rel
    grad_tokens = (
        grad_middle + r1 * z1 - token_float * (r1 * r1 * r1) * jnp.mean(z1 * token_float, axis=-1, keepdims=True)
    ).astype(bf16)
    result = from_relative(result)
    grad_tokens = from_relative(grad_tokens)

    late = jnp.concatenate([grad_output, grad_attn])
    late_sum = scatter_plane(late).astype(bf16)
    early = jnp.stack(
        [lax.dynamic_slice_in_dim(grad_ffn, relative[j] * 128, 128, 1) for j in range(16)]
    )
    early_sum = lax.psum_scatter(
        early, AXES, axis_index_groups=PLANES, scatter_dimension=0, tiled=False
    )

    def settle(summed, sizes):
        flat = jnp.concatenate(
            [
                jnp.pad(p, ((0, -p.shape[0] % 128), (0, 0)))
                for p in (summed[a : a + n] for a, n in sizes)
            ]
        ).T
        half = flat.shape[0] // 2
        keep = jnp.where(is_low, flat[:half], flat[half:])
        send = jnp.where(is_low, flat[half:], flat[:half])
        got = move(send, Y2)
        out, place = [], 0
        for _, n in sizes:
            own, far = keep[:, place : place + n], got[:, place : place + n]
            out.append(
                jnp.where(
                    is_low,
                    jnp.concatenate([own, far], axis=1),
                    jnp.concatenate([far, own], axis=1),
                ).astype(f32)
            )
            place += n + (-n % 128)
        return out

    g_gelu, g_linear, g_down = settle(early_sum, [(0, wide), (wide, wide), (2 * wide, wide)])
    g_output, g_query, g_key, g_value, g_swish = settle(
        late_sum,
        [
            (0, wide),
            (wide, kwide),
            (wide + kwide, kwide),
            (wide + 2 * kwide, wide),
            (2 * wide + 2 * kwide, wide),
        ],
    )

    def butterfly(value, *steps):
        for pairs in steps:
            value = value + move(value, pairs)
        return value

    feed_sum = butterfly(from_relative(part_feed_gain), C1, Y1, Y2, X1, X2, Z1, Z2)
    mixer_sum = butterfly(from_relative(part_mixer_gain), C1, Y1, Y2, X1, X2, Z1, Z2)
    group_half = butterfly(part_group_gain, X1, X2, Z1, Z2)
    group_far = move(group_half, Y2)
    group_sum = jnp.where(
        is_low,
        jnp.concatenate([group_half, group_far]),
        jnp.concatenate([group_far, group_half]),
    )
    return (
        result,
        grad_tokens,
        mixer_sum,
        feed_sum,
        group_sum,
        g_query,
        g_key,
        g_value,
        g_swish,
        g_output.T,
        g_gelu,
        g_linear,
        g_down.T,
    )


def solution(mesh):
    return jax.shard_map(
        shards,
        mesh=mesh,
        in_specs=(
            P(("dp", "tensor"), None),
            P("dp"),
            P("tensor"),
            P(),
            P(),
            P("tensor"),
            P("dp", "tensor"),
            P("dp", "tensor"),
            P("dp", "tensor"),
            P("dp", "tensor"),
            P("tensor", "dp"),
            P("dp", "tensor"),
            P("dp", "tensor"),
            P("tensor", "dp"),
            P(("dp", "tensor"), None),
        ),
        out_specs=(
            P(("dp", "tensor"), None),
            P(("dp", "tensor"), None),
            P(),
            P(),
            P("tensor"),
            P("dp", "tensor"),
            P("dp", "tensor"),
            P("dp", "tensor"),
            P("dp", "tensor"),
            P("tensor", "dp"),
            P("dp", "tensor"),
            P("dp", "tensor"),
            P("tensor", "dp"),
        ),
        check_vma=False,
    )
```

time: 2420 us -> 634 us (0.26)
  waiting for transfers between devices: 2150 us -> 189 us
  starting transfers between devices: 1.81 us -> 105 us
  local copies, waits for them, and re-layouts: 8.57 us -> 98.4 us
  blocking collectives: 69.4 us -> 0 us
  between operations: 15.7 us -> 60.4 us
  other arithmetic: 30.6 us -> 66.9 us
    reduce_scatter x12 -> x0, waiting for transfers between devices: 1470 us -> none  [the longest x1 192 us: shards(): lax.psum_scatter(grad_value.astype(jnp.bfloat16), 'dp', scatter_dimension...]
    all_gather x12 -> x1, waiting for transfers between devices: 676 us -> 0.01 us  [shards(): lax.all_gather(second, AXES, axis_index_groups=PLANES, axis=0, tiled=False)]
    ppermute x0 -> x103, waiting for transfers between devices: none -> 189 us  [move(): return lax.ppermute(value, AXES, pairs)]
    ppermute x0 -> x103, starting transfers between devices: none -> 105 us  [move(): return lax.ppermute(value, AXES, pairs)]
    psum x1 -> x0, blocking collectives: 69.4 us -> none  [shards(): lax.psum((grad_mixer_gain, grad_feed_gain, group_full), ('dp', 'tensor'))]
    unnamed x68 -> x331, local copies, waits for them, and re-layouts: 7.73 us -> 74.2 us
    dot_general x30, matrix products: 127 us -> 103 us  [the longest x24 99.7 us: dot(): return lax.dot_general(left, right, dims, preferred_element_type=f32)]
  transfers between devices with their start and end apart: 24 -> 105, of which waited for: 24 -> 58; matrix products, arithmetic and copies ran while one was open for 5% -> 34% of each run, Pallas kernels for 0% -> 0%
where the time goes in v1:
time: 634 us; the launch traced here: 624 us
  waiting for transfers between devices  189 us (30%)
  starting transfers between devices  105 us (17%)
  matrix products  103 us (16%)
  local copies, waits for them, and re-layouts  98.4 us (16%)
  other arithmetic  66.9 us (11%)
  between operations  60.4 us (10%)
    ppermute x103, waiting for transfers between devices, move(): return lax.ppermute(value, AXES, pairs)  189 us
    ppermute x103, starting transfers between devices, move(): return lax.ppermute(value, AXES, pairs)  105 us
    dot_general x24, matrix products, dot(): return lax.dot_general(left, right, dims, preferred_element_type=f32)  99.7 us
    unnamed x331, local copies, waits for them, and re-layouts  74.2 us
  transfers between devices with their start and end apart: 105, of which 58 were waited for; matrix products, arithmetic and copies ran while one was open for 34% of the time, Pallas kernels for 0%

profile of v1, /device:TPU:0, one launch (start us, length us, event | category | flops | bytes accessed | tf_op | source)
XLA Modules:
  0.0 623.5 jit_solution(7405612321891784469)
XLA Ops:
  96.1 4.0 collective-permute-done.10
  109.8 4.1 collective-permute-done.11
  125.6 6.2 collective-permute-done.3
  133.8 5.6 collective-permute-done.4
  178.7 17.9 %fusion.165 = (bf16[1024,2048]{1,0:T(8,128)(2,1)S(1)}, f32[1024,2048]{1,0:T(8,128)}) fusion(bf16[1024,432]{0,1:T(8,128)(2,1)S(1)} %get-tuple-element.400, bf16[1728,2048]{1,0:T(8,128)(2,1)S(1)} %bitcast_dynamic-update-slice_fusion), kind=kOutput, calls=%fused_computation.624 | convolution fusion | flops 1814036480 | bytes 15237120 | tf_op jit(solution)/shard_map/dot_general | solution.py:221
  211.2 4.0 collective-permute-done.26
  219.7 10.7 %collective-permute-done.29 = bf16[128,2048]{1,0:T(8,128)(2,1)S(1)} collective-permute-done((bf16[128,2048]{1,0:T(8,128)(2,1)S(1)}, bf16[128,2048]{1,0:T(8,128)(2,1)S(1)}, u32[]{:S(2)}, u32[]{:S(2)}) %collective-permute-start.29) | collective-permute-done | bytes 524320 | tf_op jit(solution)/shard_map/ppermute | solution.py:41
  235.0 9.5 %collective-permute-done.30 = bf16[128,2048]{1,0:T(8,128)(2,1)S(1)} collective-permute-done((bf16[128,2048]{1,0:T(8,128)(2,1)S(1)}, bf16[128,2048]{1,0:T(8,128)(2,1)S(1)}, u32[]{:S(2)}, u32[]{:S(2)}) %collective-permute-start.30) | collective-permute-done | bytes 524320 | tf_op jit(solution)/shard_map/ppermute | solution.py:41
  268.3 4.5 fusion.167
  276.0 5.7 fusion.14
  293.3 6.8 %fusion.166 = (bf16[1024,2048]{1,0:T(8,128)(2,1)}, f32[1024,2048]{1,0:T(8,128)S(1)}) fusion(f32[1024,2048]{1,0:T(8,128)} %fusion.14, bf16[1728,2048]{1,0:T(8,128)(2,1)} %copy-done.11, f32[1024,432]{0,1:T(8,128)S(1)} %copy-done.23, f32[1024,432]{0,1:T(8,128)S(1)} %copy-done.6), kind=kOutput, calls=%fused_computation.625 | convolution fusion | flops 1818787840 | bytes 26279936 | tf_op jit(solution)/shard_map/dot_general | solution.py:221
  331.1 4.5 collective-permute-done.41
  338.2 7.1 %collective-permute-done.53 = bf16[128,2048]{1,0:T(8,128)(2,1)} collective-permute-done((bf16[128,2048]{1,0:T(8,128)(2,1)}, bf16[128,2048]{1,0:T(8,128)(2,1)}, u32[]{:S(2)}, u32[]{:S(2)}) %collective-permute-start.53) | collective-permute-done | bytes 524320 | tf_op jit(solution)/shard_map/ppermute | solution.py:41
  357.5 5.7 collective-permute-done.74
  381.5 4.6 collective-permute-done.79
  389.9 4.6 multiply_reduce_fusion
  411.6 6.3 %fusion.22 = f32[1024,2048]{1,0:T(8,128)} fusion(bf16[1024,432]{0,1:T(8,128)(2,1)S(1)} %bitcast.379, bf16[1376,2048]{1,0:T(8,128)(2,1)S(1)} %bitcast.375), kind=kOutput, calls=%fused_computation.70 | convolution fusion | flops 1811939328 | bytes 11042816 | tf_op jit(solution)/shard_map/dot_general | solution.py:221
  417.9 5.6 fusion.26
  432.0 13.1 %fusion.168 = (bf16[1024,2048]{1,0:T(8,128)(2,1)}, f32[1024,2048]{1,0:T(8,128)}) fusion(f32[1024,2048]{1,0:T(8,128)} %fusion.26, f32[1024,2048]{1,0:T(8,128)} %fusion.22, f32[1024,2048]{1,0:T(8,128)S(1)} %fusion.70, bf16[1024,256]{1,0:T(8,128)(2,1)} %bitcast.371, bf16[1376,2048]{1,0:T(8,128)(2,1)} %copy-done.26), kind=kOutput, calls=%fused_computation.627 | convolution fusion | flops 1082130432 | bytes 39321600 | tf_op jit(solution)/shard_map/dot_general | solution.py:221
  445.1 4.0 collective-permute-done.80
  486.1 16.7 %collective-permute-done.89 = bf16[4,896,128]{2,1,0:T(8,128)(2,1)S(1)} collective-permute-done((bf16[4,896,128]{2,1,0:T(8,128)(2,1)S(1)}, bf16[4,896,128]{2,1,0:T(8,128)(2,1)S(1)}, u32[]{:S(2)}, u32[]{:S(2)}) %collective-permute-start.89) | collective-permute-done | bytes 917536 | tf_op jit(solution)/shard_map/ppermute | solution.py:41
  536.7 5.6 collective-permute-done.102
  553.4 4.2 collective-permute-done.64
  596.0 4.7 collective-permute-done.70
  (785 shorter events, 397.6 us)
Async XLA Ops:
  7.2 160.1 %all-gather.3.cloned.1.call-start = ((), (), s32[]{:S(2)}) async-start(), calls=%async_computation | async-start | bytes 7520256 | tf_op jit(solution)/shard_map/all_gather | solution.py:213
  13.8 34.5 %collective-permute-start.23 = (bf16[64,2048]{0,1:T(8,128)(2,1)}, bf16[64,2048]{0,1:T(8,128)(2,1)}, u32[]{:S(2)}, u32[]{:S(2)}) collective-permute-start(bf16[64,2048]{0,1:T(8,128)(2,1)} %fusion.97), channel_id=1, source_target_pairs={{0,4},{1,5},{2,6},{3,7},{4,0},{5,1},{6,2},{7,3},{8,12},{9,13},{10,... | collective-permute-start | bytes 786440 | tf_op jit(solution)/shard_map/ppermute | solution.py:41
  20.5 65.2 %collective-permute-start.6 = (bf16[64,1536]{0,1:T(8,128)(2,1)}, bf16[64,1536]{0,1:T(8,128)(2,1)}, u32[]{:S(2)}, u32[]{:S(2)}) collective-permute-start(bf16[64,1536]{0,1:T(8,128)(2,1)} %fusion.116), channel_id=1, source_target_pairs={{0,4},{1,5},{2,6},{3,7},{4,0},{5,1},{6,2},{7,3},{8,12},{9,13},{10,... | collective-permute-start | bytes 589832 | tf_op jit(solution)/shard_map/ppermute | solution.py:41
  36.3 84.3 %collective-permute-start = (bf16[128,2048]{1,0:T(8,128)(2,1)S(1)}, bf16[128,2048]{1,0:T(8,128)(2,1)S(1)}, u32[]{:S(2)}, u32[]{:S(2)}) collective-permute-start(bf16[128,2048]{1,0:T(8,128)(2,1)S(1)} %get-tuple-element.214), channel_id=1, source_target_pairs={{0,2},{1,3},{2,0},{3,1},{4,6},{5,7},{6,4},{7,5},{8,10},{9,11},{10,... | collective-permute-start | bytes 1572872 | tf_op jit(solution)/shard_map/ppermute | solution.py:41
  51.3 469.7 %all-reduce.20.cloned.1.call-start = ((), (), s32[]{:S(2)}) async-start(), calls=%async_computation.1 | async-start | bytes 10616832
  116.3 23.4 %collective-permute-start.15 = (bf16[4,688,128]{2,1,0:T(8,128)(2,1)S(1)}, bf16[4,688,128]{2,1,0:T(8,128)(2,1)S(1)}, u32[]{:S(2)}, u32[]{:S(2)}) collective-permute-start(bf16[4,688,128]{2,1,0:T(8,128)(2,1)S(1)} %pad_maximum_fusion.13), channel_id=1, source_target_pairs={{0,8},{1,9},{2,10},{3,11},{4,12},{5,13},{6,14},{7,15},{8,0},{9,1},... | collective-permute-start | bytes 2113544 | tf_op jit(solution)/shard_map/ppermute | solution.py:41
  117.9 21.8 %collective-permute-start.16 = (bf16[4,688,128]{2,1,0:T(8,128)(2,1)S(1)}, bf16[4,688,128]{2,1,0:T(8,128)(2,1)S(1)}, u32[]{:S(2)}, u32[]{:S(2)}) collective-permute-start(bf16[4,688,128]{2,1,0:T(8,128)(2,1)S(1)} %pad_maximum_fusion.13), channel_id=1, source_target_pairs={{0,24},{1,25},{2,26},{3,27},{4,28},{5,29},{6,30},{7,31},{8,16},{9,... | collective-permute-start | bytes 2113544 | tf_op jit(solution)/shard_map/ppermute | solution.py:41
  139.3 60.2 %collective-permute-start.42 = (bf16[128,2048]{1,0:T(8,128)(2,1)S(1)}, bf16[128,2048]{1,0:T(8,128)(2,1)S(1)}, u32[]{:S(2)}, u32[]{:S(2)}) collective-permute-start(bf16[128,2048]{1,0:T(8,128)(2,1)S(1)} %get-tuple-element.204), channel_id=1, source_target_pairs={{0,2},{1,3},{2,0},{3,1},{4,6},{5,7},{6,4},{7,5},{8,10},{9,11},{10,... | collective-permute-start | bytes 1572872 | tf_op jit(solution)/shard_map/ppermute | solution.py:41
  147.5 52.1 %collective-permute-start.43 = (bf16[128,2048]{1,0:T(8,128)(2,1)S(1)}, bf16[128,2048]{1,0:T(8,128)(2,1)S(1)}, u32[]{:S(2)}, u32[]{:S(2)}) collective-permute-start(bf16[128,2048]{1,0:T(8,128)(2,1)S(1)} %get-tuple-element.204), channel_id=1, source_target_pairs={{0,6},{1,7},{2,4},{3,5},{4,2},{5,3},{6,0},{7,1},{8,14},{9,15},{10,... | collective-permute-start | bytes 1572872 | tf_op jit(solution)/shard_map/ppermute | solution.py:41
  211.0 23.9 %collective-permute-start.47 = (bf16[256,2048]{1,0:T(8,128)(2,1)S(1)}, bf16[256,2048]{1,0:T(8,128)(2,1)S(1)}, u32[]{:S(2)}, u32[]{:S(2)}) collective-permute-start(bf16[256,2048]{1,0:T(8,128)(2,1)S(1)} %pad_maximum_fusion.6), channel_id=1, source_target_pairs={{0,1},{1,0},{2,3},{3,2},{4,5},{5,4},{6,7},{7,6},{8,9},{9,8},{10,11... | collective-permute-start | bytes 3145736 | tf_op jit(solution)/shard_map/ppermute | solution.py:41
  325.5 19.8 %collective-permute-start.53 = (bf16[128,2048]{1,0:T(8,128)(2,1)}, bf16[128,2048]{1,0:T(8,128)(2,1)}, u32[]{:S(2)}, u32[]{:S(2)}) collective-permute-start(bf16[128,2048]{1,0:T(8,128)(2,1)} %pad_maximum_fusion.20), channel_id=1, source_target_pairs={{0,2},{1,3},{2,0},{3,1},{4,6},{5,7},{6,4},{7,5},{8,10},{9,11},{10,... | collective-permute-start | bytes 1572872 | tf_op jit(solution)/shard_map/ppermute | solution.py:41
  326.9 19.7 %collective-permute-start.52 = (bf16[128,2048]{1,0:T(8,128)(2,1)}, bf16[128,2048]{1,0:T(8,128)(2,1)}, u32[]{:S(2)}, u32[]{:S(2)}) collective-permute-start(bf16[128,2048]{1,0:T(8,128)(2,1)} %pad_maximum_fusion.19), channel_id=1, source_target_pairs={{0,6},{1,7},{2,4},{3,5},{4,2},{5,3},{6,0},{7,1},{8,14},{9,15},{10,... | collective-permute-start | bytes 1572872 | tf_op jit(solution)/shard_map/ppermute | solution.py:41
  365.0 22.1 %collective-permute-start.56 = (bf16[256,2048]{1,0:T(8,128)(2,1)S(1)}, bf16[256,2048]{1,0:T(8,128)(2,1)S(1)}, u32[]{:S(2)}, u32[]{:S(2)}) collective-permute-start(bf16[256,2048]{1,0:T(8,128)(2,1)S(1)} %pad_maximum_fusion.7), channel_id=1, source_target_pairs={{0,1},{1,0},{2,3},{3,2},{4,5},{5,4},{6,7},{7,6},{8,9},{9,8},{10,11... | collective-permute-start | bytes 3145736 | tf_op jit(solution)/shard_map/ppermute | solution.py:41
  424.3 45.0 %collective-permute-start.88 = (bf16[2,912,128]{2,1,0:T(8,128)(2,1)}, bf16[2,912,128]{2,1,0:T(8,128)(2,1)}, u32[]{:S(2)}, u32[]{:S(2)}) collective-permute-start(bf16[2,912,128]{2,1,0:T(8,128)(2,1)} %pad_maximum_fusion.24), channel_id=1, source_target_pairs={{0,96},{1,97},{2,98},{3,99},{4,100},{5,101},{6,102},{7,103},{8,104... | collective-permute-start | bytes 1400840 | tf_op jit(solution)/shard_map/ppermute | solution.py:41
  425.6 43.7 %collective-permute-start.87 = (bf16[2,912,128]{2,1,0:T(8,128)(2,1)}, bf16[2,912,128]{2,1,0:T(8,128)(2,1)}, u32[]{:S(2)}, u32[]{:S(2)}) collective-permute-start(bf16[2,912,128]{2,1,0:T(8,128)(2,1)} %pad_maximum_fusion.23), channel_id=1, source_target_pairs={{0,32},{1,33},{2,34},{3,35},{4,36},{5,37},{6,38},{7,39},{8,40},{9,... | collective-permute-start | bytes 1400840 | tf_op jit(solution)/shard_map/ppermute | solution.py:41
  427.5 41.2 %collective-permute-start.86 = (bf16[2,896,128]{2,1,0:T(8,128)(2,1)}, bf16[2,896,128]{2,1,0:T(8,128)(2,1)}, u32[]{:S(2)}, u32[]{:S(2)}) collective-permute-start(bf16[2,896,128]{2,1,0:T(8,128)(2,1)} %pad_maximum_fusion.26), channel_id=1, source_target_pairs={{0,24},{1,25},{2,26},{3,27},{4,28},{5,29},{6,30},{7,31},{8,16},{9,... | collective-permute-start | bytes 1376264 | tf_op jit(solution)/shard_map/ppermute | solution.py:41
  429.8 39.6 %collective-permute-start.85 = (bf16[2,896,128]{2,1,0:T(8,128)(2,1)}, bf16[2,896,128]{2,1,0:T(8,128)(2,1)}, u32[]{:S(2)}, u32[]{:S(2)}) collective-permute-start(bf16[2,896,128]{2,1,0:T(8,128)(2,1)} %pad_maximum_fusion.25), channel_id=1, source_target_pairs={{0,8},{1,9},{2,10},{3,11},{4,12},{5,13},{6,14},{7,15},{8,0},{9,1},... | collective-permute-start | bytes 1376264 | tf_op jit(solution)/shard_map/ppermute | solution.py:41
  477.9 26.9 %collective-permute-start.91 = (bf16[4,912,128]{2,1,0:T(8,128)(2,1)S(1)}, bf16[4,912,128]{2,1,0:T(8,128)(2,1)S(1)}, u32[]{:S(2)}, u32[]{:S(2)}) collective-permute-start(bf16[4,912,128]{2,1,0:T(8,128)(2,1)S(1)} %pad_maximum_fusion.9), channel_id=1, source_target_pairs={{0,96},{1,97},{2,98},{3,99},{4,100},{5,101},{6,102},{7,103},{8,104... | collective-permute-start | bytes 2801672 | tf_op jit(solution)/shard_map/ppermute | solution.py:41
  479.9 24.9 %collective-permute-start.92 = (bf16[4,912,128]{2,1,0:T(8,128)(2,1)S(1)}, bf16[4,912,128]{2,1,0:T(8,128)(2,1)S(1)}, u32[]{:S(2)}, u32[]{:S(2)}) collective-permute-start(bf16[4,912,128]{2,1,0:T(8,128)(2,1)S(1)} %pad_maximum_fusion.10), channel_id=1, source_target_pairs={{0,32},{1,33},{2,34},{3,35},{4,36},{5,37},{6,38},{7,39},{8,40},{9,... | collective-permute-start | bytes 2801672 | tf_op jit(solution)/shard_map/ppermute | solution.py:41
  479.9 22.9 %collective-permute-start.89 = (bf16[4,896,128]{2,1,0:T(8,128)(2,1)S(1)}, bf16[4,896,128]{2,1,0:T(8,128)(2,1)S(1)}, u32[]{:S(2)}, u32[]{:S(2)}) collective-permute-start(bf16[4,896,128]{2,1,0:T(8,128)(2,1)S(1)} %pad_maximum_fusion.11), channel_id=1, source_target_pairs={{0,24},{1,25},{2,26},{3,27},{4,28},{5,29},{6,30},{7,31},{8,16},{9,... | collective-permute-start | bytes 2752520 | tf_op jit(solution)/shard_map/ppermute | solution.py:41
  483.4 21.4 %collective-permute-start.90 = (bf16[4,896,128]{2,1,0:T(8,128)(2,1)S(1)}, bf16[4,896,128]{2,1,0:T(8,128)(2,1)S(1)}, u32[]{:S(2)}, u32[]{:S(2)}) collective-permute-start(bf16[4,896,128]{2,1,0:T(8,128)(2,1)S(1)} %pad_maximum_fusion.12), channel_id=1, source_target_pairs={{0,8},{1,9},{2,10},{3,11},{4,12},{5,13},{6,14},{7,15},{8,0},{9,1},... | collective-permute-start | bytes 2752520 | tf_op jit(solution)/shard_map/ppermute | solution.py:41
  485.8 67.5 %collective-permute-start.65 = (bf16[128,2048]{1,0:T(8,128)(2,1)}, bf16[128,2048]{1,0:T(8,128)(2,1)S(1)}, u32[]{:S(2)}, u32[]{:S(2)}) collective-permute-start(bf16[128,2048]{1,0:T(8,128)(2,1)} %pad_maximum_fusion.22), channel_id=1, source_target_pairs={{0,2},{1,3},{2,0},{3,1},{4,6},{5,7},{6,4},{7,5},{8,10},{9,11},{10,... | collective-permute-start | bytes 1572872 | tf_op jit(solution)/shard_map/ppermute | solution.py:41
  527.4 30.2 %collective-permute-start.64 = (bf16[128,2048]{1,0:T(8,128)(2,1)}, bf16[128,2048]{1,0:T(8,128)(2,1)}, u32[]{:S(2)}, u32[]{:S(2)}) collective-permute-start(bf16[128,2048]{1,0:T(8,128)(2,1)} %pad_maximum_fusion.21), channel_id=1, source_target_pairs={{0,6},{1,7},{2,4},{3,5},{4,2},{5,3},{6,0},{7,1},{8,14},{9,15},{10,... | collective-permute-start | bytes 1572872 | tf_op jit(solution)/shard_map/ppermute | solution.py:41
  533.6 76.5 %collective-permute-start.101 = (bf16[64,2048]{0,1:T(8,128)(2,1)}, bf16[64,2048]{0,1:T(8,128)(2,1)}, u32[]{:S(2)}, u32[]{:S(2)}) collective-permute-start(bf16[64,2048]{0,1:T(8,128)(2,1)} %get-tuple-element.321), channel_id=1, source_target_pairs={{0,4},{1,5},{2,6},{3,7},{4,0},{5,1},{6,2},{7,3},{8,12},{9,13},{10,... | collective-permute-start | bytes 786440 | tf_op jit(solution)/shard_map/ppermute | solution.py:41
  (150 other events, 1774.6 us)
Sparse Core Ops, SparseCore 0:
  51.4 77.8 all-gather.2
  331.3 119.6 all-reduce.19

commit v2 on v1

v2 whole, which is shorter than its diff:
```python
import functools

import jax
import jax.numpy as jnp
from jax import lax
from jax.experimental import pallas as pl
from jax.experimental.pallas import tpu as pltpu
from jax.sharding import PartitionSpec as P

norm_eps = 1e-05
group_eps = 1.0
AXES = ("dp", "tensor")
f32 = jnp.float32
bf16 = jnp.bfloat16
NN = (((1,), (0,)), ((), ()))
NT = (((1,), (1,)), ((), ()))
TN = (((0,), (0,)), ((), ()))
MB = 1 << 20
VMEM = pl.BlockSpec(memory_space=pltpu.VMEM)
ANY = pl.BlockSpec(memory_space=pl.ANY)


def device_index(x, z, y, c):
    return ((x * 4 + z) * 2 + y // 2) * 4 + (y % 2) * 2 + c


def xor_pairs(dx=0, dz=0, dy=0, dc=0):
    return [
        (device_index(x, z, y, c), device_index(x ^ dx, z ^ dz, y ^ dy, c ^ dc))
        for x in range(4)
        for z in range(4)
        for y in range(4)
        for c in range(2)
    ]


X1, X2, X3 = (xor_pairs(dx=d) for d in (1, 2, 3))
Z1, Z2, Z3 = (xor_pairs(dz=d) for d in (1, 2, 3))
Y1, Y2, Y3 = (xor_pairs(dy=d) for d in (1, 2, 3))
C1 = xor_pairs(dc=1)
PLANES = [
    [device_index(x, z, y, c) for x in range(4) for z in range(4)]
    for y in range(4)
    for c in range(2)
]


def move(value, pairs):
    return lax.ppermute(value, AXES, pairs)


def tie(*values):
    return lax.optimization_barrier(values)


def dot(left, right, dims=NN):
    return lax.dot_general(left, right, dims, preferred_element_type=f32)


def params(mb):
    return pltpu.CompilerParams(vmem_limit_bytes=mb * MB)


def up128(n):
    return n + (-n % 128)


def stacked(*parts):
    return jnp.concatenate(parts, axis=0)


def split_kernel(q_ref, k_ref, o_ref, v_ref, s_ref, g_ref, l_ref, d_ref, keep_ref, send_ref, pack_ref):
    low = lax.axis_index("dp") % 2 == 0
    place = 0
    for ref in (q_ref, k_ref, o_ref, v_ref, s_ref):
        half = ref.shape[1] // 2
        left, right = ref[:, :half], ref[:, half:]
        keep_ref[:, place : place + half] = jnp.where(low, left, right)
        send_ref[:, place : place + half] = jnp.where(low, right, left)
        place += up128(half)
    place = 0
    for ref in (g_ref, l_ref, d_ref):
        pack_ref[:, place : place + ref.shape[1]] = ref[...]
        place += up128(ref.shape[1])


def split_weights(mixer, feed):
    size = sum(up128(w.shape[1] // 2) for w in mixer)
    pack = sum(up128(w.shape[1]) for w in feed)
    return pl.pallas_call(
        split_kernel,
        out_shape=(
            jax.ShapeDtypeStruct((64, size), bf16),
            jax.ShapeDtypeStruct((64, size), bf16),
            jax.ShapeDtypeStruct((64, pack), bf16),
        ),
        compiler_params=params(48),
    )(*mixer, *feed)


def join_kernel(groups, keep_ref, got_ref, *out_refs):
    low = lax.axis_index("dp") % 2 == 0
    place = 0
    for sizes, out_ref in zip(groups, out_refs):
        row = 0
        for size in sizes:
            wide = up128(size)
            keep, got = keep_ref[:, place : place + wide], got_ref[:, place : place + wide]
            both = stacked(jnp.where(low, keep, got), jnp.where(low, got, keep))
            out_ref[row : row + size, :] = both.T[:size]
            place += wide
            row += size


def join_weights(keep, got, *groups):
    out = pl.pallas_call(
        functools.partial(join_kernel, groups),
        out_shape=tuple(jax.ShapeDtypeStruct((sum(sizes), 128), bf16) for sizes in groups),
        compiler_params=params(16),
    )(keep, got)
    return out


def arrange_kernel(*refs):
    va, vb, out_ref, sems = refs[:4], refs[4:8], refs[8], refs[9]
    plane = lax.axis_index("dp") // 2
    ra, rb = va[0].shape[1], vb[0].shape[1]
    copies = []
    for dx in range(4):
        for dz in range(4):
            j = 4 * dx + dz
            lanes = pl.ds(pl.multiple_of(jnp.bitwise_xor(j, plane) * 128, 128), 128)
            copies.append(
                pltpu.make_async_copy(va[dz].at[dx], out_ref.at[pl.ds(0, ra), lanes], sems.at[2 * j])
            )
            copies.append(
                pltpu.make_async_copy(
                    vb[dx].at[dz], out_ref.at[pl.ds(ra, rb), lanes], sems.at[2 * j + 1]
                )
            )
    for copy in copies:
        copy.start()
    for copy in copies:
        copy.wait()


def gather_plane(a, b, later):
    ha, hb = a.shape[0] // 32 * 16, b.shape[0] // 32 * 16
    a1, a3, b1, b3 = tie(move(a, X1), move(a, X3), move(b, Z1), move(b, Z3))
    a2p, a2q, b2p, b2q = tie(
        move(a3[:ha], X1), move(a1[ha:], X3), move(b3[:hb], Z1), move(b1[hb:], Z3)
    )
    a2, b2 = stacked(a2p, a2q), stacked(b2p, b2q)
    sa, sb, later = tie(jnp.stack([a, a1, a2, a3]), jnp.stack([b, b1, b2, b3]), later)
    sa1, sa3, sb1, sb3 = tie(move(sa, Z1), move(sa, Z3), move(sb, X1), move(sb, X3))
    sa2p, sa2q, sb2p, sb2q = tie(
        move(sa3[:2], Z1), move(sa1[2:], Z3), move(sb3[:2], X1), move(sb1[2:], X3)
    )
    sa2, sb2 = stacked(sa2p, sa2q), stacked(sb2p, sb2q)
    full = pl.pallas_call(
        arrange_kernel,
        out_shape=jax.ShapeDtypeStruct((a.shape[0] + b.shape[0], 2048), bf16),
        in_specs=[ANY] * 8,
        out_specs=ANY,
        scratch_shapes=[pltpu.SemaphoreType.DMA((32,))],
        compiler_params=params(4),
    )(sa, sa1, sa2, sa3, sb, sb1, sb2, sb3)
    return full, later


def widen_kernel(in_ref, out_ref, sems):
    rows = out_ref.shape[0]
    copies = [
        pltpu.make_async_copy(
            in_ref.at[pl.ds(j * rows, rows), :], out_ref.at[:, pl.ds(128 * j, 128)], sems.at[j]
        )
        for j in range(16)
    ]
    for copy in copies:
        copy.start()
    for copy in copies:
        copy.wait()


def widen(blocks):
    rows = blocks.shape[0] // 16
    return pl.pallas_call(
        widen_kernel,
        out_shape=jax.ShapeDtypeStruct((rows, 2048), bf16),
        in_specs=[ANY],
        out_specs=ANY,
        scratch_shapes=[pltpu.SemaphoreType.DMA((16,))],
        compiler_params=params(4),
    )(blocks)


def add_low(*terms):
    total = terms[0].astype(f32)
    for term in terms[1:]:
        total = total + term.astype(f32)
    return total.astype(bf16)


def scatter_plane(a, b):
    ap, aq, bp, bq = tie(
        move(a[2, :2], Z1), move(a[2, 2:], Z3), move(b[2, :2], X1), move(b[2, 2:], X3)
    )
    a3 = stacked(add_low(a[3, :2], ap), a[3, 2:])
    a1 = stacked(a[1, :2], add_low(a[1, 2:], aq))
    b3 = stacked(add_low(b[3, :2], bp), b[3, 2:])
    b1 = stacked(b[1, :2], add_low(b[1, 2:], bq))
    a3, a1, b3, b1 = tie(a3, a1, b3, b1)
    r3, r1, s3, s1 = tie(move(a3, Z3), move(a1, Z1), move(b3, X3), move(b1, X1))
    a, b = add_low(a[0], r3, r1), add_low(b[0], s3, s1)
    a, b = tie(a, b)
    ha, hb = a.shape[1] // 32 * 16, b.shape[1] // 32 * 16
    ap, aq, bp, bq = tie(
        move(a[2, :ha], X1), move(a[2, ha:], X3), move(b[2, :hb], Z1), move(b[2, hb:], Z3)
    )
    a3 = stacked(add_low(a[3, :ha], ap), a[3, ha:])
    a1 = stacked(a[1, :ha], add_low(a[1, ha:], aq))
    b3 = stacked(add_low(b[3, :hb], bp), b[3, hb:])
    b1 = stacked(b[1, :hb], add_low(b[1, hb:], bq))
    a3, a1, b3, b1 = tie(a3, a1, b3, b1)
    r3, r1, s3, s1 = tie(move(a3, X3), move(a1, X1), move(b3, Z3), move(b1, Z1))
    return add_low(a[0], r3, r1), add_low(b[0], s3, s1)


def early_kernel(gelu_ref, linear_ref, hidden_ref, mid_ref, feed_ref, out_ref, left_ref, down_ref):
    wide = gelu_ref.shape[1]

    @pl.when(pl.program_id(0) == 0)
    def _():
        left_ref[:wide, :] = gelu_ref[...].T
        left_ref[wide:, :] = linear_ref[...].T
        down_ref[...] = hidden_ref[...].T

    up = jnp.dot(left_ref[...], mid_ref[...], preferred_element_type=f32).astype(bf16)
    down = jnp.dot(down_ref[...], feed_ref[...], preferred_element_type=f32).astype(bf16)
    for i in range(2):
        lanes = slice(128 * i, 128 * i + 128)
        out_ref[i, : 2 * wide, :] = up[:, lanes]
        out_ref[i, 2 * wide :, :] = down[:, lanes]


def early_gradients(gelu, linear, hidden, mid, feed):
    rows, wide = gelu.shape
    whole = pl.BlockSpec((rows, wide), lambda i: (0, 0))
    block = pl.BlockSpec((rows, 256), lambda i: (0, i))
    return pl.pallas_call(
        early_kernel,
        grid=(8,),
        out_shape=jax.ShapeDtypeStruct((16, 3 * wide, 128), bf16),
        in_specs=[whole, whole, whole, block, block],
        out_specs=pl.BlockSpec((2, 3 * wide, 128), lambda i: (i, 0, 0)),
        scratch_shapes=[pltpu.VMEM((2 * wide, rows), bf16), pltpu.VMEM((wide, rows), bf16)],
        compiler_params=params(32),
    )(gelu, linear, hidden, mid, feed)


def late_kernel(
    plane_ref, q_ref, k_ref, v_ref, s_ref, o_ref, x_ref, m_ref, w_ref, a_ref, b_ref, gain_ref, left_ref, out_left
):
    kwide, wide = q_ref.shape[1], v_ref.shape[1]
    keys = 2 * kwide

    @pl.when(pl.program_id(0) == 0)
    def _():
        left_ref[:kwide, :] = q_ref[...].T
        left_ref[kwide:keys, :] = k_ref[...].T
        left_ref[keys : keys + wide, :] = v_ref[...].T
        left_ref[keys + wide :, :] = s_ref[...].T
        out_left[...] = o_ref[...].T

    odd = plane_ref[0] % 2 == 1
    main = jnp.dot(left_ref[...], x_ref[...], preferred_element_type=f32)
    gain_ref[...] = jnp.sum(
        main[:keys] * w_ref[:keys, :].astype(f32), axis=0, keepdims=True
    ) + jnp.sum(main[keys:] * w_ref[keys + wide :, :].astype(f32), axis=0, keepdims=True)
    main = main.astype(bf16)
    out = jnp.dot(out_left[...], m_ref[...], preferred_element_type=f32).astype(bf16)
    for i in range(2):
        here, there = slice(128 * i, 128 * i + 128), slice(128 - 128 * i, 256 - 128 * i)
        left = jnp.where(odd, main[:, there], main[:, here])
        a_ref[i, 0, :keys, :] = left[:keys]
        a_ref[i, 0, keys:, :] = jnp.where(odd, out[:, there], out[:, here])
        b_ref[0, i, :, :] = left[keys:]


def late_gradients(plane, q, k, v, s, o, x, m, w):
    rows, kwide = q.shape
    wide = v.shape[1]
    ra, rb = 2 * kwide + wide, 2 * wide
    slim = pl.BlockSpec((rows, kwide), lambda i, p: (0, 0))
    whole = pl.BlockSpec((rows, wide), lambda i, p: (0, 0))
    block = pl.BlockSpec((rows, 256), lambda i, p: (0, jnp.bitwise_xor(i, p[0] // 2)))
    return pl.pallas_call(
        late_kernel,
        grid_spec=pltpu.PrefetchScalarGridSpec(
            num_scalar_prefetch=1,
            grid=(8,),
            in_specs=[
                slim,
                slim,
                whole,
                whole,
                whole,
                block,
                block,
                pl.BlockSpec((w.shape[0], 256), lambda i, p: (0, jnp.bitwise_xor(i, p[0] // 2))),
            ],
            out_specs=(
                pl.BlockSpec((2, 1, ra, 128), lambda i, p: (i % 2, i // 2, 0, 0)),
                pl.BlockSpec((1, 2, rb, 128), lambda i, p: (i // 2, i % 2, 0, 0)),
                pl.BlockSpec((1, 256), lambda i, p: (0, jnp.bitwise_xor(i, p[0] // 2))),
            ),
            scratch_shapes=[
                pltpu.VMEM((2 * kwide + 2 * wide, rows), bf16),
                pltpu.VMEM((wide, rows), bf16),
            ],
        ),
        out_shape=(
            jax.ShapeDtypeStruct((4, 4, ra, 128), bf16),
            jax.ShapeDtypeStruct((4, 4, rb, 128), bf16),
            jax.ShapeDtypeStruct((1, 2048), f32),
        ),
        compiler_params=params(48),
    )(plane.reshape(1), q, k, v, s, o, x, m, w)


def early_out_kernel(sum_ref, keep_ref, send_ref):
    low = lax.axis_index("dp") % 2 == 0
    wide = sum_ref.shape[0] // 3
    for i in range(3):
        flat = sum_ref[i * wide : (i + 1) * wide, :].T
        place = slice(i * up128(wide), i * up128(wide) + wide)
        keep_ref[:, place] = jnp.where(low, flat[:64], flat[64:])
        send_ref[:, place] = jnp.where(low, flat[64:], flat[:64])


def early_end_kernel(keep_ref, got_ref, *out_refs):
    wide = out_refs[0].shape[1]
    for i, out_ref in enumerate(out_refs):
        place = slice(i * up128(wide), i * up128(wide) + wide)
        out_ref[...] = keep_ref[:, place].astype(f32) + got_ref[:, place].astype(f32)


def settle_early(summed):
    wide = summed.shape[0] // 3
    flat = jax.ShapeDtypeStruct((64, 3 * up128(wide)), bf16)
    keep, send = pl.pallas_call(
        early_out_kernel, out_shape=(flat, flat), compiler_params=params(16)
    )(summed)
    return pl.pallas_call(
        early_end_kernel,
        out_shape=(jax.ShapeDtypeStruct((64, wide), f32),) * 3,
        compiler_params=params(16),
    )(keep, move(send, Y2))


def late_out_kernel(sizes, a_ref, b_ref, keep_ref, send_ref):
    low = lax.axis_index("dp") % 2 == 0
    place, row, ref = 0, 0, a_ref
    for size in sizes:
        if row == ref.shape[0]:
            row, ref = 0, b_ref
        flat = ref[row : row + size, :].T
        keep_ref[:, place : place + size] = jnp.where(low, flat[:64], flat[64:])
        send_ref[:, place : place + size] = jnp.where(low, flat[64:], flat[:64])
        row += size
        place += up128(size)


def late_end_kernel(keep_ref, got_ref, *out_refs):
    low = lax.axis_index("dp") % 2 == 0
    place = 0
    for out_ref in out_refs:
        size = out_ref.shape[1] // 2
        keep = keep_ref[:, place : place + size].astype(f32)
        got = got_ref[:, place : place + size].astype(f32)
        out_ref[:, :size] = jnp.where(low, keep, got)
        out_ref[:, size:] = jnp.where(low, got, keep)
        place += up128(size)


def settle_late(a, b, sizes):
    flat = jax.ShapeDtypeStruct((64, sum(up128(n) for n in sizes)), bf16)
    keep, send = pl.pallas_call(
        functools.partial(late_out_kernel, sizes), out_shape=(flat, flat), compiler_params=params(16)
    )(a, b)
    return pl.pallas_call(
        late_end_kernel,
        out_shape=tuple(jax.ShapeDtypeStruct((64, 2 * n), f32) for n in sizes),
        compiler_params=params(16),
    )(keep, move(send, Y2))


def gather_line(own):
    half = own.shape[0] // 2
    r1, r3 = tie(move(own, Y1), move(own, Y3))
    mine = stacked(own, r1)
    r2 = stacked(move(r3[:half], Y1), move(r1[half:], Y3))
    other = stacked(r2, r3)
    return stacked(mine, move(mine, C1), other, move(other, C1))


def scatter_line(keep_m, send_m, keep_o, send_o):
    rows = keep_m.shape[0] // 2
    half = rows // 2
    o = keep_o + move(send_o, C1).astype(f32)
    s2 = o[:rows].astype(bf16)
    t3, t1 = tie(move(s2[:half], Y1), move(s2[half:], Y3))
    m = keep_m + move(send_m, C1).astype(f32)
    s3 = stacked(o[rows : rows + half] + t3.astype(f32), o[rows + half :]).astype(bf16)
    s1 = stacked(m[rows : rows + half], m[rows + half :] + t1.astype(f32)).astype(bf16)
    u3, u1 = tie(move(s3, Y3), move(s1, Y1))
    return m[:rows] + u3.astype(f32) + u1.astype(f32)


def gather_pair(own):
    mine = stacked(own, move(own, Y1))
    return stacked(mine, move(mine, C1))


def scatter_pair(keep, send, *later):
    rows = keep.shape[0] // 2
    m = keep + move(send, C1).astype(f32)
    u1, *later = tie(move(m[rows:].astype(bf16), Y1), *later)
    return (m[:rows] + u1.astype(f32), *later)


def mixer_kernel(q_ref, k_ref, v_ref, gate_ref, decay_ref, gain_ref, retained_ref, mixed_ref):
    scores = dot(q_ref[...], k_ref[...], NT)
    weights = (scores * decay_ref[...]).astype(bf16)
    retained = dot(weights, v_ref[...])
    retained_ref[...] = retained
    center = retained - jnp.mean(retained, axis=-1, keepdims=True)
    spread = jnp.mean(center * center, axis=-1, keepdims=True)
    normed = center * lax.rsqrt(spread + group_eps)
    gate = gate_ref[...]
    mixed_ref[...] = (gate * jax.nn.sigmoid(gate) * normed * gain_ref[...]).astype(bf16)


def mixer_forward(q, k, v, gate, decay, gain):
    total, kwide = q.shape
    wide = v.shape[1]
    rows = decay.shape[0]
    slim = pl.BlockSpec((rows, kwide), lambda i: (i, 0))
    whole = pl.BlockSpec((rows, wide), lambda i: (i, 0))
    return pl.pallas_call(
        mixer_kernel,
        grid=(total // rows,),
        out_shape=(
            jax.ShapeDtypeStruct((total, wide), f32),
            jax.ShapeDtypeStruct((total, wide), bf16),
        ),
        in_specs=[
            slim,
            slim,
            whole,
            whole,
            pl.BlockSpec((rows, rows), lambda i: (0, 0)),
            pl.BlockSpec((1, wide), lambda i: (0, 0)),
        ],
        out_specs=(whole, whole),
        compiler_params=params(32),
    )(q, k, v, gate, decay, gain)


def mixer_back_kernel(
    q_ref, k_ref, v_ref, gate_ref, decay_ref, gain_ref, retained_ref, mixed_ref,
    gq_ref, gk_ref, gv_ref, gate_out_ref, gain_out_ref,
):
    q, k, v, decay = q_ref[...], k_ref[...], v_ref[...], decay_ref[...]
    gain = gain_ref[...]
    retained = retained_ref[...]
    center = retained - jnp.mean(retained, axis=-1, keepdims=True)
    rstd = lax.rsqrt(jnp.mean(center * center, axis=-1, keepdims=True) + group_eps)
    normed = center * rstd
    gate = gate_ref[...]
    sig = jax.nn.sigmoid(gate)
    grad = mixed_ref[...]
    grad_normed = grad * normed
    gate_out_ref[...] = (grad_normed * gain * (sig * (1.0 + gate * (1.0 - sig)))).astype(bf16)
    silu = gate * sig

    @pl.when(pl.program_id(0) == 0)
    def _():
        gain_out_ref[...] = jnp.zeros_like(gain_out_ref)

    gain_out_ref[...] += jnp.sum(grad_normed * silu, axis=0, keepdims=True)
    y = grad * silu * gain
    back = rstd * (
        y
        - jnp.mean(y, axis=-1, keepdims=True)
        - normed * jnp.mean(y * normed, axis=-1, keepdims=True)
    )
    back = back.astype(bf16)
    weights = (dot(q, k, NT) * decay).astype(bf16)
    grad_scores = (dot(back, v, NT) * decay).astype(bf16)
    gq_ref[...] = dot(grad_scores, k).astype(bf16)
    gk_ref[...] = dot(grad_scores, q, TN).astype(bf16)
    gv_ref[...] = dot(weights, back, TN).astype(bf16)


def mixer_backward(q, k, v, gate, decay, gain, retained, mixed):
    total, kwide = q.shape
    wide = v.shape[1]
    rows = decay.shape[0]
    slim = pl.BlockSpec((rows, kwide), lambda i: (i, 0))
    whole = pl.BlockSpec((rows, wide), lambda i: (i, 0))
    line = pl.BlockSpec((1, wide), lambda i: (0, 0))
    return pl.pallas_call(
        mixer_back_kernel,
        grid=(total // rows,),
        out_shape=(
            jax.ShapeDtypeStruct((total, kwide), bf16),
            jax.ShapeDtypeStruct((total, kwide), bf16),
            jax.ShapeDtypeStruct((total, wide), bf16),
            jax.ShapeDtypeStruct((total, wide), bf16),
            jax.ShapeDtypeStruct((1, wide), f32),
        ),
        in_specs=[
            slim,
            slim,
            whole,
            whole,
            pl.BlockSpec((rows, rows), lambda i: (0, 0)),
            line,
            whole,
            whole,
        ],
        out_specs=(slim, slim, whole, whole, line),
        compiler_params=params(32),
    )(q, k, v, gate, decay, gain, retained, mixed)


def shards(
    tokens,
    group_length,
    forget_rate,
    mixer_gain,
    feed_gain,
    group_gain,
    w_query,
    w_key,
    w_value,
    w_swish,
    w_output,
    w_gelu,
    w_linear,
    w_down,
    cotangent,
):
    rows, width = tokens.shape
    dp = lax.axis_index("dp")
    tensor = lax.axis_index("tensor")
    plane = dp // 2
    is_low = dp % 2 == 0
    feed_wide = w_gelu.shape[1]
    wide = w_value.shape[1] // 2
    kwide = w_query.shape[1] // 2
    group = 4 * rows
    half = group // 2
    score_scale = kwide ** (-0.5)
    log_keep = jnp.log1p(-jnp.where(is_low, forget_rate[0], forget_rate[1]))
    valid_rows = (tensor * rows + lax.broadcasted_iota(jnp.int32, (rows, 1), 0) < group_length[0]).astype(f32)

    keep, send, pack = split_weights(
        (w_query, w_key, w_output.T, w_value, w_swish), (w_gelu, w_linear, w_down.T)
    )
    first_a, first_b = join_weights(keep, move(send, Y2), (kwide, kwide, wide), (wide, wide))
    (second,) = join_weights(pack, move(pack, Y2), (feed_wide,) * 3)

    token_float = tokens.astype(f32)
    grad_result = cotangent.astype(f32)
    group_own = jnp.where(is_low, group_gain[:wide], group_gain[wide:]).reshape(1, wide)

    r1 = lax.rsqrt(jnp.mean(token_float * token_float, axis=-1, keepdims=True) + norm_eps)
    normed_in = (token_float * r1 * mixer_gain).astype(bf16)
    normed_group = gather_line(normed_in)
    grad_feed_out = (valid_rows * grad_result).astype(bf16)
    grad_feed_group = gather_pair(grad_feed_out)

    first_full, second = gather_plane(first_a, first_b, second)
    second_full = widen(
        lax.all_gather(second, AXES, axis_index_groups=PLANES, axis=0, tiled=True)
    )
    normed_group, grad_feed_group = tie(normed_group, grad_feed_group)
    wqk = first_full[: 2 * kwide]
    wo = first_full[2 * kwide : 2 * kwide + wide]
    wv = first_full[2 * kwide + wide : 2 * kwide + 2 * wide]
    ws = first_full[2 * kwide + 2 * wide :]
    wg, wl, wd = (second_full[i * feed_wide : (i + 1) * feed_wide] for i in range(3))

    def line_dots(pairs):
        def part(a, b, kind):
            return sum(dot(left[a:b], right) for left, right in pairs).astype(kind)

        send_o, keep_o = part(group + half, 2 * group, bf16), part(group, group + half, f32)
        send_m, keep_m = part(half, group, bf16), part(0, half, f32)
        return scatter_line(keep_m, send_m, keep_o, send_o)

    def pair_dots(pairs):
        def part(a, b, kind):
            return sum(dot(left[a:b], right) for left, right in pairs).astype(kind)

        send = part(half, group, bf16)
        return part(0, half, f32), send

    qk = dot(normed_group, wqk, NT).astype(bf16)
    q, k = qk[:, :kwide], qk[:, kwide:]
    v = dot(normed_group, wv, NT).astype(bf16)
    gate_pre = dot(normed_group, ws, NT)

    place = lax.broadcasted_iota(jnp.int32, (group, 1), 0)
    block = place // rows
    order = jnp.where(block == 1, 2, jnp.where(block == 2, 1, block))
    position = jnp.bitwise_xor(tensor, order) * rows + place % rows
    offset = position - position.reshape(1, -1)
    decay = jnp.where(
        offset >= 0, jnp.exp(jnp.maximum(offset, 0).astype(f32) * log_keep) * score_scale, 0.0
    )
    retained, mixed_low = mixer_forward(q, k, v, gate_pre, decay, group_own)
    mixer_out = line_dots([(mixed_low, wo)])
    middle = token_float + valid_rows * mixer_out
    r2 = lax.rsqrt(jnp.mean(middle * middle, axis=-1, keepdims=True) + norm_eps)
    normed_mid = (middle * r2 * feed_gain).astype(bf16)
    mid_group = gather_pair(normed_mid)
    gelu_in = dot(mid_group, wg, NT)
    linear_in = dot(mid_group, wl, NT)
    cdf = 0.5 * (1.0 + lax.erf(gelu_in * (0.5**0.5)))
    gelu = gelu_in * cdf
    gelu_slope = cdf + gelu_in * jnp.exp(-0.5 * gelu_in * gelu_in) * 0.3989422804014327
    grad_hidden = dot(grad_feed_group, wd, NT)
    hidden, grad_gelu_in, grad_linear_in = tie(
        (gelu * linear_in).astype(bf16),
        (grad_hidden * linear_in * gelu_slope).astype(bf16),
        (grad_hidden * gelu).astype(bf16),
    )
    early = early_gradients(grad_gelu_in, grad_linear_in, hidden, mid_group, grad_feed_group)
    keep, send = pair_dots([(grad_gelu_in, wg), (grad_linear_in, wl)])
    grad_normed_mid, early = scatter_pair(keep, send, early)
    early_sum = lax.psum_scatter(
        early.reshape(-1, 128), AXES, axis_index_groups=PLANES, scatter_dimension=0, tiled=True
    )

    part_feed_gain = jnp.sum(grad_normed_mid * middle * r2, axis=0)
    z2 = grad_normed_mid * feed_gain
    grad_middle = (
        grad_result + r2 * z2 - middle * (r2 * r2 * r2) * jnp.mean(z2 * middle, axis=-1, keepdims=True)
    )
    grad_mixer_out = (valid_rows * grad_middle).astype(bf16)
    keep, send = pair_dots([(hidden, wd)])
    grad_mixer_group, keep, send = tie(gather_line(grad_mixer_out), keep, send)
    (feed_out,) = scatter_pair(keep, send)
    result = (middle + valid_rows * feed_out).astype(bf16)

    grad_mixed = dot(grad_mixer_group, wo, NT)
    gq, gk, gv, grad_gate_pre, part_group_gain = mixer_backward(
        q, k, v, gate_pre, decay, group_own, retained, grad_mixed
    )
    late_a, late_b, part_mixer_gain = late_gradients(
        plane, gq, gk, gv, grad_gate_pre, mixed_low, normed_group, grad_mixer_group, first_full
    )
    grad_normed_in = line_dots([(gq, wqk[:kwide]), (gk, wqk[kwide:]), (gv, wv), (grad_gate_pre, ws)])
    sum_a, sum_b = scatter_plane(late_a, late_b)
    z1 = grad_normed_in * mixer_gain
    grad_tokens = (
        grad_middle + r1 * z1 - token_float * (r1 * r1 * r1) * jnp.mean(z1 * token_float, axis=-1, keepdims=True)
    ).astype(bf16)

    g_gelu, g_linear, g_down = settle_early(early_sum)
    g_query, g_key, g_output, g_value, g_swish = settle_late(
        sum_a, sum_b, (kwide, kwide, wide, wide, wide)
    )

    gains = jnp.concatenate(
        [part_mixer_gain.reshape(-1) / mixer_gain, part_feed_gain, part_group_gain.reshape(-1)]
    )
    for pairs in (X1, X2, Z1, Z2):
        gains = gains + move(gains, pairs)
    group_half = gains[2 * width :]
    gains = gains[: 2 * width]
    for pairs in (Y1, Y2, C1):
        gains = gains + move(gains, pairs)
    group_far = move(group_half, Y2)
    group_sum = jnp.where(
        is_low,
        jnp.concatenate([group_half, group_far]),
        jnp.concatenate([group_far, group_half]),
    )
    return (
        result,
        grad_tokens,
        gains[:width],
        gains[width:],
        group_sum,
        g_query,
        g_key,
        g_value,
        g_swish,
        g_output.T,
        g_gelu,
        g_linear,
        g_down.T,
    )


def solution(mesh):
    weight = P("dp", "tensor")
    turned = P("tensor", "dp")
    rows = P(("dp", "tensor"), None)
    return jax.shard_map(
        shards,
        mesh=mesh,
        in_specs=(
            rows,
            P("dp"),
            P("tensor"),
            P(),
            P(),
            P("tensor"),
            weight,
            weight,
            weight,
            weight,
            turned,
            weight,
            weight,
            turned,
            rows,
        ),
        out_specs=(
            rows,
            rows,
            P(),
            P(),
            P("tensor"),
            weight,
            weight,
            weight,
            weight,
            turned,
            weight,
            weight,
            turned,
        ),
        check_vma=False,
    )
```

time: 634 us -> 476 us (0.75)
  local copies, waits for them, and re-layouts: 98.4 us -> 37.7 us
  matrix products: 103 us -> 50.6 us
  between operations: 60.4 us -> 18 us
  Pallas kernels: 0 us -> 40.3 us
  other arithmetic: 66.9 us -> 27.1 us
  starting transfers between devices: 105 us -> 89.2 us
  waiting for transfers between devices: 189 us -> 204 us
    dot_general x24 -> x33, matrix products: 99.7 us -> 50.6 us  [dot(): return lax.dot_general(left, right, dims, preferred_element_type=f32)]
    unnamed x331 -> x132, local copies, waits for them, and re-layouts: 74.2 us -> 28.7 us
    pallas_call x0 -> x13, Pallas kernels: none -> 40.3 us  [the longest x1 15.7 us: late_gradients(): pl.pallas_call(late_kernel, grid_spec=pltpu.PrefetchScalarGridSpec(num_sc...]
    another operation x28 -> x8, other arithmetic: 16.7 us -> 0.49 us
    ppermute x103 -> x76, starting transfers between devices: 105 us -> 89.2 us  [move(): return lax.ppermute(value, AXES, pairs)]
    ppermute x103 -> x76, waiting for transfers between devices: 189 us -> 204 us  [move(): return lax.ppermute(value, AXES, pairs)]
    slice x33 -> x10, local copies, waits for them, and re-layouts: 15 us -> 4.69 us  [the longest x4 3.88 us: gather_line(): r2 = stacked(move(r3[:half], Y1), move(r1[half:], Y3))]
    concatenate x30 -> x21, other arithmetic: 14.5 us -> 11 us  [the longest x20 11 us: stacked(): return jnp.concatenate(parts, axis=0)]
  transfers between devices with their start and end apart: 105 -> 78, of which waited for: 58 -> 46; matrix products, arithmetic and copies ran while one was open for 34% -> 16% of each run, Pallas kernels for 0% -> 8%
where the time goes in v2:
time: 476 us; the launch traced here: 467 us
  waiting for transfers between devices  204 us (43%)
  starting transfers between devices  89.2 us (19%)
  matrix products  50.6 us (11%)
  Pallas kernels  40.3 us (8%)
  local copies, waits for them, and re-layouts  37.7 us (8%)
  other arithmetic  27.1 us (6%)
  between operations  18 us (4%)
    ppermute x76, waiting for transfers between devices, move(): return lax.ppermute(value, AXES, pairs)  204 us
    ppermute x76, starting transfers between devices, move(): return lax.ppermute(value, AXES, pairs)  89.2 us
    dot_general x33, matrix products, dot(): return lax.dot_general(left, right, dims, preferred_element_type=f32)  50.6 us
    unnamed x132, local copies, waits for them, and re-layouts  28.7 us
    pallas_call x1, Pallas kernels, late_gradients(): pl.pallas_call(late_kernel, grid_spec=pltpu.PrefetchScalarGridSpec(num_sc...  15.7 us
    concatenate x20, other arithmetic, stacked(): return jnp.concatenate(parts, axis=0)  11 us
  transfers between devices with their start and end apart: 78, of which 46 were waited for; matrix products, arithmetic and copies ran while one was open for 16% of the time, Pallas kernels for 8%

profile of v2, /device:TPU:0, one launch (start us, length us, event | category | flops | bytes accessed | tf_op | source)
XLA Modules:
  0.0 467.0 jit_solution(4970099997583857073)
XLA Ops:
  18.0 6.3 %collective-permute-done.8.got_ref = bf16[64,2048]{1,0:T(8,128)(2,1)S(1)} collective-permute-done((bf16[64,2048]{1,0:T(8,128)(2,1)S(1)}, bf16[64,2048]{1,0:T(8,128)(2,1)S(1)}, u32[]{:S(2)}, u32[]{:S(2)}) %collective-permute-start.8) | collective-permute-done | bytes 262176 | tf_op jit(solution)/shard_map/ppermute | solution.py:49
  27.6 4.0 collective-permute-start.12
  55.8 7.2 %collective-permute-done.6 = bf16[128,2048]{1,0:T(8,128)(2,1)} collective-permute-done((bf16[128,2048]{1,0:T(8,128)(2,1)S(1)}, bf16[128,2048]{1,0:T(8,128)(2,1)}, u32[]{:S(2)}, u32[]{:S(2)}) %collective-permute-start.6) | collective-permute-done | bytes 524320 | tf_op jit(solution)/shard_map/ppermute | solution.py:49
  64.3 4.7 collective-permute-done
  88.9 29.6 %collective-permute-done.21.refs_7_ = bf16[4,864,128]{2,1,0:T(8,128)(2,1)S(1)} collective-permute-done((bf16[4,864,128]{2,1,0:T(8,128)(2,1)S(1)}, bf16[4,864,128]{2,1,0:T(8,128)(2,1)S(1)}, u32[]{:S(2)}, u32[]{:S(2)}) %collective-permute-start.21) | collective-permute-done | bytes 884768 | tf_op jit(solution)/shard_map/ppermute | solution.py:49
  122.4 7.2 %collective-permute-done.19.refs_3_ = bf16[4,944,128]{2,1,0:T(8,128)(2,1)S(1)} collective-permute-done((bf16[4,944,128]{2,1,0:T(8,128)(2,1)S(1)}, bf16[4,944,128]{2,1,0:T(8,128)(2,1)S(1)}, u32[]{:S(2)}, u32[]{:S(2)}) %collective-permute-start.19) | collective-permute-done | bytes 966688 | tf_op jit(solution)/shard_map/ppermute | solution.py:49
  135.4 17.2 %collective-permute-done.25 = bf16[2,864,128]{2,1,0:T(8,128)(2,1)S(1)} collective-permute-done((bf16[2,864,128]{2,1,0:T(8,128)(2,1)S(1)}, bf16[2,864,128]{2,1,0:T(8,128)(2,1)S(1)}, u32[]{:S(2)}, u32[]{:S(2)}) %collective-permute-start.25) | collective-permute-done | bytes 442400 | tf_op jit(solution)/shard_map/ppermute | solution.py:49
  177.3 6.5 %collective-permute-done.29 = bf16[64,2048]{1,0:T(8,128)(2,1)S(1)} collective-permute-done((bf16[64,2048]{1,0:T(8,128)(2,1)S(1)}, bf16[64,2048]{1,0:T(8,128)(2,1)S(1)}, u32[]{:S(2)}, u32[]{:S(2)}) %collective-permute-start.29) | collective-permute-done | bytes 262176 | tf_op jit(solution)/shard_map/ppermute | solution.py:49
  186.6 11.1 %collective-permute-done.31 = bf16[128,2048]{1,0:T(8,128)(2,1)S(1)} collective-permute-done((bf16[128,2048]{1,0:T(8,128)(2,1)S(1)}, bf16[128,2048]{1,0:T(8,128)(2,1)S(1)}, u32[]{:S(2)}, u32[]{:S(2)}) %collective-permute-start.31) | collective-permute-done | bytes 524320 | tf_op jit(solution)/shard_map/ppermute | solution.py:49
  201.3 11.7 %collective-permute-done.32 = bf16[128,2048]{1,0:T(8,128)(2,1)S(1)} collective-permute-done((bf16[128,2048]{1,0:T(8,128)(2,1)S(1)}, bf16[128,2048]{1,0:T(8,128)(2,1)S(1)}, u32[]{:S(2)}, u32[]{:S(2)}) %collective-permute-start.32) | collective-permute-done | bytes 524320 | tf_op jit(solution)/shard_map/ppermute | solution.py:49
  214.2 4.0 copy-done.3
  221.5 4.4 fusion.16
  243.0 8.3 %shard_map.252 = bf16[16,2592,128]{2,1,0:T(8,128)(2,1)S(1)} custom-call(bf16[512,864]{1,0:T(8,128)(2,1)S(1)} %get-tuple-element.140.gelu_ref, bf16[512,864]{1,0:T(8,128)(2,1)S(1)} %get-tuple-element.141.linear_ref, bf16[512,864]{1,0:T(8,128)(2,1)S(1)} %get-tuple-element.142.hidden_ref, bf16[512,2048]{1,0:T(8,128)(2,1)S(1)} %pad_maximum_fusion.1.mid_ref, ...), custom_call_target="tpu_custom_call" | custom-call | tf_op jit(solution)/shard_map/pallas_call | solution.py:250
  263.7 12.5 %collective-permute-done.37 = bf16[128,2048]{1,0:T(8,128)(2,1)} collective-permute-done((bf16[128,2048]{1,0:T(8,128)(2,1)}, bf16[128,2048]{1,0:T(8,128)(2,1)}, u32[]{:S(2)}, u32[]{:S(2)}) %collective-permute-start.37) | collective-permute-done | bytes 524320 | tf_op jit(solution)/shard_map/ppermute | solution.py:49
  277.9 4.5 fusion.27
  286.8 4.8 %fusion.2 = f32[256,2048]{1,0:T(8,128)} fusion(bf16[2592,2048]{1,0:T(8,128)(2,1)} %copy-done.2, bf16[512,864]{1,0:T(8,128)(2,1)S(1)} %copy-done.20), kind=kOutput, calls=%fused_computation.15 | convolution fusion | flops 905969664 | bytes 6094848 | tf_op jit(solution)/shard_map/dot_general | solution.py:57
  299.4 5.3 %fusion.70.mixed_ref = f32[1024,432]{1,0:T(8,128)S(1)} fusion(bf16[1024,2048]{1,0:T(8,128)(2,1)S(1)} %constant_dynamic-update-slice_fusion.7.m_ref, bf16[1808,2048]{1,0:T(8,128)(2,1)} %copy-done), kind=kOutput, calls=%fused_computation.121 | convolution fusion | flops 1811939328 | bytes 7733248 | tf_op jit(solution)/shard_map/dot_general | solution.py:57
  304.8 4.6 shard_map.253
  313.1 15.7 %shard_map.254 = (bf16[4,4,944,128]{3,2,1,0:T(8,128)(2,1)}, bf16[4,4,864,128]{3,2,1,0:T(8,128)(2,1)}, f32[1,2048]{1,0:T(1,128)S(1)}) custom-call(s32[1]{0:T(128)} %bitcast.14.plane_ref, bf16[1024,256]{1,0:T(8,128)(2,1)S(1)} %copy-done.16, bf16[1024,256]{1,0:T(8,128)(2,1)S(1)} %copy-done.18, bf16[1024,432]{1,0:T(8,128)(2,1)S(1)} %get-tuple-element.152.v_ref, ...), custom_call_target="tpu_custom_call" | custom-call | tf_op jit(solution)/shard_map/pallas_call | solution.py:297
  344.6 8.7 %collective-permute-done.51 = f32[4528]{0:T(1024)S(1)} collective-permute-done((f32[4528]{0:T(1024)S(1)}, f32[4528]{0:T(1024)S(1)}, u32[]{:S(2)}, u32[]{:S(2)}) %collective-permute-start.51) | collective-permute-done | bytes 18144 | tf_op jit(solution)/shard_map/ppermute | solution.py:49
  359.8 8.8 %collective-permute-done.53 = f32[4528]{0:T(1024)S(1)} collective-permute-done((f32[4528]{0:T(1024)S(1)}, f32[4528]{0:T(1024)S(1)}, u32[]{:S(2)}, u32[]{:S(2)}) %collective-permute-start.53) | collective-permute-done | bytes 18144 | tf_op jit(solution)/shard_map/ppermute | solution.py:49
  395.1 5.2 %collective-permute-done.47 = bf16[64,2048]{1,0:T(8,128)(2,1)S(1)} collective-permute-done((bf16[64,2048]{1,0:T(8,128)(2,1)S(1)}, bf16[64,2048]{1,0:T(8,128)(2,1)S(1)}, u32[]{:S(2)}, u32[]{:S(2)}) %collective-permute-start.47) | collective-permute-done | bytes 262176 | tf_op jit(solution)/shard_map/ppermute | solution.py:49
  402.2 8.9 %collective-permute-done.64 = bf16[4,864,128]{2,1,0:T(8,128)(2,1)S(1)} collective-permute-done((bf16[4,864,128]{2,1,0:T(8,128)(2,1)S(1)}, bf16[4,864,128]{2,1,0:T(8,128)(2,1)S(1)}, u32[]{:S(2)}, u32[]{:S(2)}) %collective-permute-start.64) | collective-permute-done | bytes 884768 | tf_op jit(solution)/shard_map/ppermute | solution.py:49
  411.1 9.4 %collective-permute-done.65 = bf16[4,864,128]{2,1,0:T(8,128)(2,1)S(1)} collective-permute-done((bf16[4,864,128]{2,1,0:T(8,128)(2,1)S(1)}, bf16[4,864,128]{2,1,0:T(8,128)(2,1)S(1)}, u32[]{:S(2)}, u32[]{:S(2)}) %collective-permute-start.65) | collective-permute-done | bytes 884768 | tf_op jit(solution)/shard_map/ppermute | solution.py:49
  (409 shorter events, 238.1 us)
Async XLA Ops:
  7.2 207.0 %all-gather.2.cloned.1.call-start = ((), (), s32[]{:S(2)}) async-start(), calls=%async_computation.1 | async-start | bytes 11280384 | tf_op jit(solution)/shard_map/all_gather | solution.py:587
  46.0 402.4 %reduce-scatter.2.cloned.1.call-start = ((), (), s32[]{:S(2)}) async-start(), calls=%async_computation.2 | async-start | bytes 11280384 | tf_op jit(solution)/shard_map/reduce_scatter | solution.py:644
  53.1 15.8 %collective-permute-start = (bf16[128,2048]{1,0:T(8,128)(2,1)}, bf16[128,2048]{1,0:T(8,128)(2,1)S(1)}, u32[]{:S(2)}, u32[]{:S(2)}) collective-permute-start(bf16[128,2048]{1,0:T(8,128)(2,1)} %get-tuple-element.209), channel_id=1, source_target_pairs={{0,2},{1,3},{2,0},{3,1},{4,6},{5,7},{6,4},{7,5},{8,10},{9,11},{10,... | collective-permute-start | bytes 1572872 | tf_op jit(solution)/shard_map/ppermute | solution.py:49
  64.1 21.7 %collective-permute-start.7 = (bf16[256,2048]{1,0:T(8,128)(2,1)S(1)}, bf16[256,2048]{1,0:T(8,128)(2,1)S(1)}, u32[]{:S(2)}, u32[]{:S(2)}) collective-permute-start(bf16[256,2048]{1,0:T(8,128)(2,1)S(1)} %pad_maximum_fusion.4), channel_id=1, source_target_pairs={{0,1},{1,0},{2,3},{3,2},{4,5},{5,4},{6,7},{7,6},{8,9},{9,8},{10,11... | collective-permute-start | bytes 3145736 | tf_op jit(solution)/shard_map/ppermute | solution.py:49
  77.7 40.8 %collective-permute-start.21 = (bf16[4,864,128]{2,1,0:T(8,128)(2,1)S(1)}, bf16[4,864,128]{2,1,0:T(8,128)(2,1)S(1)}, u32[]{:S(2)}, u32[]{:S(2)}) collective-permute-start(bf16[4,864,128]{2,1,0:T(8,128)(2,1)S(1)} %pad_maximum_fusion.12.refs_4_), channel_id=1, source_target_pairs={{0,96},{1,97},{2,98},{3,99},{4,100},{5,101},{6,102},{7,103},{8,104... | collective-permute-start | bytes 2654216 | tf_op jit(solution)/shard_map/ppermute | solution.py:49
  81.5 40.9 %collective-permute-start.20 = (bf16[4,864,128]{2,1,0:T(8,128)(2,1)S(1)}, bf16[4,864,128]{2,1,0:T(8,128)(2,1)S(1)}, u32[]{:S(2)}, u32[]{:S(2)}) collective-permute-start(bf16[4,864,128]{2,1,0:T(8,128)(2,1)S(1)} %pad_maximum_fusion.12.refs_4_), channel_id=1, source_target_pairs={{0,32},{1,33},{2,34},{3,35},{4,36},{5,37},{6,38},{7,39},{8,40},{9,... | collective-permute-start | bytes 2654216 | tf_op jit(solution)/shard_map/ppermute | solution.py:49
  84.0 45.6 %collective-permute-start.19 = (bf16[4,944,128]{2,1,0:T(8,128)(2,1)S(1)}, bf16[4,944,128]{2,1,0:T(8,128)(2,1)S(1)}, u32[]{:S(2)}, u32[]{:S(2)}) collective-permute-start(bf16[4,944,128]{2,1,0:T(8,128)(2,1)S(1)} %pad_maximum_fusion.8.refs_0_), channel_id=1, source_target_pairs={{0,24},{1,25},{2,26},{3,27},{4,28},{5,29},{6,30},{7,31},{8,16},{9,... | collective-permute-start | bytes 2899976 | tf_op jit(solution)/shard_map/ppermute | solution.py:49
  85.9 44.4 %collective-permute-start.18 = (bf16[4,944,128]{2,1,0:T(8,128)(2,1)S(1)}, bf16[4,944,128]{2,1,0:T(8,128)(2,1)S(1)}, u32[]{:S(2)}, u32[]{:S(2)}) collective-permute-start(bf16[4,944,128]{2,1,0:T(8,128)(2,1)S(1)} %pad_maximum_fusion.8.refs_0_), channel_id=1, source_target_pairs={{0,8},{1,9},{2,10},{3,11},{4,12},{5,13},{6,14},{7,15},{8,0},{9,1},... | collective-permute-start | bytes 2899976 | tf_op jit(solution)/shard_map/ppermute | solution.py:49
  86.0 49.3 %collective-permute-start.5 = (bf16[256,2048]{1,0:T(8,128)(2,1)S(1)}, bf16[256,2048]{1,0:T(8,128)(2,1)S(1)}, u32[]{:S(2)}, u32[]{:S(2)}) collective-permute-start(bf16[256,2048]{1,0:T(8,128)(2,1)S(1)} %pad_maximum_fusion.3), channel_id=1, source_target_pairs={{0,1},{1,0},{2,3},{3,2},{4,5},{5,4},{6,7},{7,6},{8,9},{9,8},{10,11... | collective-permute-start | bytes 3145736 | tf_op jit(solution)/shard_map/ppermute | solution.py:49
  130.3 22.3 %collective-permute-start.25 = (bf16[2,864,128]{2,1,0:T(8,128)(2,1)S(1)}, bf16[2,864,128]{2,1,0:T(8,128)(2,1)S(1)}, u32[]{:S(2)}, u32[]{:S(2)}) collective-permute-start(bf16[2,864,128]{2,1,0:T(8,128)(2,1)S(1)} %slice.334), channel_id=1, source_target_pairs={{0,96},{1,97},{2,98},{3,99},{4,100},{5,101},{6,102},{7,103},{8,104... | collective-permute-start | bytes 1327112 | tf_op jit(solution)/shard_map/ppermute | solution.py:49
  133.1 20.9 %collective-permute-start.24 = (bf16[2,864,128]{2,1,0:T(8,128)(2,1)S(1)}, bf16[2,864,128]{2,1,0:T(8,128)(2,1)S(1)}, u32[]{:S(2)}, u32[]{:S(2)}) collective-permute-start(bf16[2,864,128]{2,1,0:T(8,128)(2,1)S(1)} %slice.333), channel_id=1, source_target_pairs={{0,32},{1,33},{2,34},{3,35},{4,36},{5,37},{6,38},{7,39},{8,40},{9,... | collective-permute-start | bytes 1327112 | tf_op jit(solution)/shard_map/ppermute | solution.py:49
  133.1 23.3 %collective-permute-start.22 = (bf16[2,944,128]{2,1,0:T(8,128)(2,1)S(1)}, bf16[2,944,128]{2,1,0:T(8,128)(2,1)S(1)}, u32[]{:S(2)}, u32[]{:S(2)}) collective-permute-start(bf16[2,944,128]{2,1,0:T(8,128)(2,1)S(1)} %slice.331), channel_id=1, source_target_pairs={{0,8},{1,9},{2,10},{3,11},{4,12},{5,13},{6,14},{7,15},{8,0},{9,1},... | collective-permute-start | bytes 1449992 | tf_op jit(solution)/shard_map/ppermute | solution.py:49
  133.3 24.6 %collective-permute-start.23 = (bf16[2,944,128]{2,1,0:T(8,128)(2,1)S(1)}, bf16[2,944,128]{2,1,0:T(8,128)(2,1)S(1)}, u32[]{:S(2)}, u32[]{:S(2)}) collective-permute-start(bf16[2,944,128]{2,1,0:T(8,128)(2,1)S(1)} %slice.332), channel_id=1, source_target_pairs={{0,24},{1,25},{2,26},{3,27},{4,28},{5,29},{6,30},{7,31},{8,16},{9,... | collective-permute-start | bytes 1449992 | tf_op jit(solution)/shard_map/ppermute | solution.py:49
  277.8 20.0 %collective-permute-start.38 = (bf16[256,2048]{1,0:T(8,128)(2,1)S(1)}, bf16[256,2048]{1,0:T(8,128)(2,1)S(1)}, u32[]{:S(2)}, u32[]{:S(2)}) collective-permute-start(bf16[256,2048]{1,0:T(8,128)(2,1)S(1)} %pad_maximum_fusion.6), channel_id=1, source_target_pairs={{0,1},{1,0},{2,3},{3,2},{4,5},{5,4},{6,7},{7,6},{8,9},{9,8},{10,11... | collective-permute-start | bytes 3145736 | tf_op jit(solution)/shard_map/ppermute | solution.py:49
  332.2 52.5 %collective-permute-start.61 = (bf16[2,864,128]{2,1,0:T(8,128)(2,1)S(1)}, bf16[2,864,128]{2,1,0:T(8,128)(2,1)S(1)}, u32[]{:S(2)}, u32[]{:S(2)}) collective-permute-start(bf16[2,864,128]{2,1,0:T(8,128)(2,1)S(1)} %get-tuple-element.221), channel_id=1, source_target_pairs={{0,96},{1,97},{2,98},{3,99},{4,100},{5,101},{6,102},{7,103},{8,104... | collective-permute-start | bytes 1327112 | tf_op jit(solution)/shard_map/ppermute | solution.py:49
  333.1 52.0 %collective-permute-start.60 = (bf16[2,864,128]{2,1,0:T(8,128)(2,1)S(1)}, bf16[2,864,128]{2,1,0:T(8,128)(2,1)S(1)}, u32[]{:S(2)}, u32[]{:S(2)}) collective-permute-start(bf16[2,864,128]{2,1,0:T(8,128)(2,1)S(1)} %get-tuple-element.222), channel_id=1, source_target_pairs={{0,32},{1,33},{2,34},{3,35},{4,36},{5,37},{6,38},{7,39},{8,40},{9,... | collective-permute-start | bytes 1327112 | tf_op jit(solution)/shard_map/ppermute | solution.py:49
  334.7 50.5 %collective-permute-start.59 = (bf16[2,944,128]{2,1,0:T(8,128)(2,1)S(1)}, bf16[2,944,128]{2,1,0:T(8,128)(2,1)S(1)}, u32[]{:S(2)}, u32[]{:S(2)}) collective-permute-start(bf16[2,944,128]{2,1,0:T(8,128)(2,1)S(1)} %get-tuple-element.212), channel_id=1, source_target_pairs={{0,24},{1,25},{2,26},{3,27},{4,28},{5,29},{6,30},{7,31},{8,16},{9,... | collective-permute-start | bytes 1449992 | tf_op jit(solution)/shard_map/ppermute | solution.py:49
  354.1 31.1 %collective-permute-start.58 = (bf16[2,944,128]{2,1,0:T(8,128)(2,1)S(1)}, bf16[2,944,128]{2,1,0:T(8,128)(2,1)S(1)}, u32[]{:S(2)}, u32[]{:S(2)}) collective-permute-start(bf16[2,944,128]{2,1,0:T(8,128)(2,1)S(1)} %get-tuple-element.213), channel_id=1, source_target_pairs={{0,8},{1,9},{2,10},{3,11},{4,12},{5,13},{6,14},{7,15},{8,0},{9,1},... | collective-permute-start | bytes 1449992 | tf_op jit(solution)/shard_map/ppermute | solution.py:49
  387.9 23.2 %collective-permute-start.64 = (bf16[4,864,128]{2,1,0:T(8,128)(2,1)S(1)}, bf16[4,864,128]{2,1,0:T(8,128)(2,1)S(1)}, u32[]{:S(2)}, u32[]{:S(2)}) collective-permute-start(bf16[4,864,128]{2,1,0:T(8,128)(2,1)S(1)} %get-tuple-element.168), channel_id=1, source_target_pairs={{0,96},{1,97},{2,98},{3,99},{4,100},{5,101},{6,102},{7,103},{8,104... | collective-permute-start | bytes 2654216 | tf_op jit(solution)/shard_map/ppermute | solution.py:49
  389.1 31.5 %collective-permute-start.62 = (bf16[4,944,128]{2,1,0:T(8,128)(2,1)S(1)}, bf16[4,944,128]{2,1,0:T(8,128)(2,1)S(1)}, u32[]{:S(2)}, u32[]{:S(2)}) collective-permute-start(bf16[4,944,128]{2,1,0:T(8,128)(2,1)S(1)} %get-tuple-element.166), channel_id=1, source_target_pairs={{0,24},{1,25},{2,26},{3,27},{4,28},{5,29},{6,30},{7,31},{8,16},{9,... | collective-permute-start | bytes 2899976 | tf_op jit(solution)/shard_map/ppermute | solution.py:49
  390.2 30.4 %collective-permute-start.63 = (bf16[4,944,128]{2,1,0:T(8,128)(2,1)S(1)}, bf16[4,944,128]{2,1,0:T(8,128)(2,1)S(1)}, u32[]{:S(2)}, u32[]{:S(2)}) collective-permute-start(bf16[4,944,128]{2,1,0:T(8,128)(2,1)S(1)} %get-tuple-element.167), channel_id=1, source_target_pairs={{0,8},{1,9},{2,10},{3,11},{4,12},{5,13},{6,14},{7,15},{8,0},{9,1},... | collective-permute-start | bytes 2899976 | tf_op jit(solution)/shard_map/ppermute | solution.py:49
  400.3 20.2 %collective-permute-start.65 = (bf16[4,864,128]{2,1,0:T(8,128)(2,1)S(1)}, bf16[4,864,128]{2,1,0:T(8,128)(2,1)S(1)}, u32[]{:S(2)}, u32[]{:S(2)}) collective-permute-start(bf16[4,864,128]{2,1,0:T(8,128)(2,1)S(1)} %get-tuple-element.169), channel_id=1, source_target_pairs={{0,32},{1,33},{2,34},{3,35},{4,36},{5,37},{6,38},{7,39},{8,40},{9,... | collective-permute-start | bytes 2654216 | tf_op jit(solution)/shard_map/ppermute | solution.py:49
  401.8 33.8 %collective-permute-start.43 = (bf16[128,2048]{1,0:T(8,128)(2,1)S(1)}, bf16[128,2048]{1,0:T(8,128)(2,1)S(1)}, u32[]{:S(2)}, u32[]{:S(2)}) collective-permute-start(bf16[128,2048]{1,0:T(8,128)(2,1)S(1)} %slice.678), channel_id=1, source_target_pairs={{0,2},{1,3},{2,0},{3,1},{4,6},{5,7},{6,4},{7,5},{8,10},{9,11},{10,... | collective-permute-start | bytes 1572872 | tf_op jit(solution)/shard_map/ppermute | solution.py:49
  429.9 16.9 %collective-permute-start.48 = (bf16[128,2048]{1,0:T(8,128)(2,1)S(1)}, bf16[128,2048]{1,0:T(8,128)(2,1)S(1)}, u32[]{:S(2)}, u32[]{:S(2)}) collective-permute-start(bf16[128,2048]{1,0:T(8,128)(2,1)S(1)} %pad_maximum_fusion.18), channel_id=1, source_target_pairs={{0,6},{1,7},{2,4},{3,5},{4,2},{5,3},{6,0},{7,1},{8,14},{9,15},{10,... | collective-permute-start | bytes 1572872 | tf_op jit(solution)/shard_map/ppermute | solution.py:49
  (115 other events, 878.8 us)
Sparse Core Ops, SparseCore 0:
  46.1 112.3 all-gather.1
  255.7 95.4 reduce-scatter.1

commit v3 on v2

v3 whole, which is shorter than its diff:
```python
import functools

import jax
import jax.numpy as jnp
from jax import lax
from jax.experimental import pallas as pl
from jax.experimental.pallas import tpu as pltpu
from jax.sharding import PartitionSpec as P

norm_eps = 1e-05
group_eps = 1.0
AXES = ("dp", "tensor")
f32 = jnp.float32
bf16 = jnp.bfloat16
NN = (((1,), (0,)), ((), ()))
NT = (((1,), (1,)), ((), ()))
TN = (((0,), (0,)), ((), ()))
MB = 1 << 20
VMEM = pl.BlockSpec(memory_space=pltpu.VMEM)
ANY = pl.BlockSpec(memory_space=pl.ANY)


def device_index(x, z, y, c):
    return ((x * 4 + z) * 2 + y // 2) * 4 + (y % 2) * 2 + c


def xor_pairs(dx=0, dz=0, dy=0, dc=0):
    return [
        (device_index(x, z, y, c), device_index(x ^ dx, z ^ dz, y ^ dy, c ^ dc))
        for x in range(4)
        for z in range(4)
        for y in range(4)
        for c in range(2)
    ]


X1, X2, X3 = (xor_pairs(dx=d) for d in (1, 2, 3))
Z1, Z2, Z3 = (xor_pairs(dz=d) for d in (1, 2, 3))
Y1, Y2, Y3 = (xor_pairs(dy=d) for d in (1, 2, 3))
C1 = xor_pairs(dc=1)
LINES = [
    [device_index(x, z, y, c) for y in range(4) for c in range(2)]
    for x in range(4)
    for z in range(4)
]
LINE_ORDER = ((0, 0), (1, 0), (0, 1), (1, 1), (2, 0), (3, 0), (2, 1), (3, 1))
PLANES = [
    [device_index(x, z, y, c) for x in range(4) for z in range(4)]
    for y in range(4)
    for c in range(2)
]


def move(value, pairs):
    return lax.ppermute(value, AXES, pairs)


def tie(*values):
    return lax.optimization_barrier(values)


def dot(left, right, dims=NN):
    return lax.dot_general(left, right, dims, preferred_element_type=f32)


def params(mb):
    return pltpu.CompilerParams(vmem_limit_bytes=mb * MB)


def up128(n):
    return n + (-n % 128)


def stacked(*parts):
    return jnp.concatenate(parts, axis=0)


def split_kernel(*refs):
    ins, held, (keep_ref, send_ref), sems = refs[:8], refs[10:18], refs[8:10], refs[18]
    copies = [pltpu.make_async_copy(i, h, sems.at[n]) for n, (i, h) in enumerate(zip(ins, held))]
    for copy in copies:
        copy.start()
    low = lax.axis_index("dp") % 2 == 0
    place = 0
    for n, ref in enumerate(held):
        copies[n].wait()
        if n < 5:
            half = ref.shape[1] // 2
            left, right = ref[:, :half], ref[:, half:]
            keep_ref[:, place : place + half] = jnp.where(low, left, right)
            send_ref[:, place : place + half] = jnp.where(low, right, left)
        else:
            half = ref.shape[1]
            keep_ref[:, place : place + half] = ref[...]
            send_ref[:, place : place + half] = ref[...]
        place += up128(half)


def split_weights(mixer, feed):
    size = sum(up128(w.shape[1] // 2) for w in mixer) + sum(up128(w.shape[1]) for w in feed)
    return pl.pallas_call(
        split_kernel,
        out_shape=(jax.ShapeDtypeStruct((64, size), bf16),) * 2,
        in_specs=[ANY] * 8,
        scratch_shapes=[pltpu.VMEM(w.shape, bf16) for w in (*mixer, *feed)]
        + [pltpu.SemaphoreType.DMA((8,))],
        compiler_params=params(60),
    )(*mixer, *feed)


def join_kernel(groups, keep_ref, got_ref, *out_refs):
    low = lax.axis_index("dp") % 2 == 0
    place = 0
    for sizes, out_ref in zip(groups, out_refs):
        row = 0
        for size in sizes:
            wide = up128(size)
            keep, got = keep_ref[:, place : place + wide], got_ref[:, place : place + wide]
            both = stacked(jnp.where(low, keep, got), jnp.where(low, got, keep))
            out_ref[row : row + size, :] = both.T[:size]
            place += wide
            row += size


def join_weights(keep, got, *groups):
    out = pl.pallas_call(
        functools.partial(join_kernel, groups),
        out_shape=tuple(jax.ShapeDtypeStruct((sum(sizes), 128), bf16) for sizes in groups),
        compiler_params=params(16),
    )(keep, got)
    return out


def pick_kernel(starts, *refs):
    count = len(starts)
    ins, outs, sems = refs[:count], refs[count : 2 * count], refs[2 * count]
    copies = [
        pltpu.make_async_copy(i.at[pl.ds(start, o.shape[0])], o, sems.at[n])
        for n, (i, o, start) in enumerate(zip(ins, outs, starts))
    ]
    for copy in copies:
        copy.start()
    for copy in copies:
        copy.wait()


def pick(values, starts, sizes):
    return pl.pallas_call(
        functools.partial(pick_kernel, starts),
        out_shape=tuple(
            jax.ShapeDtypeStruct((n, *v.shape[1:]), v.dtype) for v, n in zip(values, sizes)
        ),
        in_specs=[ANY] * len(values),
        out_specs=(ANY,) * len(values),
        scratch_shapes=[pltpu.SemaphoreType.DMA((len(values),))],
        compiler_params=params(4),
    )(*values)


def gather_plane(a, b):
    ha, hb = a.shape[0] // 32 * 16, b.shape[0] // 32 * 16
    a1, a3, b1, b3 = tie(move(a, X1), move(a, X3), move(b, Z1), move(b, Z3))
    a2p, a2q, b2p, b2q = tie(
        move(a3[:ha], X1), move(a1[ha:], X3), move(b3[:hb], Z1), move(b1[hb:], Z3)
    )
    a2, b2 = stacked(a2p, a2q), stacked(b2p, b2q)
    sa, sb = tie(jnp.stack([a, a1, a2, a3]), jnp.stack([b, b1, b2, b3]))
    sa1, sa3, sb1, sb3 = tie(move(sa, Z1), move(sa, Z3), move(sb, X1), move(sb, X3))
    ap, aq, bp, bq = pick((sa3, sa1, sb3, sb1), (0, 2, 0, 2), (2,) * 4)
    sa2p, sa2q, sb2p, sb2q = tie(move(ap, Z1), move(aq, Z3), move(bp, X1), move(bq, X3))
    return sa, sa1, sa2p, sa2q, sa3, sb, sb1, sb2p, sb2q, sb3


def add_low(*terms):
    total = terms[0].astype(f32)
    for term in terms[1:]:
        total = total + term.astype(f32)
    return total.astype(bf16)


def scatter_start(a, b):
    ap, aq, bp, bq = pick(
        (a.reshape(16, *a.shape[2:]),) * 2 + (b.reshape(16, *b.shape[2:]),) * 2, (8, 10, 8, 10), (2,) * 4
    )
    return move(ap, Z1), move(aq, Z3), move(bp, X1), move(bq, X3)


def scatter_add(a, b, moved, half_a, half_b):
    ap, aq, bp, bq = moved
    a3 = stacked(add_low(a[3, :half_a], ap), a[3, half_a:])
    a1 = stacked(a[1, :half_a], add_low(a[1, half_a:], aq))
    b3 = stacked(add_low(b[3, :half_b], bp), b[3, half_b:])
    b1 = stacked(b[1, :half_b], add_low(b[1, half_b:], bq))
    return tie(a3, a1, b3, b1)


def feed_kernel(
    w_ref, x0_ref, x1_ref, g_ref, hidden_ref, gelu_ref, linear_ref, keep_ref, send_ref,
    held_ref, x_ref, grad_ref, sems,
):
    wide = hidden_ref.shape[0]
    half = x0_ref.shape[0]
    given = [
        pltpu.make_async_copy(x0_ref, x_ref.at[pl.ds(0, half), :], sems.at[48]),
        pltpu.make_async_copy(x1_ref, x_ref.at[pl.ds(half, half), :], sems.at[49]),
    ]
    weights = [
        [
            pltpu.make_async_copy(
                w_ref.at[pl.ds((3 * j + i) * wide, wide), :],
                held_ref.at[pl.ds(i * wide, wide), pl.ds(128 * j, 128)],
                sems.at[16 * i + j],
            )
            for j in range(16)
        ]
        for i in range(3)
    ]
    grad = pltpu.make_async_copy(g_ref, grad_ref, sems.at[50])
    for copy in given + weights[0] + weights[1] + [grad] + weights[2]:
        copy.start()
    for copy in given + weights[0]:
        copy.wait()
    step = wide // 2
    for i in range(2):
        a, b, c = (slice(n * wide + i * step, n * wide + (i + 1) * step) for n in range(3))
        gelu_in = dot(held_ref[a, :], x_ref[...], NT)
        if i == 0:
            for copy in weights[1]:
                copy.wait()
        linear_in = dot(held_ref[b, :], x_ref[...], NT)
        if i == 0:
            for copy in [grad] + weights[2]:
                copy.wait()
        back = dot(held_ref[c, :], grad_ref[...], NT)
        cdf = 0.5 * (1.0 + lax.erf(gelu_in * (0.5**0.5)))
        gelu = gelu_in * cdf
        slope = cdf + gelu_in * jnp.exp(-0.5 * gelu_in * gelu_in) * 0.3989422804014327
        hidden_ref[a, :] = (gelu * linear_in).astype(bf16)
        gelu_ref[a, :] = (back * linear_in * slope).astype(bf16)
        linear_ref[a, :] = (back * gelu).astype(bf16)
    up, down = slice(0, wide), slice(wide, 2 * wide)
    for rows, out_ref in ((slice(half, 2 * half), send_ref), (slice(0, half), keep_ref)):
        total = dot(gelu_ref[:, rows], held_ref[up, :], TN)
        total += dot(linear_ref[:, rows], held_ref[down, :], TN)
        out_ref[...] = total.astype(out_ref.dtype)


def feed_forward_back(w, x0, x1, g):
    half, width = x0.shape
    wide = w.shape[0] // 48
    turned = jax.ShapeDtypeStruct((wide, 2 * half), bf16)
    return pl.pallas_call(
        feed_kernel,
        out_shape=(
            turned,
            turned,
            turned,
            jax.ShapeDtypeStruct((half, width), f32),
            jax.ShapeDtypeStruct((half, width), bf16),
        ),
        in_specs=[ANY] * 4,
        scratch_shapes=[
            pltpu.VMEM((3 * wide, width), bf16),
            pltpu.VMEM((2 * half, width), bf16),
            pltpu.VMEM((2 * half, width), bf16),
            pltpu.SemaphoreType.DMA((51,)),
        ],
        compiler_params=params(56),
    )(w, x0, x1, g)


def early_kernel(
    hidden_ref, gelu_ref, linear_ref, x0_ref, x1_ref, g_ref, w_ref, out_ref, keep_ref, send_ref, turn_ref
):
    wide = gelu_ref.shape[0]
    half = x0_ref.shape[0]

    @pl.when(pl.program_id(0) == 0)
    def _():
        turn_ref[...] = hidden_ref[...].T

    x = stacked(x0_ref[...], x1_ref[...])
    for n, (left, right) in enumerate(((gelu_ref, x), (linear_ref, x), (hidden_ref, g_ref[...]))):
        part = dot(left[...], right).astype(bf16)
        for i in range(2):
            out_ref[i, n * wide : (n + 1) * wide, :] = part[:, 128 * i : 128 * i + 128]
    w = jnp.concatenate([w_ref[0], w_ref[1]], axis=1)
    keep_ref[...] = dot(turn_ref[:half, :], w)
    send_ref[...] = dot(turn_ref[half:, :], w).astype(bf16)


def early_gradients(hidden, gelu, linear, x0, x1, g, w):
    wide, rows = gelu.shape
    half, width = x0.shape
    whole = pl.BlockSpec((wide, rows), lambda i: (0, 0))
    block = pl.BlockSpec((half, 256), lambda i: (0, i))
    return pl.pallas_call(
        early_kernel,
        grid=(8,),
        out_shape=(
            jax.ShapeDtypeStruct((16, 3 * wide, 128), bf16),
            jax.ShapeDtypeStruct((half, width), f32),
            jax.ShapeDtypeStruct((half, width), bf16),
        ),
        in_specs=[
            whole,
            whole,
            whole,
            block,
            block,
            pl.BlockSpec((rows, 256), lambda i: (0, i)),
            pl.BlockSpec((2, wide, 128), lambda i: (i, 2, 0)),
        ],
        out_specs=(pl.BlockSpec((2, 3 * wide, 128), lambda i: (i, 0, 0)), block, block),
        scratch_shapes=[pltpu.VMEM((rows, wide), bf16)],
        compiler_params=params(48),
    )(hidden, gelu, linear, x0, x1, g, w.reshape(16, 3 * wide, 128))


def late_kernel(plane_ref, q_ref, k_ref, o_ref, v_ref, s_ref, x_ref, *refs):
    m_refs, (a_ref, b_ref) = refs[:4], refs[4:]
    odd = plane_ref[0] % 2
    x = x_ref[...]
    row = 0
    for n, left in enumerate((q_ref, k_ref, o_ref, v_ref, s_ref)):
        if n == 2:
            step = m_refs[0].shape[0]
            part = sum(
                dot(left[:, i * step : (i + 1) * step], m_ref[...]) for i, m_ref in enumerate(m_refs)
            )
        else:
            part = dot(left[...], x)
        part = part.astype(bf16)
        rows = slice(row, row + left.shape[0])
        for i in range(2):
            there = jnp.bitwise_xor(odd, i)
            if n < 3:
                a_ref[there, 0, rows, :] = part[:, 128 * i : 128 * i + 128]
            else:
                b_ref[0, there, rows, :] = part[:, 128 * i : 128 * i + 128]
        row = 0 if n == 2 else row + left.shape[0]


def late_gradients(plane, q, k, o, v, s, x, m):
    kwide, rows = q.shape
    wide = v.shape[0]
    ra, rb = 2 * kwide + wide, 2 * wide
    slim = pl.BlockSpec((kwide, rows), lambda i, p: (0, 0))
    whole = pl.BlockSpec((wide, rows), lambda i, p: (0, 0))
    lanes = lambda i, p: (0, jnp.bitwise_xor(i, p[0] // 2))
    return pl.pallas_call(
        late_kernel,
        grid_spec=pltpu.PrefetchScalarGridSpec(
            num_scalar_prefetch=1,
            grid=(8,),
            in_specs=[slim, slim, whole, whole, whole, pl.BlockSpec((rows, 256), lanes)]
            + [pl.BlockSpec((rows // 4, 256), lanes)] * 4,
            out_specs=(
                pl.BlockSpec((2, 1, ra, 128), lambda i, p: (i % 2, i // 2, 0, 0)),
                pl.BlockSpec((1, 2, rb, 128), lambda i, p: (i // 2, i % 2, 0, 0)),
            ),
        ),
        out_shape=(
            jax.ShapeDtypeStruct((4, 4, ra, 128), bf16),
            jax.ShapeDtypeStruct((4, 4, rb, 128), bf16),
        ),
        compiler_params=params(40),
    )(plane.reshape(1), q, k, o, v, s, x, *m)


def early_out_kernel(sum_ref, keep_ref, send_ref):
    low = lax.axis_index("dp") % 2 == 0
    wide = sum_ref.shape[0] // 3
    for i in range(3):
        flat = sum_ref[i * wide : (i + 1) * wide, :].T
        place = slice(i * up128(wide), i * up128(wide) + wide)
        keep_ref[:, place] = jnp.where(low, flat[:64], flat[64:])
        send_ref[:, place] = jnp.where(low, flat[64:], flat[:64])


def early_end_kernel(keep_ref, got_ref, *out_refs):
    wide = out_refs[0].shape[1]
    for i, out_ref in enumerate(out_refs):
        place = slice(i * up128(wide), i * up128(wide) + wide)
        out_ref[...] = keep_ref[:, place].astype(f32) + got_ref[:, place].astype(f32)


def settle_early(summed):
    wide = summed.shape[0] // 3
    flat = jax.ShapeDtypeStruct((64, 3 * up128(wide)), bf16)
    keep, send = pl.pallas_call(
        early_out_kernel, out_shape=(flat, flat), compiler_params=params(16)
    )(summed)
    return pl.pallas_call(
        early_end_kernel,
        out_shape=(jax.ShapeDtypeStruct((64, wide), f32),) * 3,
        compiler_params=params(16),
    )(keep, move(send, Y2))


def late_out_kernel(sizes, a_ref, b_ref, keep_ref, send_ref):
    low = lax.axis_index("dp") % 2 == 0
    place, row, ref = 0, 0, a_ref
    for size in sizes:
        if row == ref.shape[0]:
            row, ref = 0, b_ref
        flat = ref[row : row + size, :].T
        keep_ref[:, place : place + size] = jnp.where(low, flat[:64], flat[64:])
        send_ref[:, place : place + size] = jnp.where(low, flat[64:], flat[:64])
        row += size
        place += up128(size)


def late_end_kernel(keep_ref, got_ref, *out_refs):
    low = lax.axis_index("dp") % 2 == 0
    place = 0
    for out_ref in out_refs:
        size = out_ref.shape[1] // 2
        keep = keep_ref[:, place : place + size].astype(f32)
        got = got_ref[:, place : place + size].astype(f32)
        out_ref[:, :size] = jnp.where(low, keep, got)
        out_ref[:, size:] = jnp.where(low, got, keep)
        place += up128(size)


def settle_late(a, b, sizes):
    flat = jax.ShapeDtypeStruct((64, sum(up128(n) for n in sizes)), bf16)
    keep, send = pl.pallas_call(
        functools.partial(late_out_kernel, sizes), out_shape=(flat, flat), compiler_params=params(16)
    )(a, b)
    return pl.pallas_call(
        late_end_kernel,
        out_shape=tuple(jax.ShapeDtypeStruct((64, 2 * n), f32) for n in sizes),
        compiler_params=params(16),
    )(keep, move(send, Y2))


def line_place(block):
    dp, tensor = lax.axis_index("dp"), lax.axis_index("tensor")
    y, c = dp % 2 * 2 + tensor // 2, tensor % 2
    dy, dc = LINE_ORDER[block]
    return jnp.bitwise_xor(y, dy) * 2 + jnp.bitwise_xor(c, dc)


def reorder_kernel(in_ref, out_ref, sems):
    rows = in_ref.shape[0] // 8
    copies = [
        pltpu.make_async_copy(
            in_ref.at[pl.ds(pl.multiple_of(line_place(j) * rows, rows), rows), :],
            out_ref.at[pl.ds(j * rows, rows), :],
            sems.at[j],
        )
        for j in range(8)
    ]
    for copy in copies:
        copy.start()
    for copy in copies:
        copy.wait()


def gather_line_whole(own):
    rows = lax.all_gather(own, AXES, axis_index_groups=LINES, axis=0, tiled=True)
    return pl.pallas_call(
        reorder_kernel,
        out_shape=jax.ShapeDtypeStruct(rows.shape, rows.dtype),
        in_specs=[ANY],
        out_specs=ANY,
        scratch_shapes=[pltpu.SemaphoreType.DMA((8,))],
        compiler_params=params(4),
    )(rows)


def back_kernel(q_ref, k_ref, v_ref, s_ref, w_ref, x_ref, out_ref, gain_ref, held_ref, sems):
    kwide, wide = q_ref.shape[0], v_ref.shape[0]
    rows = q_ref.shape[1] // 4
    step = pl.program_id(0)
    total = dot(q_ref[...], w_ref[:kwide, :], TN)
    total += dot(k_ref[...], w_ref[kwide : 2 * kwide, :], TN)
    total += dot(v_ref[...], w_ref[2 * kwide + wide : 2 * kwide + 2 * wide, :], TN)
    total += dot(s_ref[...], w_ref[2 * kwide + 2 * wide :, :], TN)
    held_ref[...] = total.astype(bf16)
    copies = []
    for j in range(4):
        where = jnp.where(step == 0, line_place(j), line_place(j + 4))
        copies.append(
            pltpu.make_async_copy(
                held_ref.at[pl.ds(j * rows, rows), :],
                out_ref.at[pl.ds(pl.multiple_of(where * rows, rows), rows), :],
                sems.at[j],
            )
        )
    for copy in copies:
        copy.start()
    gain = jnp.sum(total * x_ref[...].astype(f32), axis=0, keepdims=True)

    @pl.when(step == 0)
    def _():
        gain_ref[...] = gain

    @pl.when(step > 0)
    def _():
        gain_ref[...] += gain

    for copy in copies:
        copy.wait()


def input_gradients(q, k, v, s, w, x):
    kwide, total = q.shape
    wide = v.shape[0]
    half = total // 2
    slim = pl.BlockSpec((kwide, half), lambda i: (0, i))
    whole = pl.BlockSpec((wide, half), lambda i: (0, i))
    return pl.pallas_call(
        back_kernel,
        grid=(2,),
        out_shape=(
            jax.ShapeDtypeStruct((total, w.shape[1]), bf16),
            jax.ShapeDtypeStruct((1, w.shape[1]), f32),
        ),
        in_specs=[
            slim,
            slim,
            whole,
            whole,
            pl.BlockSpec(w.shape, lambda i: (0, 0)),
            pl.BlockSpec((half, w.shape[1]), lambda i: (i, 0)),
        ],
        out_specs=(ANY, pl.BlockSpec((1, w.shape[1]), lambda i: (0, 0))),
        scratch_shapes=[pltpu.VMEM((half, w.shape[1]), bf16), pltpu.SemaphoreType.DMA((4,))],
        compiler_params=params(48),
    )(q, k, v, s, w, x)


def gather_line(own):
    half = own.shape[0] // 2
    r1, r3 = tie(move(own, Y1), move(own, Y3))
    mine = stacked(own, r1)
    r2p, r2q = move(r3[:half], Y1), move(r1[half:], Y3)
    other = stacked(r2p, r2q, r3)
    return mine, move(mine, C1), other, move(other, C1)


def scatter_line(keep, send, *beside):
    rows = keep.shape[0] // 4
    half = rows // 2
    keep = keep + move(send, C1).astype(f32)
    m, o = keep[: 2 * rows], keep[2 * rows :]
    s2 = o[:rows].astype(bf16)
    t3, t1 = tie(move(s2[:half], Y1), move(s2[half:], Y3))
    s3 = stacked(o[rows : rows + half] + t3.astype(f32), o[rows + half :]).astype(bf16)
    s1 = stacked(m[rows : rows + half], m[rows + half :] + t1.astype(f32)).astype(bf16)
    u3, u1, *beside = tie(move(s3, Y3), move(s1, Y1), *beside)
    return (m[:rows] + u3.astype(f32) + u1.astype(f32), *beside)


def gather_pair(own):
    mine = stacked(own, move(own, Y1))
    return mine, move(mine, C1)


def scatter_pair(keep, send, *beside):
    rows = keep.shape[0] // 2
    m = keep + move(send, C1).astype(f32)
    u1, *beside = tie(move(m[rows:].astype(bf16), Y1), *beside)
    return (m[:rows] + u1.astype(f32), *beside)


def mixer_kernel(*refs):
    blocks, (x_ref, decay_ref, gain_ref) = refs[:10], refs[10:13]
    w_out, q_ref, k_ref, v_ref, gate_ref, retained_ref, mixed_ref, keep_ref, send_ref = refs[13:22]
    w_ref, sems = refs[22:]
    va, vb = blocks[:5], blocks[5:]
    kwide, wide = q_ref.shape[1], v_ref.shape[1]
    half = keep_ref.shape[0]
    plane = lax.axis_index("dp") // 2
    ra, rb = va[0].shape[1], vb[0].shape[1]
    step = pl.program_id(0)
    copies = []
    for dx in range(4):
        for dz in range(4):
            j = 4 * dx + dz
            lanes = pl.ds(pl.multiple_of(jnp.bitwise_xor(j, plane) * 128, 128), 128)
            for n, (first, then, start, size) in enumerate(((dz, dx, 0, ra), (dx, dz, ra, rb))):
                part = (va, vb)[n]
                if first == 2:
                    source = part[2 + then // 2].at[then % 2]
                else:
                    source = part[(0, 1, None, 4)[first]].at[then]
                copies.append(
                    pltpu.make_async_copy(source, w_ref.at[pl.ds(start, size), lanes], sems.at[2 * j + n])
                )
    back = pltpu.make_async_copy(w_ref, w_out, sems.at[32])

    @pl.when(step == 0)
    def _():
        for copy in copies:
            copy.start()
        for copy in copies:
            copy.wait()
        back.start()

    keys = 2 * kwide
    x = x_ref[...]
    q = dot(x, w_ref[:kwide, :], NT).astype(bf16)
    k = dot(x, w_ref[kwide:keys, :], NT).astype(bf16)
    v = dot(x, w_ref[keys + wide : keys + 2 * wide, :], NT).astype(bf16)
    gate = dot(x, w_ref[keys + 2 * wide :, :], NT)
    q_ref[...], k_ref[...], v_ref[...], gate_ref[...] = q, k, v, gate
    weights = (dot(q, k, NT) * decay_ref[...]).astype(bf16)
    retained = dot(weights, v)
    retained_ref[...] = retained
    center = retained - jnp.mean(retained, axis=-1, keepdims=True)
    spread = jnp.mean(center * center, axis=-1, keepdims=True)
    normed = center * lax.rsqrt(spread + group_eps)
    mixed = (gate * jax.nn.sigmoid(gate) * normed * gain_ref[...]).astype(bf16)
    mixed_ref[...] = mixed.T
    wo = w_ref[keys : keys + wide, :]
    send_ref[...] = dot(mixed[half:], wo).astype(bf16)
    keep_ref[...] = dot(mixed[:half], wo)

    @pl.when(step == 1)
    def _():
        back.wait()


def mixer_forward(blocks, x, decay, gain, kwide):
    total, width = x.shape
    rows = decay.shape[0]
    wide = gain.shape[1]
    size = 2 * kwide + 3 * wide
    slim = pl.BlockSpec((rows, kwide), lambda i: (i, 0))
    whole = pl.BlockSpec((rows, wide), lambda i: (i, 0))
    part = pl.BlockSpec((rows // 2, width), lambda i: (i, 0))
    return pl.pallas_call(
        mixer_kernel,
        grid=(2,),
        out_shape=(
            jax.ShapeDtypeStruct((size, width), bf16),
            jax.ShapeDtypeStruct((total, kwide), bf16),
            jax.ShapeDtypeStruct((total, kwide), bf16),
            jax.ShapeDtypeStruct((total, wide), bf16),
            jax.ShapeDtypeStruct((total, wide), f32),
            jax.ShapeDtypeStruct((total, wide), f32),
            jax.ShapeDtypeStruct((wide, total), bf16),
            jax.ShapeDtypeStruct((rows, width), f32),
            jax.ShapeDtypeStruct((rows, width), bf16),
        ),
        in_specs=[ANY] * 10
        + [
            pl.BlockSpec((rows, width), lambda i: (i, 0)),
            pl.BlockSpec((rows, rows), lambda i: (0, 0)),
            pl.BlockSpec((1, wide), lambda i: (0, 0)),
        ],
        out_specs=(
            ANY,
            slim,
            slim,
            whole,
            whole,
            whole,
            pl.BlockSpec((wide, rows), lambda i: (0, i)),
            part,
            part,
        ),
        scratch_shapes=[pltpu.VMEM((size, width), bf16), pltpu.SemaphoreType.DMA((33,))],
        compiler_params=params(56),
    )(*blocks, x, decay, gain)


def mixer_back_kernel(
    g0_ref, g1_ref, g2_ref, g3_ref, w_ref, q_ref, k_ref, v_ref, gate_ref, decay_ref, gain_ref, retained_ref,
    gq_ref, gk_ref, gv_ref, gate_out_ref, gain_out_ref, grad_ref, wo_ref, sems,
):
    kwide, wide = q_ref.shape[1], v_ref.shape[1]
    rows, half = q_ref.shape[0], g0_ref.shape[0]
    step = pl.program_id(0)
    copies = [
        pltpu.make_async_copy(g_ref, grad_ref.at[pl.ds(i * half, half), :], sems.at[i])
        for i, g_ref in enumerate((g0_ref, g1_ref, g2_ref, g3_ref))
    ]
    weight = pltpu.make_async_copy(w_ref.at[pl.ds(2 * kwide, wide), :], wo_ref, sems.at[4])

    @pl.when(step == 0)
    def _():
        weight.start()
        for copy in copies:
            copy.start()
        weight.wait()
        copies[0].wait()
        copies[1].wait()

    @pl.when(step == 1)
    def _():
        copies[2].wait()
        copies[3].wait()

    grad = dot(grad_ref[pl.ds(pl.multiple_of(step * rows, rows), rows), :], wo_ref[...], NT)
    q, k, v, decay = q_ref[...], k_ref[...], v_ref[...], decay_ref[...]
    gain = gain_ref[...]
    retained = retained_ref[...]
    center = retained - jnp.mean(retained, axis=-1, keepdims=True)
    rstd = lax.rsqrt(jnp.mean(center * center, axis=-1, keepdims=True) + group_eps)
    normed = center * rstd
    gate = gate_ref[...]
    sig = jax.nn.sigmoid(gate)
    grad_normed = grad * normed
    gate_out_ref[...] = (grad_normed * gain * (sig * (1.0 + gate * (1.0 - sig)))).astype(bf16).T
    silu = gate * sig
    gain_part = jnp.sum(grad_normed * silu, axis=0, keepdims=True)

    @pl.when(step == 0)
    def _():
        gain_out_ref[...] = gain_part

    @pl.when(step > 0)
    def _():
        gain_out_ref[...] += gain_part

    y = grad * silu * gain
    back = rstd * (
        y
        - jnp.mean(y, axis=-1, keepdims=True)
        - normed * jnp.mean(y * normed, axis=-1, keepdims=True)
    )
    back = back.astype(bf16)
    weights = (dot(q, k, NT) * decay).astype(bf16)
    grad_scores = (dot(back, v, NT) * decay).astype(bf16)
    gq_ref[...] = dot(grad_scores, k).astype(bf16).T
    gk_ref[...] = dot(q, grad_scores, TN).astype(bf16)
    gv_ref[...] = dot(back, weights, TN).astype(bf16)


def mixer_backward(grads, w, q, k, v, gate, decay, gain, retained):
    total, kwide = q.shape
    wide = v.shape[1]
    rows = decay.shape[0]
    slim = pl.BlockSpec((rows, kwide), lambda i: (i, 0))
    whole = pl.BlockSpec((rows, wide), lambda i: (i, 0))
    line = pl.BlockSpec((1, wide), lambda i: (0, 0))
    slim_turned = pl.BlockSpec((kwide, rows), lambda i: (0, i))
    whole_turned = pl.BlockSpec((wide, rows), lambda i: (0, i))
    return pl.pallas_call(
        mixer_back_kernel,
        grid=(2,),
        out_shape=(
            jax.ShapeDtypeStruct((kwide, total), bf16),
            jax.ShapeDtypeStruct((kwide, total), bf16),
            jax.ShapeDtypeStruct((wide, total), bf16),
            jax.ShapeDtypeStruct((wide, total), bf16),
            jax.ShapeDtypeStruct((1, wide), f32),
        ),
        in_specs=[ANY] * 5
        + [slim, slim, whole, whole, pl.BlockSpec((rows, rows), lambda i: (0, 0)), line, whole],
        out_specs=(slim_turned, slim_turned, whole_turned, whole_turned, line),
        scratch_shapes=[
            pltpu.VMEM((total, w.shape[1]), bf16),
            pltpu.VMEM((wide, w.shape[1]), bf16),
            pltpu.SemaphoreType.DMA((5,)),
        ],
        compiler_params=params(48),
    )(*grads, w, q, k, v, gate, decay, gain, retained)


def shards(
    tokens,
    group_length,
    forget_rate,
    mixer_gain,
    feed_gain,
    group_gain,
    w_query,
    w_key,
    w_value,
    w_swish,
    w_output,
    w_gelu,
    w_linear,
    w_down,
    cotangent,
):
    rows, width = tokens.shape
    dp = lax.axis_index("dp")
    tensor = lax.axis_index("tensor")
    plane = dp // 2
    is_low = dp % 2 == 0
    feed_wide = w_gelu.shape[1]
    wide = w_value.shape[1] // 2
    kwide = w_query.shape[1] // 2
    group = 4 * rows
    score_scale = kwide ** (-0.5)
    log_keep = jnp.log1p(-jnp.where(is_low, forget_rate[0], forget_rate[1]))
    valid_rows = (tensor * rows + lax.broadcasted_iota(jnp.int32, (rows, 1), 0) < group_length[0]).astype(f32)

    keep, send = split_weights(
        (w_query, w_key, w_output.T, w_value, w_swish), (w_gelu, w_linear, w_down.T)
    )
    token_float = tokens.astype(f32)
    grad_result = cotangent.astype(f32)
    group_own = jnp.where(is_low, group_gain[:wide], group_gain[wide:]).reshape(1, wide)

    r1 = lax.rsqrt(jnp.mean(token_float * token_float, axis=-1, keepdims=True) + norm_eps)
    normed_in = (token_float * r1 * mixer_gain).astype(bf16)
    got, normed_in = tie(move(send, Y2), normed_in)
    first_a, first_b, second = join_weights(
        keep, got, (kwide, kwide, wide), (wide, wide), (feed_wide,) * 3
    )
    normed_group = gather_line_whole(normed_in)
    grad_feed_out = (valid_rows * grad_result).astype(bf16)
    grad_feed_group = gather_pair(grad_feed_out)

    first = gather_plane(first_a, first_b)
    second = lax.all_gather(second, AXES, axis_index_groups=PLANES, axis=0, tiled=True)
    normed_group, grad_feed_group = tie(normed_group, stacked(*grad_feed_group))

    place = lax.broadcasted_iota(jnp.int32, (group, 1), 0)
    block = place // rows
    order = jnp.where(block == 1, 2, jnp.where(block == 2, 1, block))
    position = jnp.bitwise_xor(tensor, order) * rows + place % rows
    offset = position - position.reshape(1, -1)
    decay = jnp.where(
        offset >= 0, jnp.exp(jnp.maximum(offset, 0).astype(f32) * log_keep) * score_scale, 0.0
    )
    w_mixer, q, k, v, gate, retained, mixed, keep, send = mixer_forward(
        first, normed_group, decay, group_own, kwide
    )
    (mixer_out,) = scatter_line(keep, send)
    middle = token_float + valid_rows * mixer_out
    r2 = lax.rsqrt(jnp.mean(middle * middle, axis=-1, keepdims=True) + norm_eps)
    normed_mid = (middle * r2 * feed_gain).astype(bf16)
    mid = gather_pair(normed_mid)
    hidden, grad_gelu, grad_linear, keep, send = feed_forward_back(second, *mid, grad_feed_group)
    early, feed_keep, feed_send = early_gradients(
        hidden, grad_gelu, grad_linear, *mid, grad_feed_group, second
    )
    grad_normed_mid, early, feed_keep, feed_send = scatter_pair(keep, send, early, feed_keep, feed_send)
    early_sum = lax.psum_scatter(
        early.reshape(-1, 128), AXES, axis_index_groups=PLANES, scatter_dimension=0, tiled=True
    )

    part_feed_gain = jnp.sum(grad_normed_mid * middle * r2, axis=0)
    z2 = grad_normed_mid * feed_gain
    grad_middle = (
        grad_result + r2 * z2 - middle * (r2 * r2 * r2) * jnp.mean(z2 * middle, axis=-1, keepdims=True)
    )
    grad_mixer_out = (valid_rows * grad_middle).astype(bf16)
    grad_mixer = gather_line(grad_mixer_out)
    *grad_mixer, feed_send = tie(*grad_mixer, feed_send)
    gq, gk, gv, gs, part_group_gain = mixer_backward(
        grad_mixer, w_mixer, q, k, v, gate, decay, group_own, retained
    )
    a, b = late_gradients(plane, gq, gk, mixed, gv, gs, normed_group, grad_mixer)
    a, b, gq, feed_got = tie(a, b, gq, move(feed_send, C1))

    back, part_mixer_gain = input_gradients(gq, gk, gv, gs, w_mixer, normed_group)
    feed_keep = feed_keep + feed_got.astype(f32)
    feed_far = move(feed_keep[rows:].astype(bf16), Y1)
    *moved, back, part_mixer_gain, feed_far = tie(
        *scatter_start(a, b), back, part_mixer_gain, feed_far
    )
    result = (middle + valid_rows * (feed_keep[:rows] + feed_far.astype(f32))).astype(bf16)
    a3, a1, b3, b1 = scatter_add(a, b, moved, 2, 2)
    moved = move(a3, Z3), move(a1, Z1), move(b3, X3), move(b1, X1)
    gains = jnp.concatenate([part_mixer_gain.reshape(-1) / mixer_gain, part_feed_gain])
    for pairs in (C1, Y1, Y2):
        gains = gains + move(gains, pairs)
    part_group_gain = part_group_gain.reshape(-1)
    group_far = move(part_group_gain, Y2)
    gains = jnp.concatenate(
        [
            gains,
            jnp.where(is_low, part_group_gain, group_far),
            jnp.where(is_low, group_far, part_group_gain),
        ]
    )
    gains = gains + move(gains, X1)
    r3, r1_, s3, s1, gains, early_sum, back = tie(*moved, gains, early_sum, back)
    grad_normed_in = lax.psum_scatter(
        back, AXES, axis_index_groups=LINES, scatter_dimension=0, tiled=True
    ).astype(f32)
    a, b = tie(add_low(a[0], r3, r1_), add_low(b[0], s3, s1))
    ha, hb = a.shape[1] // 32 * 16, b.shape[1] // 32 * 16
    *moved, gains = tie(
        move(a[2, :ha], X1),
        move(a[2, ha:], X3),
        move(b[2, :hb], Z1),
        move(b[2, hb:], Z3),
        gains + move(gains, X2),
    )
    a3, a1, b3, b1 = scatter_add(a, b, moved, ha, hb)
    r3, r1_, s3, s1, gains, g_gelu, g_linear, g_down = tie(
        move(a3, X3),
        move(a1, X1),
        move(b3, Z3),
        move(b1, Z1),
        gains + move(gains, Z1),
        *settle_early(early_sum),
    )
    sum_a, sum_b = add_low(a[0], r3, r1_), add_low(b[0], s3, s1)
    gains = gains + move(gains, Z2)
    z1 = grad_normed_in * mixer_gain
    grad_tokens = (
        grad_middle + r1 * z1 - token_float * (r1 * r1 * r1) * jnp.mean(z1 * token_float, axis=-1, keepdims=True)
    ).astype(bf16)

    g_query, g_key, g_output, g_value, g_swish = settle_late(
        sum_a, sum_b, (kwide, kwide, wide, wide, wide)
    )

    return (
        result,
        grad_tokens,
        gains[:width],
        gains[width : 2 * width],
        gains[2 * width :],
        g_query,
        g_key,
        g_value,
        g_swish,
        g_output.T,
        g_gelu,
        g_linear,
        g_down.T,
    )


def solution(mesh):
    weight = P("dp", "tensor")
    turned = P("tensor", "dp")
    rows = P(("dp", "tensor"), None)
    return jax.shard_map(
        shards,
        mesh=mesh,
        in_specs=(
            rows,
            P("dp"),
            P("tensor"),
            P(),
            P(),
            P("tensor"),
            weight,
            weight,
            weight,
            weight,
            turned,
            weight,
            weight,
            turned,
            rows,
        ),
        out_specs=(
            rows,
            rows,
            P(),
            P(),
            P("tensor"),
            weight,
            weight,
            weight,
            weight,
            turned,
            weight,
            weight,
            turned,
        ),
        check_vma=False,
    )
```

time: 476 us -> 400 us (0.84)
  waiting for transfers between devices: 204 us -> 141 us
  Pallas kernels: 40.3 us -> 94.9 us
  matrix products: 50.6 us -> 0 us
  local copies, waits for them, and re-layouts: 37.7 us -> 22.9 us
  other arithmetic: 27.1 us -> 41.5 us
  starting transfers between devices: 89.2 us -> 75.9 us
    ppermute x76 -> x62, waiting for transfers between devices: 204 us -> 138 us  [move(): return lax.ppermute(value, AXES, pairs)]
    pallas_call x5 -> x8, Pallas kernels: 20.7 us -> 76.3 us  [the longest x1 18.9 us: mixer_forward(): pl.pallas_call(mixer_kernel, grid=(2,), out_shape=(jax.ShapeDtypeStruct((...]
    dot_general x33 -> x0, matrix products: 50.6 us -> none  [dot(): return lax.dot_general(left, right, dims, preferred_element_type=f32)]
    ppermute x76 -> x62, starting transfers between devices: 89.2 us -> 75.8 us  [move(): return lax.ppermute(value, AXES, pairs)]
    unnamed x132 -> x134, local copies, waits for them, and re-layouts: 28.7 us -> 17.3 us
    convert_element_type x9, other arithmetic: 1.55 us -> 7.36 us  [add_low(): return total.astype(bf16)]
    another operation x8 -> x6, other arithmetic: 0.49 us -> 5.58 us
    concatenate x20 -> x12, other arithmetic: 11 us -> 7.06 us  [stacked(): return jnp.concatenate(parts, axis=0)]
  transfers between devices with their start and end apart: 78 -> 66, of which waited for: 46 -> 33; matrix products, arithmetic and copies ran while one was open for 16% -> 11% of each run, Pallas kernels for 8% -> 19%
where the time goes in v3:
time: 400 us; the launch traced here: 393 us
  waiting for transfers between devices  141 us (35%)
  Pallas kernels  94.9 us (24%)
  starting transfers between devices  75.9 us (19%)
  other arithmetic  41.5 us (10%)
  local copies, waits for them, and re-layouts  22.9 us (6%)
  between operations  17.2 us (4%)
    ppermute x62, waiting for transfers between devices, move(): return lax.ppermute(value, AXES, pairs)  138 us
    ppermute x62, starting transfers between devices, move(): return lax.ppermute(value, AXES, pairs)  75.8 us
    pallas_call x1, Pallas kernels, mixer_forward(): pl.pallas_call(mixer_kernel, grid=(2,), out_shape=(jax.ShapeDtypeStruct((...  18.9 us
    unnamed x134, local copies, waits for them, and re-layouts  17.3 us
    pallas_call x1, Pallas kernels, feed_forward_back(): pl.pallas_call(feed_kernel, out_shape=(turned, turned, turned, jax.ShapeD...  15.9 us
    pallas_call x1, Pallas kernels, input_gradients(): pl.pallas_call(back_kernel, grid=(2,), out_shape=(jax.ShapeDtypeStruct((t...  13.7 us
    pallas_call x1, Pallas kernels, early_gradients(): pl.pallas_call(early_kernel, grid=(8,), out_shape=(jax.ShapeDtypeStruct((...  13.3 us
    pallas_call x1, Pallas kernels, late_gradients(): pl.pallas_call(late_kernel, grid_spec=pltpu.PrefetchScalarGridSpec(num_sc...  12.5 us
  transfers between devices with their start and end apart: 66, of which 33 were waited for; matrix products, arithmetic and copies ran while one was open for 11% of the time, Pallas kernels for 19%

profile of v3, /device:TPU:0, one launch (start us, length us, event | category | flops | bytes accessed | tf_op | source)
XLA Modules:
  0.0 393.5 jit_solution(9989848507385875413)
XLA Ops:
  9.9 3.4 collective-permute-start
  17.1 10.0 %collective-permute-done.got_ref = bf16[64,4736]{1,0:T(8,128)(2,1)S(1)} collective-permute-done((bf16[64,4736]{1,0:T(8,128)(2,1)}, bf16[64,4736]{1,0:T(8,128)(2,1)S(1)}, u32[]{:S(2)}, u32[]{:S(2)}) %collective-permute-start) | collective-permute-done | bytes 606240 | tf_op jit(solution)/shard_map/ppermute | solution.py:55
  57.8 12.5 %collective-permute-done.17 = bf16[128,2048]{1,0:T(8,128)(2,1)S(1)} collective-permute-done((bf16[128,2048]{1,0:T(8,128)(2,1)S(1)}, bf16[128,2048]{1,0:T(8,128)(2,1)S(1)}, u32[]{:S(2)}, u32[]{:S(2)}) %collective-permute-start.17) | collective-permute-done | bytes 524320 | tf_op jit(solution)/shard_map/ppermute | solution.py:55
  86.8 7.8 %collective-permute-done.15.refs_7_ = bf16[2,864,128]{2,1,0:T(8,128)(2,1)S(1)} collective-permute-done((bf16[2,864,128]{2,1,0:T(8,128)(2,1)S(1)}, bf16[2,864,128]{2,1,0:T(8,128)(2,1)S(1)}, u32[]{:S(2)}, u32[]{:S(2)}) %collective-permute-start.15) | collective-permute-done | bytes 442400 | tf_op jit(solution)/shard_map/ppermute | solution.py:55
  94.6 4.6 %collective-permute-done.16.refs_8_ = bf16[2,864,128]{2,1,0:T(8,128)(2,1)S(1)} collective-permute-done((bf16[2,864,128]{2,1,0:T(8,128)(2,1)S(1)}, bf16[2,864,128]{2,1,0:T(8,128)(2,1)S(1)}, u32[]{:S(2)}, u32[]{:S(2)}) %collective-permute-start.16) | collective-permute-done | bytes 442400 | tf_op jit(solution)/shard_map/ppermute | solution.py:55
  105.3 18.9 %shard_map.250 = (bf16[1808,2048]{1,0:T(8,128)(2,1)}, bf16[1024,256]{1,0:T(8,128)(2,1)}, bf16[1024,256]{1,0:T(8,128)(2,1)}, bf16[1024,432]{1,0:T(8,128)(2,1)}, f...) custom-call(bf16[4,944,128]{2,1,0:T(8,128)(2,1)} %pad_maximum_fusion, ...), custom_call_target="tpu_custom_call" | custom-call | tf_op jit(solution)/shard_map/pallas_call | solution.py:635
  124.3 4.4 %collective-permute-done.19 = bf16[512,2048]{1,0:T(8,128)(2,1)S(1)} collective-permute-done((bf16[512,2048]{1,0:T(8,128)(2,1)}, bf16[512,2048]{1,0:T(8,128)(2,1)S(1)}, u32[]{:S(2)}, u32[]{:S(2)}) %collective-permute-start.19) | collective-permute-done | bytes 2097184 | tf_op jit(solution)/shard_map/ppermute | solution.py:55
  136.0 4.4 %collective-permute-done.20 = bf16[64,2048]{1,0:T(8,128)(2,1)S(1)} collective-permute-done((bf16[64,2048]{1,0:T(8,128)(2,1)S(1)}, bf16[64,2048]{1,0:T(8,128)(2,1)S(1)}, u32[]{:S(2)}, u32[]{:S(2)}) %collective-permute-start.20) | collective-permute-done | bytes 262176 | tf_op jit(solution)/shard_map/ppermute | solution.py:55
  145.6 11.8 %collective-permute-done.22 = bf16[128,2048]{1,0:T(8,128)(2,1)S(1)} collective-permute-done((bf16[128,2048]{1,0:T(8,128)(2,1)S(1)}, bf16[128,2048]{1,0:T(8,128)(2,1)S(1)}, u32[]{:S(2)}, u32[]{:S(2)}) %collective-permute-start.22) | collective-permute-done | bytes 524320 | tf_op jit(solution)/shard_map/ppermute | solution.py:55
  159.1 11.5 %collective-permute-done.24 = bf16[128,2048]{1,0:T(8,128)(2,1)S(1)} collective-permute-done((bf16[128,2048]{1,0:T(8,128)(2,1)S(1)}, bf16[128,2048]{1,0:T(8,128)(2,1)S(1)}, u32[]{:S(2)}, u32[]{:S(2)}) %collective-permute-start.24) | collective-permute-done | bytes 524320 | tf_op jit(solution)/shard_map/ppermute | solution.py:55
  174.6 15.9 %shard_map.251 = (bf16[864,512]{1,0:T(8,128)(2,1)}, bf16[864,512]{1,0:T(8,128)(2,1)}, bf16[864,512]{1,0:T(8,128)(2,1)}, f32[256,2048]{1,0:T(8,128)}, bf16[256,2048]{1,0:T(8,128)(2,1)}) custom-call(bf16[41472,128]{1,0:T(8,128)(2,1)} %all-gather.5.cloned.1.call-done.w_ref, bf16[256,2048]{1,0:T(8,128)(2,1)} %copy-done.2, bf16[256,2048]{1,0:T(8,128)(2,1)} %copy-done.8, ...), custom_call_target="tpu_custom_call" | custom-call | tf_op jit(solution)/shard_map/pallas_call | solution.py:252
  196.4 13.3 %shard_map.252 = (bf16[16,2592,128]{2,1,0:T(8,128)(2,1)}, f32[256,2048]{1,0:T(8,128)}, bf16[256,2048]{1,0:T(8,128)(2,1)}) custom-call(bf16[864,512]{1,0:T(8,128)(2,1)S(1)} %copy-done.19, bf16[864,512]{1,0:T(8,128)(2,1)S(1)} %copy-done.20, bf16[864,512]{1,0:T(8,128)(2,1)S(1)} %copy-done.21, bf16[256,2048]{1,0:T(8,128)(2,1)S(1)} %copy-done.3, ...), custom_call_target="tpu_custom_call" | custom-call | tf_op jit(solution)/shard_map/pallas_call | solution.py:297
  217.6 11.1 %collective-permute-done.28 = bf16[128,2048]{1,0:T(8,128)(2,1)S(1)} collective-permute-done((bf16[128,2048]{1,0:T(8,128)(2,1)S(1)}, bf16[128,2048]{1,0:T(8,128)(2,1)S(1)}, u32[]{:S(2)}, u32[]{:S(2)}) %collective-permute-start.28) | collective-permute-done | bytes 524320 | tf_op jit(solution)/shard_map/ppermute | solution.py:55
  232.6 5.0 %collective-permute-done.31 = bf16[64,2048]{1,0:T(8,128)(2,1)S(1)} collective-permute-done((bf16[64,2048]{1,0:T(8,128)(2,1)S(1)}, bf16[64,2048]{1,0:T(8,128)(2,1)S(1)}, u32[]{:S(2)}, u32[]{:S(2)}) %collective-permute-start.31) | collective-permute-done | bytes 262176 | tf_op jit(solution)/shard_map/ppermute | solution.py:55
  245.0 11.0 %shard_map.253 = (bf16[256,1024]{1,0:T(8,128)(2,1)S(1)}, bf16[256,1024]{1,0:T(8,128)(2,1)S(1)}, bf16[432,1024]{1,0:T(8,128)(2,1)S(1)}, bf16[432,1024]{1,0:T(8,128)(2,1)S(1)}, f32[1,432]{1,0:T(1,128)S(1)}) custom-call(bf16[256,2048]{1,0:T(8,128)(2,1)S(1)} %pad_maximum_fusion.3.g0_ref.refs_0_, bf16[256,2048]{1,0:T(8,128)(2,1)S(1)} %collective-permute-done.30.g1_ref.refs_1_, ...), custom_call_target="tpu_custom_call" | custom-call | tf_op jit(solution)/shard_map/pallas_call | solution.py:743
  259.8 12.5 %shard_map.254 = (bf16[4,4,944,128]{3,2,1,0:T(8,128)(2,1)}, bf16[4,4,864,128]{3,2,1,0:T(8,128)(2,1)S(1)}) custom-call(s32[1]{0:T(128)} %bitcast.15.plane_ref, bf16[256,1024]{1,0:T(8,128)(2,1)S(1)} %get-tuple-element.217.q_ref, bf16[256,1024]{1,0:T(8,128)(2,1)S(1)} %get-tuple-element.203.k_ref, bf16[432,1024]{1,0:T(8,128)(2,1)S(1)} %copy-done.18, ...), custom_call_target="tpu_custom_call" | custom-call | tf_op jit(solution)/shard_map/pallas_call | solution.py:351
  279.2 4.2 %collective-permute-start.38 = (bf16[2,864,128]{2,1,0:T(8,128)(2,1)S(1)}, bf16[2,864,128]{2,1,0:T(8,128)(2,1)S(1)}, u32[]{:S(2)}, u32[]{:S(2)}) collective-permute-start(bf16[2,864,128]{2,1,0:T(8,128)(2,1)S(1)} %get-tuple-element.216), channel_id=1, source_target_pairs={{0,96},{1,97},{2,98},{3,99},{4,100},{5,101},{6,102},{7,103},{8,104... | collective-permute-start | bytes 1327112 | tf_op jit(solution)/shard_map/ppermute | solution.py:55
  283.3 13.7 %shard_map.256 = (bf16[1024,2048]{1,0:T(8,128)(2,1)}, f32[1,2048]{1,0:T(1,128)S(1)}) custom-call(bf16[256,1024]{1,0:T(8,128)(2,1)S(1)} %get-tuple-element.217.q_ref, bf16[256,1024]{1,0:T(8,128)(2,1)S(1)} %get-tuple-element.203.k_ref, bf16[432,1024]{1,0:T(8,128)(2,1)S(1)} %get-tuple-element.205.v_ref, bf16[432,1024]{1,0:T(8,128)(2,1)S(1)} %get-tuple-element.206.s_ref, ...), custom_call_target="tpu_custom_call" | custom-call | tf_op jit(solution)/shard_map/pallas_call | solution.py:514
  311.0 3.7 collective-permute-start.42
  320.9 3.9 collective-permute-done.47
  326.6 3.5 collective-permute-done.46
  358.0 3.6 collective-permute-done.58
  361.6 4.7 %collective-permute-done.59.got_ref = bf16[64,2688]{1,0:T(8,128)(2,1)S(1)} collective-permute-done((bf16[64,2688]{1,0:T(8,128)(2,1)S(1)}, bf16[64,2688]{1,0:T(8,128)(2,1)S(1)}, u32[]{:S(2)}, u32[]{:S(2)}) %collective-permute-start.59) | collective-permute-done | bytes 344096 | tf_op jit(solution)/shard_map/ppermute | solution.py:55
  374.0 5.2 %collective-permute-done.61.got_ref = bf16[64,2048]{1,0:T(8,128)(2,1)S(1)} collective-permute-done((bf16[64,2048]{1,0:T(8,128)(2,1)S(1)}, bf16[64,2048]{1,0:T(8,128)(2,1)S(1)}, u32[]{:S(2)}, u32[]{:S(2)}) %collective-permute-start.61) | collective-permute-done | bytes 262176 | tf_op jit(solution)/shard_map/ppermute | solution.py:55
  (337 shorter events, 175.7 us)
Async XLA Ops:
  7.2 93.6 %all-gather.3.cloned.1.call-start = ((), (), s32[]{:S(2)}) async-start(), calls=%async_computation.2 | async-start | bytes 4718592 | tf_op jit(solution)/shard_map/all_gather | solution.py:462
  9.9 17.2 %collective-permute-start = (bf16[64,4736]{1,0:T(8,128)(2,1)}, bf16[64,4736]{1,0:T(8,128)(2,1)S(1)}, u32[]{:S(2)}, u32[]{:S(2)}) collective-permute-start(bf16[64,4736]{1,0:T(8,128)(2,1)} %get-tuple-element.143), channel_id=1, source_target_pairs={{0,4},{1,5},{2,6},{3,7},{4,0},{5,1},{6,2},{7,3},{8,12},{9,13},{10,... | collective-permute-start | bytes 1818632 | tf_op jit(solution)/shard_map/ppermute | solution.py:55
  27.1 146.5 %all-gather.5.cloned.1.call-start = ((), (), s32[]{:S(2)}) async-start(), calls=%async_computation.3 | async-start | bytes 11280384 | tf_op jit(solution)/shard_map/all_gather | solution.py:813
  28.4 308.4 %reduce-scatter.3.cloned.1.call-start = ((), (), s32[]{:S(2)}) async-start(), calls=%async_computation.4 | async-start | bytes 11280384 | tf_op jit(solution)/shard_map/reduce_scatter | solution.py:837
  46.0 24.4 %collective-permute-start.17 = (bf16[128,2048]{1,0:T(8,128)(2,1)S(1)}, bf16[128,2048]{1,0:T(8,128)(2,1)S(1)}, u32[]{:S(2)}, u32[]{:S(2)}) collective-permute-start(bf16[128,2048]{1,0:T(8,128)(2,1)S(1)} %fusion.4), channel_id=1, source_target_pairs={{0,2},{1,3},{2,0},{3,1},{4,6},{5,7},{6,4},{7,5},{8,10},{9,11},{10,... | collective-permute-start | bytes 1572872 | tf_op jit(solution)/shard_map/ppermute | solution.py:55
  51.4 24.2 %collective-permute-start.9 = (bf16[4,944,128]{2,1,0:T(8,128)(2,1)}, bf16[4,944,128]{2,1,0:T(8,128)(2,1)S(1)}, u32[]{:S(2)}, u32[]{:S(2)}) collective-permute-start(bf16[4,944,128]{2,1,0:T(8,128)(2,1)} %pad_maximum_fusion.4.refs_0_), channel_id=1, source_target_pairs={{0,8},{1,9},{2,10},{3,11},{4,12},{5,13},{6,14},{7,15},{8,0},{9,1},... | collective-permute-start | bytes 2899976 | tf_op jit(solution)/shard_map/ppermute | solution.py:55
  51.8 23.8 %collective-permute-start.10 = (bf16[4,944,128]{2,1,0:T(8,128)(2,1)}, bf16[4,944,128]{2,1,0:T(8,128)(2,1)S(1)}, u32[]{:S(2)}, u32[]{:S(2)}) collective-permute-start(bf16[4,944,128]{2,1,0:T(8,128)(2,1)} %pad_maximum_fusion.4.refs_0_), channel_id=1, source_target_pairs={{0,24},{1,25},{2,26},{3,27},{4,28},{5,29},{6,30},{7,31},{8,16},{9,... | collective-permute-start | bytes 2899976 | tf_op jit(solution)/shard_map/ppermute | solution.py:55
  54.4 21.2 %collective-permute-start.11 = (bf16[4,864,128]{2,1,0:T(8,128)(2,1)}, bf16[4,864,128]{2,1,0:T(8,128)(2,1)S(1)}, u32[]{:S(2)}, u32[]{:S(2)}) collective-permute-start(bf16[4,864,128]{2,1,0:T(8,128)(2,1)} %pad_maximum_fusion.7.refs_5_), channel_id=1, source_target_pairs={{0,32},{1,33},{2,34},{3,35},{4,36},{5,37},{6,38},{7,39},{8,40},{9,... | collective-permute-start | bytes 2654216 | tf_op jit(solution)/shard_map/ppermute | solution.py:55
  55.7 19.9 %collective-permute-start.12 = (bf16[4,864,128]{2,1,0:T(8,128)(2,1)}, bf16[4,864,128]{2,1,0:T(8,128)(2,1)}, u32[]{:S(2)}, u32[]{:S(2)}) collective-permute-start(bf16[4,864,128]{2,1,0:T(8,128)(2,1)} %pad_maximum_fusion.7.refs_5_), channel_id=1, source_target_pairs={{0,96},{1,97},{2,98},{3,99},{4,100},{5,101},{6,102},{7,103},{8,104... | collective-permute-start | bytes 2654216 | tf_op jit(solution)/shard_map/ppermute | solution.py:55
  77.6 21.6 %collective-permute-start.13 = (bf16[2,944,128]{2,1,0:T(8,128)(2,1)S(1)}, bf16[2,944,128]{2,1,0:T(8,128)(2,1)S(1)}, u32[]{:S(2)}, u32[]{:S(2)}) collective-permute-start(bf16[2,944,128]{2,1,0:T(8,128)(2,1)S(1)} %get-tuple-element.161), channel_id=1, source_target_pairs={{0,8},{1,9},{2,10},{3,11},{4,12},{5,13},{6,14},{7,15},{8,0},{9,1},... | collective-permute-start | bytes 1449992 | tf_op jit(solution)/shard_map/ppermute | solution.py:55
  78.9 21.9 %collective-permute-start.14 = (bf16[2,944,128]{2,1,0:T(8,128)(2,1)S(1)}, bf16[2,944,128]{2,1,0:T(8,128)(2,1)}, u32[]{:S(2)}, u32[]{:S(2)}) collective-permute-start(bf16[2,944,128]{2,1,0:T(8,128)(2,1)S(1)} %get-tuple-element.162), channel_id=1, source_target_pairs={{0,24},{1,25},{2,26},{3,27},{4,28},{5,29},{6,30},{7,31},{8,16},{9,... | collective-permute-start | bytes 1449992 | tf_op jit(solution)/shard_map/ppermute | solution.py:55
  79.5 15.0 %collective-permute-start.15 = (bf16[2,864,128]{2,1,0:T(8,128)(2,1)S(1)}, bf16[2,864,128]{2,1,0:T(8,128)(2,1)S(1)}, u32[]{:S(2)}, u32[]{:S(2)}) collective-permute-start(bf16[2,864,128]{2,1,0:T(8,128)(2,1)S(1)} %get-tuple-element.163), channel_id=1, source_target_pairs={{0,32},{1,33},{2,34},{3,35},{4,36},{5,37},{6,38},{7,39},{8,40},{9,... | collective-permute-start | bytes 1327112 | tf_op jit(solution)/shard_map/ppermute | solution.py:55
  80.8 18.4 %collective-permute-start.16 = (bf16[2,864,128]{2,1,0:T(8,128)(2,1)S(1)}, bf16[2,864,128]{2,1,0:T(8,128)(2,1)S(1)}, u32[]{:S(2)}, u32[]{:S(2)}) collective-permute-start(bf16[2,864,128]{2,1,0:T(8,128)(2,1)S(1)} %get-tuple-element.164), channel_id=1, source_target_pairs={{0,96},{1,97},{2,98},{3,99},{4,100},{5,101},{6,102},{7,103},{8,104... | collective-permute-start | bytes 1327112 | tf_op jit(solution)/shard_map/ppermute | solution.py:55
  209.8 173.1 %reduce-scatter.5.cloned.1.call-start = ((), (), s32[]{:S(2)}) async-start(), calls=%async_computation.5 | async-start | bytes 4718592 | tf_op jit(solution)/shard_map/reduce_scatter | solution.py:878
  242.8 29.4 %collective-permute-start.34 = (bf16[256,2048]{1,0:T(8,128)(2,1)}, bf16[256,2048]{1,0:T(8,128)(2,1)}, u32[]{:S(2)}, u32[]{:S(2)}) collective-permute-start(bf16[256,2048]{1,0:T(8,128)(2,1)} %get-tuple-element.209), channel_id=1, source_target_pairs={{0,1},{1,0},{2,3},{3,2},{4,5},{5,4},{6,7},{7,6},{8,9},{9,8},{10,11... | collective-permute-start | bytes 3145736 | tf_op jit(solution)/shard_map/ppermute | solution.py:55
  274.0 28.3 %collective-permute-start.39 = (bf16[128,2048]{1,0:T(8,128)(2,1)S(1)}, bf16[128,2048]{1,0:T(8,128)(2,1)S(1)}, u32[]{:S(2)}, u32[]{:S(2)}) collective-permute-start(bf16[128,2048]{1,0:T(8,128)(2,1)S(1)} %slice.277), channel_id=1, source_target_pairs={{0,2},{1,3},{2,0},{3,1},{4,6},{5,7},{6,4},{7,5},{8,10},{9,11},{10,... | collective-permute-start | bytes 1572872 | tf_op jit(solution)/shard_map/ppermute | solution.py:55
  276.5 25.9 %collective-permute-start.35 = (bf16[2,944,128]{2,1,0:T(8,128)(2,1)S(1)}, bf16[2,944,128]{2,1,0:T(8,128)(2,1)S(1)}, u32[]{:S(2)}, u32[]{:S(2)}) collective-permute-start(bf16[2,944,128]{2,1,0:T(8,128)(2,1)S(1)} %get-tuple-element.213), channel_id=1, source_target_pairs={{0,8},{1,9},{2,10},{3,11},{4,12},{5,13},{6,14},{7,15},{8,0},{9,1},... | collective-permute-start | bytes 1449992 | tf_op jit(solution)/shard_map/ppermute | solution.py:55
  276.6 25.8 %collective-permute-start.36 = (bf16[2,944,128]{2,1,0:T(8,128)(2,1)S(1)}, bf16[2,944,128]{2,1,0:T(8,128)(2,1)S(1)}, u32[]{:S(2)}, u32[]{:S(2)}) collective-permute-start(bf16[2,944,128]{2,1,0:T(8,128)(2,1)S(1)} %get-tuple-element.214), channel_id=1, source_target_pairs={{0,24},{1,25},{2,26},{3,27},{4,28},{5,29},{6,30},{7,31},{8,16},{9,... | collective-permute-start | bytes 1449992 | tf_op jit(solution)/shard_map/ppermute | solution.py:55
  279.2 19.9 %collective-permute-start.37 = (bf16[2,864,128]{2,1,0:T(8,128)(2,1)S(1)}, bf16[2,864,128]{2,1,0:T(8,128)(2,1)S(1)}, u32[]{:S(2)}, u32[]{:S(2)}) collective-permute-start(bf16[2,864,128]{2,1,0:T(8,128)(2,1)S(1)} %get-tuple-element.215), channel_id=1, source_target_pairs={{0,32},{1,33},{2,34},{3,35},{4,36},{5,37},{6,38},{7,39},{8,40},{9,... | collective-permute-start | bytes 1327112 | tf_op jit(solution)/shard_map/ppermute | solution.py:55
  279.2 23.2 %collective-permute-start.38 = (bf16[2,864,128]{2,1,0:T(8,128)(2,1)S(1)}, bf16[2,864,128]{2,1,0:T(8,128)(2,1)S(1)}, u32[]{:S(2)}, u32[]{:S(2)}) collective-permute-start(bf16[2,864,128]{2,1,0:T(8,128)(2,1)S(1)} %get-tuple-element.216), channel_id=1, source_target_pairs={{0,96},{1,97},{2,98},{3,99},{4,100},{5,101},{6,102},{7,103},{8,104... | collective-permute-start | bytes 1327112 | tf_op jit(solution)/shard_map/ppermute | solution.py:55
  310.3 26.5 %collective-permute-start.40 = (bf16[4,944,128]{2,1,0:T(8,128)(2,1)}, bf16[4,944,128]{2,1,0:T(8,128)(2,1)}, u32[]{:S(2)}, u32[]{:S(2)}) collective-permute-start(bf16[4,944,128]{2,1,0:T(8,128)(2,1)} %get-tuple-element.225), channel_id=1, source_target_pairs={{0,24},{1,25},{2,26},{3,27},{4,28},{5,29},{6,30},{7,31},{8,16},{9,... | collective-permute-start | bytes 2899976 | tf_op jit(solution)/shard_map/ppermute | solution.py:55
  310.3 26.5 %collective-permute-start.41 = (bf16[4,944,128]{2,1,0:T(8,128)(2,1)}, bf16[4,944,128]{2,1,0:T(8,128)(2,1)}, u32[]{:S(2)}, u32[]{:S(2)}) collective-permute-start(bf16[4,944,128]{2,1,0:T(8,128)(2,1)} %get-tuple-element.226), channel_id=1, source_target_pairs={{0,8},{1,9},{2,10},{3,11},{4,12},{5,13},{6,14},{7,15},{8,0},{9,1},... | collective-permute-start | bytes 2899976 | tf_op jit(solution)/shard_map/ppermute | solution.py:55
  311.0 25.8 %collective-permute-start.42 = (bf16[4,864,128]{2,1,0:T(8,128)(2,1)}, bf16[4,864,128]{2,1,0:T(8,128)(2,1)}, u32[]{:S(2)}, u32[]{:S(2)}) collective-permute-start(bf16[4,864,128]{2,1,0:T(8,128)(2,1)} %get-tuple-element.227), channel_id=1, source_target_pairs={{0,96},{1,97},{2,98},{3,99},{4,100},{5,101},{6,102},{7,103},{8,104... | collective-permute-start | bytes 2654216 | tf_op jit(solution)/shard_map/ppermute | solution.py:55
  314.7 22.1 %collective-permute-start.43 = (bf16[4,864,128]{2,1,0:T(8,128)(2,1)}, bf16[4,864,128]{2,1,0:T(8,128)(2,1)}, u32[]{:S(2)}, u32[]{:S(2)}) collective-permute-start(bf16[4,864,128]{2,1,0:T(8,128)(2,1)} %get-tuple-element.228), channel_id=1, source_target_pairs={{0,32},{1,33},{2,34},{3,35},{4,36},{5,37},{6,38},{7,39},{8,40},{9,... | collective-permute-start | bytes 2654216 | tf_op jit(solution)/shard_map/ppermute | solution.py:55
  (108 other events, 1063.1 us)
Sparse Core Ops, SparseCore 0:
  27.2 44.7 all-gather.2
  74.2 85.7 all-gather.4
  209.9 95.3 reduce-scatter.2
  337.0 45.9 reduce-scatter.4

commit v4 on v3

v4 whole, which is shorter than its diff:
```python
import functools

import jax
import jax.numpy as jnp
from jax import lax
from jax.experimental import pallas as pl
from jax.experimental.pallas import tpu as pltpu
from jax.sharding import PartitionSpec as P

norm_eps = 1e-05
group_eps = 1.0
AXES = ("dp", "tensor")
f32 = jnp.float32
bf16 = jnp.bfloat16
NN = (((1,), (0,)), ((), ()))
NT = (((1,), (1,)), ((), ()))
TN = (((0,), (0,)), ((), ()))
MB = 1 << 20
VMEM = pl.BlockSpec(memory_space=pltpu.VMEM)
ANY = pl.BlockSpec(memory_space=pl.ANY)


def device_index(x, z, y, c):
    return ((x * 4 + z) * 2 + y // 2) * 4 + (y % 2) * 2 + c


def xor_pairs(dx=0, dz=0, dy=0, dc=0):
    return [
        (device_index(x, z, y, c), device_index(x ^ dx, z ^ dz, y ^ dy, c ^ dc))
        for x in range(4)
        for z in range(4)
        for y in range(4)
        for c in range(2)
    ]


X1, X2, X3 = (xor_pairs(dx=d) for d in (1, 2, 3))
Z1, Z2, Z3 = (xor_pairs(dz=d) for d in (1, 2, 3))
Y1, Y2, Y3 = (xor_pairs(dy=d) for d in (1, 2, 3))
C1 = xor_pairs(dc=1)
LINES = [
    [device_index(x, z, y, c) for y in range(4) for c in range(2)]
    for x in range(4)
    for z in range(4)
]
LINE_ORDER = ((0, 0), (1, 0), (0, 1), (1, 1), (2, 0), (3, 0), (2, 1), (3, 1))
PLANES = [
    [device_index(x, z, y, c) for x in range(4) for z in range(4)]
    for y in range(4)
    for c in range(2)
]


def move(value, pairs):
    return lax.ppermute(value, AXES, pairs)


def tie(*values):
    return lax.optimization_barrier(values)


def dot(left, right, dims=NN):
    return lax.dot_general(left, right, dims, preferred_element_type=f32)


def params(mb):
    return pltpu.CompilerParams(vmem_limit_bytes=mb * MB)


def cost(flops, moved):
    return pl.CostEstimate(flops=flops, bytes_accessed=moved, transcendentals=0)


def up128(n):
    return n + (-n % 128)


def stacked(*parts):
    return jnp.concatenate(parts, axis=0)


def split_kernel(*refs):
    ins, (keep_ref, send_ref, pack_ref), held, sems = refs[:8], refs[8:11], refs[11:19], refs[19]
    copies = [pltpu.make_async_copy(i, h, sems.at[n]) for n, (i, h) in enumerate(zip(ins, held))]
    for copy in copies:
        copy.start()
    low = lax.axis_index("dp") % 2 == 0
    place = 0
    for n, ref in enumerate(held[:5]):
        copies[n].wait()
        half = ref.shape[1] // 2
        left, right = ref[:, :half], ref[:, half:]
        keep_ref[:, place : place + half] = jnp.where(low, left, right)
        send_ref[:, place : place + half] = jnp.where(low, right, left)
        place += up128(half)
    place = 0
    for n, ref in enumerate(held[5:]):
        copies[5 + n].wait()
        pack_ref[:, place : place + ref.shape[1]] = ref[...]
        place += up128(ref.shape[1])


def split_weights(mixer, feed):
    size = sum(up128(w.shape[1] // 2) for w in mixer)
    pack = sum(up128(w.shape[1]) for w in feed)
    return pl.pallas_call(
        split_kernel,
        out_shape=(
            jax.ShapeDtypeStruct((64, size), bf16),
            jax.ShapeDtypeStruct((64, size), bf16),
            jax.ShapeDtypeStruct((64, pack), bf16),
        ),
        in_specs=[ANY] * 8,
        scratch_shapes=[pltpu.VMEM(w.shape, bf16) for w in (*mixer, *feed)]
        + [pltpu.SemaphoreType.DMA((8,))],
        compiler_params=params(63),
    )(*mixer, *feed)


def join_kernel(groups, keep_ref, got_ref, *out_refs):
    low = lax.axis_index("dp") % 2 == 0
    place = 0
    for sizes, out_ref in zip(groups, out_refs):
        row = 0
        for size in sizes:
            wide = up128(size)
            keep, got = keep_ref[:, place : place + wide], got_ref[:, place : place + wide]
            both = stacked(jnp.where(low, keep, got), jnp.where(low, got, keep))
            out_ref[row : row + size, :] = both.T[:size]
            place += wide
            row += size


def join_weights(keep, got, *groups):
    out = pl.pallas_call(
        functools.partial(join_kernel, groups),
        out_shape=tuple(jax.ShapeDtypeStruct((sum(sizes), 128), bf16) for sizes in groups),
        compiler_params=params(16),
    )(keep, got)
    return out


def pick_kernel(starts, *refs):
    count = len(starts)
    ins, outs, sems = refs[:count], refs[count : 2 * count], refs[2 * count]
    copies = [
        pltpu.make_async_copy(i.at[pl.ds(start, o.shape[0])], o, sems.at[n])
        for n, (i, o, start) in enumerate(zip(ins, outs, starts))
    ]
    for copy in copies:
        copy.start()
    for copy in copies:
        copy.wait()


def pick(values, starts, sizes):
    return pl.pallas_call(
        functools.partial(pick_kernel, starts),
        out_shape=tuple(
            jax.ShapeDtypeStruct((n, *v.shape[1:]), v.dtype) for v, n in zip(values, sizes)
        ),
        in_specs=[ANY] * len(values),
        out_specs=(ANY,) * len(values),
        scratch_shapes=[pltpu.SemaphoreType.DMA((len(values),))],
        compiler_params=params(4),
    )(*values)


def gather_plane(a, b, pack, rows):
    a1, a3, b1, b3, a2, b2 = tie(
        move(a, X1), move(a, X3), move(b, Z1), move(b, Z3), move(a, X2), move(b, Z2)
    )
    sa, sb = tie(jnp.stack([a, a1, a2, a3]), jnp.stack([b, b1, b2, b3]))
    sa1, sa3, sb1, sb3, got = tie(
        move(sa, Z1), move(sa, Z3), move(sb, X1), move(sb, X3), move(pack, Y2)
    )
    ap, aq, bp, bq, rows, got = tie(*pick((sa3, sa1, sb3, sb1), (0, 2, 0, 2), (2,) * 4), rows, got)
    sa2p, sa2q, sb2p, sb2q, far = tie(
        move(ap, Z1), move(aq, Z3), move(bp, X1), move(bq, X3), move(rows, Y1)
    )
    return (sa, sa1, sa2p, sa2q, sa3, sb, sb1, sb2p, sb2q, sb3), got, stacked(rows, far)


def add_low(*terms):
    total = terms[0].astype(f32)
    for term in terms[1:]:
        total = total + term.astype(f32)
    return total.astype(bf16)


def fold_kernel(*refs):
    olds, more, outs = refs[:4], refs[4:8], refs[8:12]
    held, sems = refs[12:20], refs[20]
    loads, stores = [], []
    for n in range(4):
        start = 2 * (n % 2)
        loads.append(pltpu.make_async_copy(olds[n].at[pl.ds(start, 2)], held[n], sems.at[n, 0]))
        loads.append(pltpu.make_async_copy(more[n], held[4 + n], sems.at[n, 1]))
        stores.append(pltpu.make_async_copy(held[n], outs[n].at[pl.ds(start, 2)], sems.at[n, 2]))
    for copy in loads:
        copy.start()
    for n in range(4):
        loads[2 * n].wait()
        loads[2 * n + 1].wait()
        held[n][...] = (held[n][...].astype(f32) + held[4 + n][...].astype(f32)).astype(bf16)
        stores[n].start()
    for copy in stores:
        copy.wait()


def fold(a3, a1, b3, b1, ap, aq, bp, bq):
    values, more = (a3, a1, b3, b1), (ap, aq, bp, bq)
    return pl.pallas_call(
        fold_kernel,
        out_shape=tuple(jax.ShapeDtypeStruct(v.shape, v.dtype) for v in values),
        in_specs=[ANY] * 8,
        out_specs=(ANY,) * 4,
        scratch_shapes=[pltpu.VMEM(v.shape, bf16) for v in more * 2] + [pltpu.SemaphoreType.DMA((4, 3))],
        input_output_aliases={i: i for i in range(4)},
        compiler_params=params(63),
    )(*values, *more)


def add_kernel(*refs):
    ins, outs = refs[:6], refs[6:]
    for j in range(4):

        @pl.when(pl.program_id(0) == j)
        def _():
            for n in range(2):
                total = sum(ref[0].astype(f32) for ref in ins[3 * n : 3 * n + 3])
                outs[4 * n + j][...] = total.astype(bf16)


def add_blocks(a, b):
    blocks = [pl.BlockSpec((1, *v.shape[1:]), lambda i: (i, 0, 0)) for v in (*a, *b)]
    outs = [v.shape[1:] for v in (a[0],) * 4 + (b[0],) * 4]
    out = pl.pallas_call(
        add_kernel,
        grid=(4,),
        out_shape=tuple(jax.ShapeDtypeStruct(shape, bf16) for shape in outs),
        in_specs=blocks,
        out_specs=tuple(pl.BlockSpec(shape, lambda i: (0, 0)) for shape in outs),
        compiler_params=params(32),
    )(*a, *b)
    return out[:4], out[4:]


def feed_kernel(
    w_ref, x0_ref, x1_ref, g0_ref, g1_ref, hidden_ref, grads_ref, keep_ref, send_ref,
    held_ref, x_ref, grad_ref, sems,
):
    wide = hidden_ref.shape[0]
    half = x0_ref.shape[0]
    given = [
        pltpu.make_async_copy(x0_ref, x_ref.at[pl.ds(0, half), :], sems.at[48]),
        pltpu.make_async_copy(x1_ref, x_ref.at[pl.ds(half, half), :], sems.at[49]),
    ]
    weights = [
        [
            pltpu.make_async_copy(
                w_ref.at[pl.ds((3 * j + i) * wide, wide), :],
                held_ref.at[pl.ds(i * wide, wide), pl.ds(128 * j, 128)],
                sems.at[16 * i + j],
            )
            for j in range(16)
        ]
        for i in range(3)
    ]
    grads = [
        pltpu.make_async_copy(g0_ref, grad_ref.at[pl.ds(0, half), :], sems.at[50]),
        pltpu.make_async_copy(g1_ref, grad_ref.at[pl.ds(half, half), :], sems.at[51]),
    ]
    for copy in given + weights[0] + weights[1] + grads + weights[2]:
        copy.start()
    for copy in given + weights[0]:
        copy.wait()
    up, down, last = (slice(n * wide, (n + 1) * wide) for n in range(3))
    gelu_in = dot(held_ref[up, :], x_ref[...], NT)
    for copy in weights[1]:
        copy.wait()
    linear_in = dot(held_ref[down, :], x_ref[...], NT)
    for copy in grads + weights[2]:
        copy.wait()
    back = dot(held_ref[last, :], grad_ref[...], NT)
    cdf = 0.5 * (1.0 + lax.erf(gelu_in * (0.5**0.5)))
    gelu = gelu_in * cdf
    slope = cdf + gelu_in * jnp.exp(-0.5 * gelu_in * gelu_in) * 0.3989422804014327
    hidden_ref[...] = (gelu * linear_in).astype(bf16)
    grads_ref[up, :] = (back * linear_in * slope).astype(bf16)
    grads_ref[down, :] = (back * gelu).astype(bf16)
    for rows, out_ref in ((slice(half, 2 * half), send_ref), (slice(0, half), keep_ref)):
        out_ref[...] = dot(grads_ref[:, rows], held_ref[: 2 * wide, :], TN).astype(out_ref.dtype)


def feed_forward_back(w, x0, x1, g0, g1):
    half, width = x0.shape
    wide = w.shape[0] // 48
    return pl.pallas_call(
        feed_kernel,
        out_shape=(
            jax.ShapeDtypeStruct((wide, 2 * half), bf16),
            jax.ShapeDtypeStruct((2 * wide, 2 * half), bf16),
            jax.ShapeDtypeStruct((half, width), f32),
            jax.ShapeDtypeStruct((half, width), bf16),
        ),
        in_specs=[ANY] * 5,
        scratch_shapes=[
            pltpu.VMEM((3 * wide, width), bf16),
            pltpu.VMEM((2 * half, width), bf16),
            pltpu.VMEM((2 * half, width), bf16),
            pltpu.SemaphoreType.DMA((52,)),
        ],
        cost_estimate=cost(20 * half * wide * width, 10 * wide * width),
        compiler_params=params(63),
    )(w, x0, x1, g0, g1)


def early_kernel(
    hidden_ref, grads_ref, x0_ref, x1_ref, g0_ref, g1_ref, w_ref, out_ref, keep_ref, send_ref, turn_ref
):
    wide = hidden_ref.shape[0]
    half = x0_ref.shape[0]

    @pl.when(pl.program_id(0) == 0)
    def _():
        turn_ref[...] = hidden_ref[...].T

    up = dot(grads_ref[...], stacked(x0_ref[...], x1_ref[...])).astype(bf16)
    down = dot(hidden_ref[...], stacked(g0_ref[...], g1_ref[...])).astype(bf16)
    for i in range(4):
        lanes = slice(128 * i, 128 * i + 128)
        out_ref[i, : 2 * wide, :] = up[:, lanes]
        out_ref[i, 2 * wide :, :] = down[:, lanes]
    w = jnp.concatenate([w_ref[i] for i in range(4)], axis=1)
    keep_ref[...] = dot(turn_ref[:half, :], w).astype(bf16)
    send_ref[...] = dot(turn_ref[half:, :], w).astype(bf16)


def early_gradients(hidden, grads, x0, x1, g0, g1, w):
    wide, rows = hidden.shape
    half, width = x0.shape
    block = pl.BlockSpec((half, 512), lambda i: (0, i))
    return pl.pallas_call(
        early_kernel,
        grid=(4,),
        out_shape=(
            jax.ShapeDtypeStruct((16, 3 * wide, 128), bf16),
            jax.ShapeDtypeStruct((half, width), bf16),
            jax.ShapeDtypeStruct((half, width), bf16),
        ),
        in_specs=[
            pl.BlockSpec((wide, rows), lambda i: (0, 0)),
            pl.BlockSpec((2 * wide, rows), lambda i: (0, 0)),
            block,
            block,
            block,
            block,
            pl.BlockSpec((4, wide, 128), lambda i: (i, 2, 0)),
        ],
        out_specs=(pl.BlockSpec((4, 3 * wide, 128), lambda i: (i, 0, 0)), block, block),
        scratch_shapes=[pltpu.VMEM((rows, wide), bf16)],
        cost_estimate=cost(14 * half * wide * width, 10 * wide * width),
        compiler_params=params(63),
    )(hidden, grads, x0, x1, g0, g1, w.reshape(16, 3 * wide, 128))


def parts_kernel(steps, g_in, o_in, x_in, *refs):
    m_in, refs = refs[:4], refs[4:]
    outs, (g_ref, o_ref, x_ref, m_ref, sems) = refs[:-5], refs[-5:]
    plane = lax.axis_index("dp") // 2
    wide = o_ref.shape[0]
    keys = g_ref.shape[0] - 2 * wide
    size = m_in[0].shape[0]

    def lanes(dx, dz):
        return pl.ds(pl.multiple_of(jnp.bitwise_xor(4 * dx + dz, plane) * 128, 128), 128)

    fixed = [
        pltpu.make_async_copy(g_in.at[pl.ds(0, keys)], g_ref.at[pl.ds(0, keys)], sems.at[0]),
        pltpu.make_async_copy(g_in.at[pl.ds(keys, 2 * wide)], g_ref.at[pl.ds(keys, 2 * wide)], sems.at[1]),
        pltpu.make_async_copy(o_in, o_ref, sems.at[2]),
    ]
    waits = []
    for n, d in enumerate(steps):
        base = 3 + 24 * n
        copies = [[], [], []]
        for i in range(4):
            here = pl.ds(128 * i, 128)
            for k, at in enumerate((lanes(i, d), lanes(d, i))):
                copies[k].append(
                    pltpu.make_async_copy(
                        x_in.at[:, at], x_ref.at[2 * n + k, :, here], sems.at[base + 4 * k + i]
                    )
                )
            for k, m in enumerate(m_in):
                copies[2].append(
                    pltpu.make_async_copy(
                        m.at[:, lanes(i, d)],
                        m_ref.at[n, pl.ds(k * size, size), here],
                        sems.at[base + 8 + 4 * i + k],
                    )
                )
        if n == 0:
            for k in range(3):
                copies[k].append(fixed[k])
        waits.append(copies)
    for copies in waits:
        for part in copies:
            for copy in part:
                copy.start()

    per = len(outs) // len(steps) // 2

    def store(value, refs, rows):
        value = value.astype(bf16)
        for i in range(4):
            refs[i * per // 4][i % (4 // per), rows, :] = value[:, 128 * i : 128 * i + 128]

    for n in range(len(steps)):
        a_refs = outs[2 * per * n : 2 * per * n + per]
        b_refs = outs[2 * per * n + per : 2 * per * (n + 1)]
        for copy in waits[n][0]:
            copy.wait()
        store(dot(g_ref[:keys, :], x_ref[2 * n]), a_refs, slice(wide, wide + keys))
        for copy in waits[n][1]:
            copy.wait()
        store(dot(g_ref[keys:, :], x_ref[2 * n + 1]), b_refs, slice(0, 2 * wide))
        for copy in waits[n][2]:
            copy.wait()
        store(dot(o_ref[...], m_ref[n]), a_refs, slice(0, wide))


def gradient_parts(steps, per, g, o, x, m):
    wide, rows = o.shape
    rb = 2 * wide
    ra = g.shape[0] - rb + wide
    shapes = ([(4 // per, ra, 128)] * per + [(4 // per, rb, 128)] * per) * len(steps)
    return pl.pallas_call(
        functools.partial(parts_kernel, steps),
        grid=(1,),
        out_shape=tuple(jax.ShapeDtypeStruct(shape, bf16) for shape in shapes),
        in_specs=[ANY] * 7,
        out_specs=tuple(pl.BlockSpec(shape, lambda i: (0, 0, 0)) for shape in shapes),
        scratch_shapes=[
            pltpu.VMEM(g.shape, bf16),
            pltpu.VMEM(o.shape, bf16),
            pltpu.VMEM((2 * len(steps), rows, 512), bf16),
            pltpu.VMEM((len(steps), rows, 512), bf16),
            pltpu.SemaphoreType.DMA((3 + 24 * len(steps),)),
        ],
        cost_estimate=cost(rows * 512 * (ra + rb) * 2 * len(steps), 6 * rows * 2048),
        compiler_params=params(63),
    )(g, o, x, *m)


def early_out_kernel(sum_ref, keep_ref, send_ref):
    low = lax.axis_index("dp") % 2 == 0
    wide = sum_ref.shape[0] // 3
    for i in range(3):
        flat = sum_ref[i * wide : (i + 1) * wide, :].T
        place = slice(i * up128(wide), i * up128(wide) + wide)
        keep_ref[:, place] = jnp.where(low, flat[:64], flat[64:])
        send_ref[:, place] = jnp.where(low, flat[64:], flat[:64])


def early_end_kernel(keep_ref, got_ref, *out_refs):
    wide = out_refs[0].shape[1]
    for i, out_ref in enumerate(out_refs):
        place = slice(i * up128(wide), i * up128(wide) + wide)
        out_ref[...] = keep_ref[:, place].astype(f32) + got_ref[:, place].astype(f32)


def settle_early(summed):
    wide = summed.shape[0] // 3
    flat = jax.ShapeDtypeStruct((64, 3 * up128(wide)), bf16)
    keep, send = pl.pallas_call(
        early_out_kernel, out_shape=(flat, flat), compiler_params=params(16)
    )(summed)
    return pl.pallas_call(
        early_end_kernel,
        out_shape=(jax.ShapeDtypeStruct((64, wide), f32),) * 3,
        compiler_params=params(16),
    )(keep, move(send, Y2))


def late_out_kernel(sizes, *refs):
    a_refs, b_refs, (keep_ref, send_ref) = refs[:4], refs[4:8], refs[8:]
    low = lax.axis_index("dp") % 2 == 0
    place, row, parts = 0, 0, a_refs
    for size in sizes:
        if row == parts[0].shape[0]:
            row, parts = 0, b_refs
        total = sum(ref[row : row + size, :].astype(f32) for ref in parts)
        flat = total.astype(bf16).T
        keep_ref[:, place : place + size] = jnp.where(low, flat[:64], flat[64:])
        send_ref[:, place : place + size] = jnp.where(low, flat[64:], flat[:64])
        row += size
        place += up128(size)


def late_end_kernel(keep_ref, got_ref, *out_refs):
    low = lax.axis_index("dp") % 2 == 0
    place = 0
    for out_ref in out_refs:
        size = out_ref.shape[1] // 2
        keep = keep_ref[:, place : place + size].astype(f32)
        got = got_ref[:, place : place + size].astype(f32)
        out_ref[:, :size] = jnp.where(low, keep, got)
        out_ref[:, size:] = jnp.where(low, got, keep)
        place += up128(size)


def settle_late(a, b, sizes):
    flat = jax.ShapeDtypeStruct((64, sum(up128(n) for n in sizes)), bf16)
    keep, send = pl.pallas_call(
        functools.partial(late_out_kernel, sizes), out_shape=(flat, flat), compiler_params=params(16)
    )(*a, *b)
    return pl.pallas_call(
        late_end_kernel,
        out_shape=tuple(jax.ShapeDtypeStruct((64, 2 * n), f32) for n in sizes),
        compiler_params=params(16),
    )(keep, move(send, Y2))


def line_place(block):
    dp, tensor = lax.axis_index("dp"), lax.axis_index("tensor")
    y, c = dp % 2 * 2 + tensor // 2, tensor % 2
    dy, dc = LINE_ORDER[block]
    return jnp.bitwise_xor(y, dy) * 2 + jnp.bitwise_xor(c, dc)


def back_kernel(g_ref, w_ref, x_ref, out_ref, gain_ref, held_ref, sems):
    rows = g_ref.shape[1] // 4
    step = pl.program_id(0)
    total = dot(g_ref[...], w_ref[w_ref.shape[0] - g_ref.shape[0] :, :], TN)
    held_ref[...] = total.astype(bf16)
    copies = []
    for j in range(4):
        where = jnp.where(step == 0, line_place(j), line_place(j + 4))
        copies.append(
            pltpu.make_async_copy(
                held_ref.at[pl.ds(j * rows, rows), :],
                out_ref.at[pl.ds(pl.multiple_of(where * rows, rows), rows), :],
                sems.at[j],
            )
        )
    for copy in copies:
        copy.start()
    gain = jnp.sum(total * x_ref[...].astype(f32), axis=0, keepdims=True)

    @pl.when(step == 0)
    def _():
        gain_ref[...] = gain

    @pl.when(step > 0)
    def _():
        gain_ref[...] += gain

    for copy in copies:
        copy.wait()


def input_gradients(g, w, x):
    size, total = g.shape
    width = w.shape[1]
    half = total // 2
    return pl.pallas_call(
        back_kernel,
        grid=(2,),
        out_shape=(
            jax.ShapeDtypeStruct((total, width), bf16),
            jax.ShapeDtypeStruct((1, width), f32),
        ),
        in_specs=[
            pl.BlockSpec((size, half), lambda i: (0, i)),
            pl.BlockSpec(w.shape, lambda i: (0, 0)),
            pl.BlockSpec((half, width), lambda i: (i, 0)),
        ],
        out_specs=(ANY, pl.BlockSpec((1, width), lambda i: (0, 0))),
        scratch_shapes=[pltpu.VMEM((half, width), bf16), pltpu.SemaphoreType.DMA((4,))],
        cost_estimate=cost(2 * size * total * width, 10 * total * width),
        compiler_params=params(63),
    )(g, w, x)


def gather_line_first(own, *beside):
    r1, r3, *beside = tie(move(own, Y1), move(own, Y3), *beside)
    mine = stacked(own, r1)
    half = own.shape[0] // 2
    return (mine, move(mine, C1)), (move(r3[:half], Y1), move(r1[half:], Y3), r3), beside


def gather_line_last(r2p, r2q, r3):
    other = stacked(r2p, r2q, r3)
    return other, move(other, C1)


def scatter_line(keep_m, send_m, keep_o, send_o):
    rows = keep_m.shape[0] // 2
    half = rows // 2
    o = keep_o.astype(f32) + move(send_o, C1).astype(f32)
    s2 = o[:rows].astype(bf16)
    t3, t1 = tie(move(s2[:half], Y1), move(s2[half:], Y3))
    m = keep_m.astype(f32) + move(send_m, C1).astype(f32)
    s3 = stacked(o[rows : rows + half] + t3.astype(f32), o[rows + half :]).astype(bf16)
    s1 = stacked(m[rows : rows + half], m[rows + half :] + t1.astype(f32)).astype(bf16)
    u3, u1 = tie(move(s3, Y3), move(s1, Y1))
    return m[:rows] + u3.astype(f32) + u1.astype(f32)


def gather_pair(own):
    mine = stacked(own, move(own, Y1))
    return mine, move(mine, C1)


def scatter_pair(keep, send, *beside):
    rows = keep.shape[0] // 2
    m = keep + move(send, C1).astype(f32)
    u1, *beside = tie(move(m[rows:].astype(bf16), Y1), *beside)
    return (m[:rows] + u1.astype(f32), *beside)


def mixer_kernel(*refs):
    blocks, (line_ref, decay_ref, gain_ref) = refs[:10], refs[10:13]
    w_out, x_out, q_ref, k_ref, v_ref, gate_ref, retained_ref, mixed_ref = refs[13:21]
    parts, (w_ref, x_ref, sems) = refs[21:25], refs[25:]
    va, vb = blocks[:5], blocks[5:]
    kwide, wide = q_ref.shape[1], v_ref.shape[1]
    rows, half = q_ref.shape[0], parts[0].shape[0]
    plane = lax.axis_index("dp") // 2
    ra, rb = va[0].shape[1], vb[0].shape[1]
    keys = 2 * kwide
    step = pl.program_id(0)
    copies = []
    for dx in range(4):
        for dz in range(4):
            j = 4 * dx + dz
            lanes = pl.ds(pl.multiple_of(jnp.bitwise_xor(j, plane) * 128, 128), 128)
            for n, (part, first, then, row, size) in enumerate(((va, dz, dx, 0, ra), (vb, dx, dz, ra, rb))):
                if first == 2:
                    source = part[2 + then // 2].at[then % 2]
                else:
                    source = part[(0, 1, None, 4)[first]].at[then]
                copies.append(
                    pltpu.make_async_copy(
                        source, w_ref.at[pl.ds(row, size), lanes], sems.at[2 * j + n]
                    )
                )
    size = rows // 4
    given = [
        pltpu.make_async_copy(
            line_ref.at[pl.ds(pl.multiple_of(line_place(j) * size, size), size), :],
            x_ref.at[pl.ds(j * size, size), :],
            sems.at[32 + j],
        )
        for j in range(8)
    ]
    w_back = pltpu.make_async_copy(w_ref, w_out, sems.at[40])
    x_back = pltpu.make_async_copy(x_ref, x_out, sems.at[41])

    @pl.when(step == 0)
    def _():
        for copy in given[:4] + copies + given[4:]:
            copy.start()
        for copy in given[:4] + copies:
            copy.wait()
        w_back.start()

    @pl.when(step == 1)
    def _():
        for copy in given[4:]:
            copy.wait()
        x_back.start()

    x = x_ref[pl.ds(pl.multiple_of(step * rows, rows), rows), :]
    both = dot(x, w_ref[wide : keys + 2 * wide, :], NT).astype(bf16)
    q, k, v = both[:, :kwide], both[:, kwide:keys], both[:, keys:]
    gate = dot(x, w_ref[keys + 2 * wide :, :], NT)
    q_ref[...], k_ref[...], v_ref[...], gate_ref[...] = q, k, v, gate
    weights = (dot(q, k, NT) * decay_ref[...]).astype(bf16)
    retained = dot(weights, v)
    retained_ref[...] = retained
    center = retained - jnp.mean(retained, axis=-1, keepdims=True)
    spread = jnp.mean(center * center, axis=-1, keepdims=True)
    normed = center * lax.rsqrt(spread + group_eps)
    mixed = (gate * jax.nn.sigmoid(gate) * normed * gain_ref[...]).astype(bf16)
    mixed_ref[...] = mixed.T
    wo = w_ref[:wide, :]
    send, keep = dot(mixed[half:], wo).astype(bf16), dot(mixed[:half], wo).astype(bf16)

    @pl.when(step == 0)
    def _():
        parts[0][...], parts[1][...] = keep, send

    @pl.when(step == 1)
    def _():
        parts[2][...], parts[3][...] = keep, send
        w_back.wait()
        x_back.wait()


def mixer_forward(blocks, line, decay, gain, kwide):
    total, width = line.shape
    rows = decay.shape[0]
    wide = gain.shape[1]
    size = 2 * kwide + 3 * wide
    slim = pl.BlockSpec((rows, kwide), lambda i: (i, 0))
    whole = pl.BlockSpec((rows, wide), lambda i: (i, 0))
    part = pl.BlockSpec((rows // 2, width), lambda i: (0, 0))
    return pl.pallas_call(
        mixer_kernel,
        grid=(2,),
        out_shape=(
            jax.ShapeDtypeStruct((size, width), bf16),
            jax.ShapeDtypeStruct((total, width), bf16),
            jax.ShapeDtypeStruct((total, kwide), bf16),
            jax.ShapeDtypeStruct((total, kwide), bf16),
            jax.ShapeDtypeStruct((total, wide), bf16),
            jax.ShapeDtypeStruct((total, wide), f32),
            jax.ShapeDtypeStruct((total, wide), f32),
            jax.ShapeDtypeStruct((wide, total), bf16),
        )
        + (jax.ShapeDtypeStruct((rows // 2, width), bf16),) * 4,
        in_specs=[ANY] * 11
        + [
            pl.BlockSpec((rows, rows), lambda i: (0, 0)),
            pl.BlockSpec((1, wide), lambda i: (0, 0)),
        ],
        out_specs=(
            ANY,
            ANY,
            slim,
            slim,
            whole,
            whole,
            whole,
            pl.BlockSpec((wide, rows), lambda i: (0, i)),
            part,
            part,
            part,
            part,
        ),
        scratch_shapes=[
            pltpu.VMEM((size, width), bf16),
            pltpu.VMEM((total, width), bf16),
            pltpu.SemaphoreType.DMA((42,)),
        ],
        cost_estimate=cost(2 * size * total * width, 16 * total * width),
        compiler_params=params(63),
    )(*blocks, line, decay, gain)


def mixer_back_kernel(
    g0_ref, g1_ref, w_ref, q_ref, k_ref, v_ref, gate_ref, decay_ref, gain_ref, retained_ref, *refs
):
    out_ref, gain_out_ref, grad_ref, wo_ref, sems = refs[-5:]
    kwide, wide = q_ref.shape[1], v_ref.shape[1]
    keys = 2 * kwide
    half = g0_ref.shape[0]
    copies = [
        pltpu.make_async_copy(w_ref.at[pl.ds(0, wide), :], wo_ref, sems.at[2]),
        pltpu.make_async_copy(g0_ref, grad_ref.at[pl.ds(0, half), :], sems.at[0]),
        pltpu.make_async_copy(g1_ref, grad_ref.at[pl.ds(half, half), :], sems.at[1]),
    ]
    for copy in copies:
        copy.start()
    q, k, v, decay = q_ref[...], k_ref[...], v_ref[...], decay_ref[...]
    weights = (dot(q, k, NT) * decay).astype(bf16)
    gain = gain_ref[...]
    retained = retained_ref[...]
    center = retained - jnp.mean(retained, axis=-1, keepdims=True)
    rstd = lax.rsqrt(jnp.mean(center * center, axis=-1, keepdims=True) + group_eps)
    normed = center * rstd
    gate = gate_ref[...]
    sig = jax.nn.sigmoid(gate)
    silu = gate * sig
    for copy in copies:
        copy.wait()
    grad = dot(grad_ref[...], wo_ref[...], NT)
    grad_normed = grad * normed
    out_ref[keys + wide :, :] = (grad_normed * gain * (sig * (1.0 + gate * (1.0 - sig)))).astype(bf16).T
    gain_out_ref[...] = jnp.sum(grad_normed * silu, axis=0, keepdims=True)
    y = grad * silu * gain
    back = rstd * (
        y
        - jnp.mean(y, axis=-1, keepdims=True)
        - normed * jnp.mean(y * normed, axis=-1, keepdims=True)
    )
    back = back.astype(bf16)
    grad_scores = (dot(back, v, NT) * decay).astype(bf16)
    out_ref[keys : keys + wide, :] = dot(back, weights, TN).astype(bf16)
    out_ref[kwide:keys, :] = dot(q, grad_scores, TN).astype(bf16)
    out_ref[:kwide, :] = dot(grad_scores, k).astype(bf16).T


def mixer_backward(group, grads, w, q, k, v, gate, decay, gain, retained, before=None):
    kwide, wide = q.shape[1], v.shape[1]
    rows = decay.shape[0]
    slim = pl.BlockSpec((rows, kwide), lambda i: (group, 0))
    whole = pl.BlockSpec((rows, wide), lambda i: (group, 0))
    line = pl.BlockSpec((1, wide), lambda i: (0, 0))
    size = 2 * kwide + 2 * wide
    given = [] if before is None else [before]
    return pl.pallas_call(
        mixer_back_kernel,
        grid=(1,),
        out_shape=(
            jax.ShapeDtypeStruct((size, q.shape[0]), bf16),
            jax.ShapeDtypeStruct((1, wide), f32),
        ),
        in_specs=[ANY] * 3
        + [slim, slim, whole, whole, pl.BlockSpec((rows, rows), lambda i: (0, 0)), line, whole]
        + [ANY] * len(given),
        out_specs=(pl.BlockSpec((size, rows), lambda i: (0, group)), line),
        input_output_aliases={10: 0} if given else {},
        scratch_shapes=[
            pltpu.VMEM((rows, w.shape[1]), bf16),
            pltpu.VMEM((wide, w.shape[1]), bf16),
            pltpu.SemaphoreType.DMA((3,)),
        ],
        cost_estimate=cost(2 * rows * (size + wide) * 1024, 8 * rows * 2048),
        compiler_params=params(63),
    )(*grads, w, q, k, v, gate, decay, gain, retained, *given)


def shards(
    tokens,
    group_length,
    forget_rate,
    mixer_gain,
    feed_gain,
    group_gain,
    w_query,
    w_key,
    w_value,
    w_swish,
    w_output,
    w_gelu,
    w_linear,
    w_down,
    cotangent,
):
    rows, width = tokens.shape
    dp = lax.axis_index("dp")
    tensor = lax.axis_index("tensor")
    is_low = dp % 2 == 0
    feed_wide = w_gelu.shape[1]
    wide = w_value.shape[1] // 2
    kwide = w_query.shape[1] // 2
    group = 4 * rows
    score_scale = kwide ** (-0.5)
    log_keep = jnp.log1p(-jnp.where(is_low, forget_rate[0], forget_rate[1]))
    valid_rows = (tensor * rows + lax.broadcasted_iota(jnp.int32, (rows, 1), 0) < group_length[0]).astype(f32)

    keep, send, pack = split_weights(
        (w_output.T, w_query, w_key, w_value, w_swish), (w_gelu, w_linear, w_down.T)
    )

    token_float = tokens.astype(f32)
    grad_result = cotangent.astype(f32)
    group_own = jnp.where(is_low, group_gain[:wide], group_gain[wide:]).reshape(1, wide)

    r1 = lax.rsqrt(jnp.mean(token_float * token_float, axis=-1, keepdims=True) + norm_eps)
    normed_in = (token_float * r1 * mixer_gain).astype(bf16)
    place = lax.broadcasted_iota(jnp.int32, (group, 1), 0)
    block = place // rows
    order = jnp.where(block == 1, 2, jnp.where(block == 2, 1, block))
    position = jnp.bitwise_xor(tensor, order) * rows + place % rows
    offset = position - position.reshape(1, -1)
    decay = jnp.where(
        offset >= 0, jnp.exp(jnp.maximum(offset, 0).astype(f32) * log_keep) * score_scale, 0.0
    )

    got, normed_in, decay = tie(move(send, Y2), normed_in, decay)
    first_a, first_b = join_weights(keep, got, (wide, kwide, kwide), (wide, wide))
    normed_line = lax.all_gather(normed_in, AXES, axis_index_groups=LINES, axis=0, tiled=True)
    grad_feed_out = (valid_rows * grad_result).astype(bf16)
    first, got, grad_feed = gather_plane(first_a, first_b, pack, grad_feed_out)
    (second,) = join_weights(pack, got, (feed_wide,) * 3)
    second = lax.all_gather(second, AXES, axis_index_groups=PLANES, axis=0, tiled=True)

    w_mixer, normed_group, q, k, v, gate, retained, mixed, *parts = mixer_forward(
        first, normed_line, decay, group_own, kwide
    )
    *parts, grad_feed_other = tie(*parts, move(grad_feed, C1))
    grad_feed = grad_feed, grad_feed_other
    mixer_out = scatter_line(*parts)
    middle = token_float + valid_rows * mixer_out
    r2 = lax.rsqrt(jnp.mean(middle * middle, axis=-1, keepdims=True) + norm_eps)
    normed_mid = (middle * r2 * feed_gain).astype(bf16)
    mid = gather_pair(normed_mid)
    hidden, grads, keep, send = feed_forward_back(second, *mid, *grad_feed)
    early, feed_keep, feed_send = early_gradients(
        hidden, grads, *mid, *grad_feed, second
    )
    grad_normed_mid, early, feed_keep, feed_send = scatter_pair(keep, send, early, feed_keep, feed_send)
    early_sum = lax.psum_scatter(
        early.reshape(-1, 128), AXES, axis_index_groups=PLANES, scatter_dimension=0, tiled=True
    )

    part_feed_gain = jnp.sum(grad_normed_mid * middle * r2, axis=0)
    z2 = grad_normed_mid * feed_gain
    grad_middle = (
        grad_result + r2 * z2 - middle * (r2 * r2 * r2) * jnp.mean(z2 * middle, axis=-1, keepdims=True)
    )
    grad_mixer_out = (valid_rows * grad_middle).astype(bf16)
    grad_mixer_out, feed_send = tie(grad_mixer_out, feed_send)
    feed_got = move(feed_send, C1)
    grad_mixer_m, left, (feed_keep, feed_send) = gather_line_first(
        grad_mixer_out,
        feed_keep[:rows].astype(f32) + feed_got[:rows].astype(f32),
        add_low(feed_keep[rows:], feed_got[rows:]),
    )
    grads, gain_m = mixer_backward(
        0, grad_mixer_m, w_mixer, q, k, v, gate, decay, group_own, retained
    )
    left, grads, feed_send = tie(left, grads, feed_send)
    grad_mixer_o = gather_line_last(*left)
    grads, gain_o = mixer_backward(
        1, grad_mixer_o, w_mixer, q, k, v, gate, decay, group_own, retained, grads
    )
    part_group_gain = (gain_m + gain_o).reshape(-1)
    grad_mixer = *grad_mixer_m, *grad_mixer_o
    *sent, grads, feed_far, group_far = tie(
        *gradient_parts((2,), 2, grads, mixed, normed_group, grad_mixer),
        grads,
        move(feed_send, Y1),
        move(part_group_gain, Y2),
    )

    moved = [move(part, pairs) for part, pairs in zip(sent, (Z1, Z3, X1, X3))]
    back, part_mixer_gain = input_gradients(grads, w_mixer, normed_group)
    back, grads = tie(back, grads)
    gains = jnp.concatenate([part_mixer_gain.reshape(-1) / mixer_gain, part_feed_gain])
    *moved, (a1, b1, a3, b3), grads, gains = tie(
        *moved,
        gradient_parts((1, 3), 1, grads, mixed, normed_group, grad_mixer),
        grads,
        gains + move(gains, C1),
    )
    a3, a1, b3, b1, grads, gains = tie(
        *fold(a3, a1, b3, b1, *moved), grads, gains + move(gains, Y1)
    )
    moved = move(a3, Z3), move(a1, Z1), move(b3, X3), move(b1, X1)
    a0, b0 = gradient_parts((0,), 1, grads, mixed, normed_group, grad_mixer)
    result = (middle + valid_rows * (feed_keep + feed_far.astype(f32))).astype(bf16)
    gains = gains + move(gains, Y2)
    gains = jnp.concatenate(
        [
            gains,
            jnp.where(is_low, part_group_gain, group_far),
            jnp.where(is_low, group_far, part_group_gain),
        ]
    )
    back, early_sum, _ = tie(back, early_sum, a3)
    grad_normed_in = lax.psum_scatter(
        back, AXES, axis_index_groups=LINES, scatter_dimension=0, tiled=True
    ).astype(f32)
    gains, a0, b0, result = tie(gains, a0, b0, result)
    r3, r1_, s3, s1, gains = tie(*moved, gains + move(gains, X1))
    a, b = tie(*add_blocks((a0, r3, r1_), (b0, s3, s1)))
    z1 = grad_normed_in * mixer_gain
    grad_tokens = (
        grad_middle + r1 * z1 - token_float * (r1 * r1 * r1) * jnp.mean(z1 * token_float, axis=-1, keepdims=True)
    ).astype(bf16)
    *moved, gains, g_gelu, g_linear, g_down, grad_tokens = tie(
        *(move(a[i], (X1, X2, X3)[i - 1]) for i in (1, 2, 3)),
        *(move(b[i], (Z1, Z2, Z3)[i - 1]) for i in (1, 2, 3)),
        gains + move(gains, X2),
        *settle_early(early_sum),
        grad_tokens,
    )
    for pairs in (Z1, Z2):
        gains = gains + move(gains, pairs)
    sum_a, sum_b = (a[0], *moved[:3]), (b[0], *moved[3:])
    g_output, g_query, g_key, g_value, g_swish = settle_late(
        sum_a, sum_b, (wide, kwide, kwide, wide, wide)
    )

    return (
        result,
        grad_tokens,
        gains[:width],
        gains[width : 2 * width],
        gains[2 * width :],
        g_query,
        g_key,
        g_value,
        g_swish,
        g_output.T,
        g_gelu,
        g_linear,
        g_down.T,
    )


def solution(mesh):
    weight = P("dp", "tensor")
    turned = P("tensor", "dp")
    rows = P(("dp", "tensor"), None)
    return jax.shard_map(
        shards,
        mesh=mesh,
        in_specs=(
            rows,
            P("dp"),
            P("tensor"),
            P(),
            P(),
            P("tensor"),
            weight,
            weight,
            weight,
            weight,
            turned,
            weight,
            weight,
            turned,
            rows,
        ),
        out_specs=(
            rows,
            rows,
            P(),
            P(),
            P("tensor"),
            weight,
            weight,
            weight,
            weight,
            turned,
            weight,
            weight,
            turned,
        ),
        check_vma=False,
    )
```

time: 400 us -> 366 us (0.915)
  waiting for transfers between devices: 141 us -> 104 us
  Pallas kernels: 94.9 us -> 113 us
  other arithmetic: 41.5 us -> 27.9 us
    ppermute x62 -> x60, waiting for transfers between devices: 138 us -> 103 us  [move(): return lax.ppermute(value, AXES, pairs)]
    pallas_call x5 -> x9, Pallas kernels: 53 us -> 71.5 us  [the longest x3 20.1 us: gradient_parts(): pl.pallas_call(functools.partial(parts_kernel, steps), grid=(1,), out_sha...]
    concatenate x12 -> x3, other arithmetic: 7.06 us -> 0.18 us  [stacked(): return jnp.concatenate(parts, axis=0)]
    convert_element_type x9 -> x1, other arithmetic: 7.36 us -> 1.49 us  [add_low(): return total.astype(bf16)]
    ppermute x62 -> x60, starting transfers between devices: 75.8 us -> 71.6 us  [move(): return lax.ppermute(value, AXES, pairs)]
    unnamed x134 -> x104, local copies, waits for them, and re-layouts: 17.3 us -> 20.1 us
  transfers between devices with their start and end apart: 66 -> 64, of which waited for: 33 -> 26; matrix products, arithmetic and copies ran while one was open for 11% -> 10% of each run, Pallas kernels for 19% -> 26%
where the time goes in v4:
time: 366 us; the launch traced here: 360 us
  Pallas kernels  113 us (31%)
  waiting for transfers between devices  104 us (28%)
  starting transfers between devices  72 us (20%)
  other arithmetic  27.9 us (8%)
  local copies, waits for them, and re-layouts  25.4 us (7%)
  between operations  16.7 us (5%)
    ppermute x60, waiting for transfers between devices, move(): return lax.ppermute(value, AXES, pairs)  103 us
    ppermute x60, starting transfers between devices, move(): return lax.ppermute(value, AXES, pairs)  71.6 us
    unnamed x104, local copies, waits for them, and re-layouts  20.1 us
    pallas_call x3, Pallas kernels, gradient_parts(): pl.pallas_call(functools.partial(parts_kernel, steps), grid=(1,), out_sha...  20.1 us
    pallas_call x1, Pallas kernels, mixer_forward(): pl.pallas_call(mixer_kernel, grid=(2,), out_shape=(jax.ShapeDtypeStruct((...  19.7 us
    pallas_call x2, Pallas kernels, mixer_backward(): pl.pallas_call(mixer_back_kernel, grid=(1,), out_shape=(jax.ShapeDtypeStr...  16.7 us
    pallas_call x1, Pallas kernels, feed_forward_back(): pl.pallas_call(feed_kernel, out_shape=(jax.ShapeDtypeStruct((wide, 2 * ha...  15 us
    pallas_call x1, Pallas kernels, input_gradients(): pl.pallas_call(back_kernel, grid=(2,), out_shape=(jax.ShapeDtypeStruct((t...  14.5 us
  transfers between devices with their start and end apart: 64, of which 26 were waited for; matrix products, arithmetic and copies ran while one was open for 10% of the time, Pallas kernels for 26%

profile of v4, /device:TPU:0, one launch (start us, length us, event | category | flops | bytes accessed | tf_op | source)
XLA Modules:
  0.0 359.9 jit_solution(7096157934492423913)
XLA Ops:
  9.6 3.4 collective-permute-start
  32.0 7.4 %collective-permute-done.4 = bf16[864,128]{1,0:T(8,128)(2,1)S(1)} collective-permute-done((bf16[864,128]{1,0:T(8,128)(2,1)S(1)}, bf16[864,128]{1,0:T(8,128)(2,1)S(1)}, u32[]{:S(2)}, u32[]{:S(2)}) %collective-permute-start.4) | collective-permute-done | bytes 221216 | tf_op jit(solution)/shard_map/ppermute | solution.py:55
  51.6 8.6 %collective-permute-done.11.got_ref = bf16[64,2688]{1,0:T(8,128)(2,1)S(1)} collective-permute-done((bf16[64,2688]{1,0:T(8,128)(2,1)S(1)}, bf16[64,2688]{1,0:T(8,128)(2,1)S(1)}, u32[]{:S(2)}, u32[]{:S(2)}) %collective-permute-start.11) | collective-permute-done | bytes 344096 | tf_op jit(solution)/shard_map/ppermute | solution.py:55
  60.2 3.3 collective-permute-done.9.refs_3_.refs_6_
  77.1 8.4 %collective-permute-done.14.refs_7_ = bf16[2,864,128]{2,1,0:T(8,128)(2,1)S(1)} collective-permute-done((bf16[2,864,128]{2,1,0:T(8,128)(2,1)}, bf16[2,864,128]{2,1,0:T(8,128)(2,1)S(1)}, u32[]{:S(2)}, u32[]{:S(2)}) %collective-permute-start.14) | collective-permute-done | bytes 442400 | tf_op jit(solution)/shard_map/ppermute | solution.py:55
  89.9 19.7 %shard_map.249 = (bf16[1808,2048]{1,0:T(8,128)(2,1)}, bf16[1024,2048]{1,0:T(8,128)(2,1)}, bf16[1024,256]{1,0:T(8,128)(2,1)}, bf16[1024,256]{1,0:T(8,128)(2,1)}, ...) custom-call(bf16[4,944,128]{2,1,0:T(8,128)(2,1)} %pad_maximum_fusion, ...), custom_call_target="tpu_custom_call" | custom-call | flops 7583301632 | bytes 33554432 | tf_op jit(solution)/shard_map/pallas_call | solution.py:711
  117.5 5.6 %collective-permute-done.20 = bf16[64,2048]{1,0:T(8,128)(2,1)S(1)} collective-permute-done((bf16[64,2048]{1,0:T(8,128)(2,1)S(1)}, bf16[64,2048]{1,0:T(8,128)(2,1)S(1)}, u32[]{:S(2)}, u32[]{:S(2)}) %collective-permute-start.20) | collective-permute-done | bytes 262176 | tf_op jit(solution)/shard_map/ppermute | solution.py:55
  127.0 12.7 %collective-permute-done.22 = bf16[128,2048]{1,0:T(8,128)(2,1)S(1)} collective-permute-done((bf16[128,2048]{1,0:T(8,128)(2,1)S(1)}, bf16[128,2048]{1,0:T(8,128)(2,1)S(1)}, u32[]{:S(2)}, u32[]{:S(2)}) %collective-permute-start.22) | collective-permute-done | bytes 524320 | tf_op jit(solution)/shard_map/ppermute | solution.py:55
  141.8 11.9 %collective-permute-done.24 = bf16[128,2048]{1,0:T(8,128)(2,1)S(1)} collective-permute-done((bf16[128,2048]{1,0:T(8,128)(2,1)S(1)}, bf16[128,2048]{1,0:T(8,128)(2,1)S(1)}, u32[]{:S(2)}, u32[]{:S(2)}) %collective-permute-start.24) | collective-permute-done | bytes 524320 | tf_op jit(solution)/shard_map/ppermute | solution.py:55
  157.7 15.0 %shard_map.251 = (bf16[864,512]{1,0:T(8,128)(2,1)}, bf16[1728,512]{1,0:T(8,128)(2,1)}, f32[256,2048]{1,0:T(8,128)}, bf16[256,2048]{1,0:T(8,128)(2,1)}) custom-call(bf16[41472,128]{1,0:T(8,128)(2,1)} %all-gather.5.cloned.1.call-done.w_ref, bf16[256,2048]{1,0:T(8,128)(2,1)} %copy-done.28, bf16[256,2048]{1,0:T(8,128)(2,1)} %collective-permute-done.25.x1_ref, ...), custom_call_target="tpu_custom_call" | custom-call | flops 9059696640 | bytes 17694720 | tf_op jit(solution)/shard_map/pallas_call | solution.py:299
  180.2 12.8 %shard_map.252 = (bf16[16,2592,128]{2,1,0:T(8,128)(2,1)}, bf16[256,2048]{1,0:T(8,128)(2,1)}, bf16[256,2048]{1,0:T(8,128)(2,1)}) custom-call(bf16[864,512]{1,0:T(8,128)(2,1)} %get-tuple-element.230.hidden_ref, bf16[1728,512]{1,0:T(8,128)(2,1)} %get-tuple-element.231.grads_ref, bf16[256,2048]{1,0:T(8,128)(2,1)} %copy-done.28, ...), custom_call_target="tpu_custom_call" | custom-call | flops 6341787648 | bytes 17694720 | tf_op jit(solution)/shard_map/pallas_call | solution.py:344
  203.8 10.2 %collective-permute-done.28 = bf16[128,2048]{1,0:T(8,128)(2,1)S(1)} collective-permute-done((bf16[128,2048]{1,0:T(8,128)(2,1)S(1)}, bf16[128,2048]{1,0:T(8,128)(2,1)S(1)}, u32[]{:S(2)}, u32[]{:S(2)}) %collective-permute-start.28) | collective-permute-done | bytes 524320 | tf_op jit(solution)/shard_map/ppermute | solution.py:55
  220.2 8.4 %shard_map.253 = (bf16[1376,1024]{1,0:T(8,128)(2,1)}, f32[1,432]{1,0:T(1,128)}) custom-call(bf16[256,2048]{1,0:T(8,128)(2,1)} %copy-done.18, bf16[256,2048]{1,0:T(8,128)(2,1)} %copy-done.22, bf16[1808,2048]{1,0:T(8,128)(2,1)} %get-tuple-element.242.w_ref, bf16[1024,256]{1,0:T(8,128)(2,1)} %get-tuple-element.243.q_ref, ...), custom_call_target="tpu_custom_call" | custom-call | flops 1895825408 | bytes 8388608 | tf_op jit(solution)/shard_map/pallas_call | solution.py:805
  234.4 8.3 %shard_map.254 = (bf16[1376,1024]{1,0:T(8,128)(2,1)}, f32[1,432]{1,0:T(1,128)}) custom-call(bf16[256,2048]{1,0:T(8,128)(2,1)} %copy-done.19, bf16[256,2048]{1,0:T(8,128)(2,1)} %collective-permute-done.34.g1_ref.refs_3_, bf16[1808,2048]{1,0:T(8,128)(2,1)} %get-tuple-element.242.w_ref, ...), custom_call_target="tpu_custom_call", output_to_operand_aliasing={{0}: (10, {})} | custom-call | flops 1895825408 | bytes 8388608 | tf_op jit(solution)/shard_map/pallas_call | solution.py:805
  245.6 5.8 %shard_map.255 = (bf16[2,944,128]{2,1,0:T(8,128)(2,1)}, bf16[2,944,128]{2,1,0:T(8,128)(2,1)}, bf16[2,864,128]{2,1,0:T(8,128)(2,1)}, bf16[2,864,128]{2,1,0:T(8,128)(2,1)}) custom-call(bf16[1376,1024]{1,0:T(8,128)(2,1)} %get-tuple-element.292.g_in.g_ref, bf16[432,1024]{1,0:T(8,128)(2,1)} %get-tuple-element.255.o_in, ...), custom_call_target="tpu_custom_call" | custom-call | flops 1895825408 | bytes 12582912 | tf_op jit(solution)/shard_map/pallas_call | solution.py:439
  256.2 14.5 %shard_map.256 = (bf16[1024,2048]{1,0:T(8,128)(2,1)}, f32[1,2048]{1,0:T(1,128)}) custom-call(bf16[1376,1024]{1,0:T(8,128)(2,1)} %get-tuple-element.292.g_in.g_ref, bf16[1808,2048]{1,0:T(8,128)(2,1)} %get-tuple-element.242.w_ref, bf16[1024,2048]{1,0:T(8,128)(2,1)} %get-tuple-element.256.x_in.x_ref), custom_call_target="tpu_custom_call" | custom-call | flops 5771362304 | bytes 20971520 | tf_op jit(solution)/shard_map/pallas_call | solution.py:568
  271.4 8.4 %shard_map.257 = (bf16[4,944,128]{2,1,0:T(8,128)(2,1)}, bf16[4,864,128]{2,1,0:T(8,128)(2,1)}, bf16[4,944,128]{2,1,0:T(8,128)(2,1)}, bf16[4,864,128]{2,1,0:T(8,128)(2,1)}) custom-call(bf16[1376,1024]{1,0:T(8,128)(2,1)} %get-tuple-element.292.g_in.g_ref, bf16[432,1024]{1,0:T(8,128)(2,1)} %get-tuple-element.255.o_in, ...), custom_call_target="tpu_custom_call" | custom-call | flops 3791650816 | bytes 12582912 | tf_op jit(solution)/shard_map/pallas_call | solution.py:439
  280.7 3.0 shard_map.258
  291.4 3.1 collective-permute-start.43
  294.5 5.8 %shard_map.259 = (bf16[4,944,128]{2,1,0:T(8,128)(2,1)}, bf16[4,864,128]{2,1,0:T(8,128)(2,1)}) custom-call(bf16[1376,1024]{1,0:T(8,128)(2,1)} %get-tuple-element.292.g_in.g_ref, bf16[432,1024]{1,0:T(8,128)(2,1)} %get-tuple-element.255.o_in, bf16[1024,2048]{1,0:T(8,128)(2,1)} %get-tuple-element.256.x_in.x_ref, bf16[256,2048]{1,0:T(8,128)(2,1)} %copy-done.18, ...), custom_call_target="tpu_custom_call" | custom-call | flops 1895825408 | bytes 12582912 | tf_op jit(solution)/shard_map/pallas_call | solution.py:439
  304.3 6.7 %collective-permute-done.48 = f32[4960]{0:T(1024)S(1)} collective-permute-done((f32[4960]{0:T(1024)S(1)}, f32[4960]{0:T(1024)S(1)}, u32[]{:S(2)}, u32[]{:S(2)}) %collective-permute-start.48) | collective-permute-done | bytes 19872 | tf_op jit(solution)/shard_map/ppermute | solution.py:55
  317.9 3.9 %shard_map.260 = (bf16[944,128]{1,0:T(8,128)(2,1)S(1)}, bf16[944,128]{1,0:T(8,128)(2,1)S(1)}, bf16[944,128]{1,0:T(8,128)(2,1)}, bf16[944,128]{1,0:T(8,128)(2,1)}...) custom-call(bf16[4,944,128]{2,1,0:T(8,128)(2,1)S(1)} %copy-done.2, ...), custom_call_target="tpu_custom_call" | custom-call | tf_op jit(solution)/shard_map/pallas_call | solution.py:238
  338.2 3.6 %collective-permute-done.54.refs_7_ = bf16[864,128]{1,0:T(8,128)(2,1)S(1)} collective-permute-done((bf16[864,128]{1,0:T(8,128)(2,1)}, bf16[864,128]{1,0:T(8,128)(2,1)S(1)}, u32[]{:S(2)}, u32[]{:S(2)}) %collective-permute-start.54) | collective-permute-done | bytes 221216 | tf_op jit(solution)/shard_map/ppermute | solution.py:55
  347.6 3.3 collective-permute-done.58
  (283 shorter events, 149.5 us)
Async XLA Ops:
  7.2 82.7 %all-gather.3.cloned.1.call-start = ((), (), s32[]{:S(2)}) async-start(), calls=%async_computation.2 | async-start | bytes 4718592 | tf_op jit(solution)/shard_map/all_gather | solution.py:877
  20.9 136.8 %all-gather.5.cloned.1.call-start = ((), (), s32[]{:S(2)}) async-start(), calls=%async_computation.3 | async-start | bytes 11280384 | tf_op jit(solution)/shard_map/all_gather | solution.py:881
  23.2 16.2 %collective-permute-start.1 = (bf16[944,128]{1,0:T(8,128)(2,1)S(1)}, bf16[944,128]{1,0:T(8,128)(2,1)S(1)}, u32[]{:S(2)}, u32[]{:S(2)}) collective-permute-start(bf16[944,128]{1,0:T(8,128)(2,1)S(1)} %get-tuple-element.182), channel_id=1, source_target_pairs={{0,32},{1,33},{2,34},{3,35},{4,36},{5,37},{6,38},{7,39},{8,40},{9,... | collective-permute-start | bytes 725000 | tf_op jit(solution)/shard_map/ppermute | solution.py:55
  41.6 23.2 %collective-permute-start.7 = (bf16[4,944,128]{2,1,0:T(8,128)(2,1)}, bf16[4,944,128]{2,1,0:T(8,128)(2,1)S(1)}, u32[]{:S(2)}, u32[]{:S(2)}) collective-permute-start(bf16[4,944,128]{2,1,0:T(8,128)(2,1)} %pad_maximum_fusion.1.refs_0_), channel_id=1, source_target_pairs={{0,8},{1,9},{2,10},{3,11},{4,12},{5,13},{6,14},{7,15},{8,0},{9,1},... | collective-permute-start | bytes 2899976 | tf_op jit(solution)/shard_map/ppermute | solution.py:55
  42.2 22.7 %collective-permute-start.8 = (bf16[4,944,128]{2,1,0:T(8,128)(2,1)}, bf16[4,944,128]{2,1,0:T(8,128)(2,1)S(1)}, u32[]{:S(2)}, u32[]{:S(2)}) collective-permute-start(bf16[4,944,128]{2,1,0:T(8,128)(2,1)} %pad_maximum_fusion.1.refs_0_), channel_id=1, source_target_pairs={{0,24},{1,25},{2,26},{3,27},{4,28},{5,29},{6,30},{7,31},{8,16},{9,... | collective-permute-start | bytes 2899976 | tf_op jit(solution)/shard_map/ppermute | solution.py:55
  44.5 19.0 %collective-permute-start.9 = (bf16[4,864,128]{2,1,0:T(8,128)(2,1)}, bf16[4,864,128]{2,1,0:T(8,128)(2,1)S(1)}, u32[]{:S(2)}, u32[]{:S(2)}) collective-permute-start(bf16[4,864,128]{2,1,0:T(8,128)(2,1)} %pad_maximum_fusion.2.refs_5_), channel_id=1, source_target_pairs={{0,32},{1,33},{2,34},{3,35},{4,36},{5,37},{6,38},{7,39},{8,40},{9,... | collective-permute-start | bytes 2654216 | tf_op jit(solution)/shard_map/ppermute | solution.py:55
  45.8 19.1 %collective-permute-start.10 = (bf16[4,864,128]{2,1,0:T(8,128)(2,1)}, bf16[4,864,128]{2,1,0:T(8,128)(2,1)}, u32[]{:S(2)}, u32[]{:S(2)}) collective-permute-start(bf16[4,864,128]{2,1,0:T(8,128)(2,1)} %pad_maximum_fusion.2.refs_5_), channel_id=1, source_target_pairs={{0,96},{1,97},{2,98},{3,99},{4,100},{5,101},{6,102},{7,103},{8,104... | collective-permute-start | bytes 2654216 | tf_op jit(solution)/shard_map/ppermute | solution.py:55
  70.8 214.5 %reduce-scatter.3.cloned.1.call-start = ((), (), s32[]{:S(2)}) async-start(), calls=%async_computation.4 | async-start | bytes 11280384 | tf_op jit(solution)/shard_map/reduce_scatter | solution.py:898
  70.8 16.8 %collective-permute-start.16 = (bf16[128,2048]{1,0:T(8,128)(2,1)}, bf16[128,2048]{1,0:T(8,128)(2,1)S(1)}, u32[]{:S(2)}, u32[]{:S(2)}) collective-permute-start(bf16[128,2048]{1,0:T(8,128)(2,1)} %fusion), channel_id=1, source_target_pairs={{0,2},{1,3},{2,0},{3,1},{4,6},{5,7},{6,4},{7,5},{8,10},{9,11},{10,... | collective-permute-start | bytes 1572872 | tf_op jit(solution)/shard_map/ppermute | solution.py:55
  88.7 20.9 %collective-permute-start.17 = (bf16[256,2048]{1,0:T(8,128)(2,1)}, bf16[256,2048]{1,0:T(8,128)(2,1)}, u32[]{:S(2)}, u32[]{:S(2)}) collective-permute-start(bf16[256,2048]{1,0:T(8,128)(2,1)} %constant_dynamic-update-slice_fusion.g0_ref), channel_id=1, source_target_pairs={{0,1},{1,0},{2,3},{3,2},{4,5},{5,4},{6,7},{7,6},{8,9},{9,8},{10,11... | collective-permute-start | bytes 3145736 | tf_op jit(solution)/shard_map/ppermute | solution.py:55
  194.7 136.0 %reduce-scatter.5.cloned.1.call-start = ((), (), s32[]{:S(2)}) async-start(), calls=%async_computation.5 | async-start | bytes 4718592 | tf_op jit(solution)/shard_map/reduce_scatter | solution.py:957
  231.8 19.7 %collective-permute-start.35 = (bf16[128,2048]{1,0:T(8,128)(2,1)}, bf16[128,2048]{1,0:T(8,128)(2,1)S(1)}, u32[]{:S(2)}, u32[]{:S(2)}) collective-permute-start(bf16[128,2048]{1,0:T(8,128)(2,1)} %get-tuple-element.261), channel_id=1, source_target_pairs={{0,2},{1,3},{2,0},{3,1},{4,6},{5,7},{6,4},{7,5},{8,10},{9,11},{10,... | collective-permute-start | bytes 1572872 | tf_op jit(solution)/shard_map/ppermute | solution.py:55
  251.5 28.4 %collective-permute-start.37 = (bf16[2,944,128]{2,1,0:T(8,128)(2,1)}, bf16[2,944,128]{2,1,0:T(8,128)(2,1)}, u32[]{:S(2)}, u32[]{:S(2)}) collective-permute-start(bf16[2,944,128]{2,1,0:T(8,128)(2,1)} %get-tuple-element.264), channel_id=1, source_target_pairs={{0,8},{1,9},{2,10},{3,11},{4,12},{5,13},{6,14},{7,15},{8,0},{9,1},... | collective-permute-start | bytes 1449992 | tf_op jit(solution)/shard_map/ppermute | solution.py:55
  252.6 27.3 %collective-permute-start.38 = (bf16[2,944,128]{2,1,0:T(8,128)(2,1)}, bf16[2,944,128]{2,1,0:T(8,128)(2,1)}, u32[]{:S(2)}, u32[]{:S(2)}) collective-permute-start(bf16[2,944,128]{2,1,0:T(8,128)(2,1)} %get-tuple-element.265), channel_id=1, source_target_pairs={{0,24},{1,25},{2,26},{3,27},{4,28},{5,29},{6,30},{7,31},{8,16},{9,... | collective-permute-start | bytes 1449992 | tf_op jit(solution)/shard_map/ppermute | solution.py:55
  253.8 26.1 %collective-permute-start.39 = (bf16[2,864,128]{2,1,0:T(8,128)(2,1)}, bf16[2,864,128]{2,1,0:T(8,128)(2,1)S(1)}, u32[]{:S(2)}, u32[]{:S(2)}) collective-permute-start(bf16[2,864,128]{2,1,0:T(8,128)(2,1)} %get-tuple-element.266), channel_id=1, source_target_pairs={{0,32},{1,33},{2,34},{3,35},{4,36},{5,37},{6,38},{7,39},{8,40},{9,... | collective-permute-start | bytes 1327112 | tf_op jit(solution)/shard_map/ppermute | solution.py:55
  254.2 25.7 %collective-permute-start.40 = (bf16[2,864,128]{2,1,0:T(8,128)(2,1)}, bf16[2,864,128]{2,1,0:T(8,128)(2,1)}, u32[]{:S(2)}, u32[]{:S(2)}) collective-permute-start(bf16[2,864,128]{2,1,0:T(8,128)(2,1)} %get-tuple-element.267), channel_id=1, source_target_pairs={{0,96},{1,97},{2,98},{3,99},{4,100},{5,101},{6,102},{7,103},{8,104... | collective-permute-start | bytes 1327112 | tf_op jit(solution)/shard_map/ppermute | solution.py:55
  285.4 28.2 %collective-permute-start.44 = (bf16[4,944,128]{2,1,0:T(8,128)(2,1)}, bf16[4,944,128]{2,1,0:T(8,128)(2,1)S(1)}, u32[]{:S(2)}, u32[]{:S(2)}) collective-permute-start(bf16[4,944,128]{2,1,0:T(8,128)(2,1)} %get-tuple-element.299), channel_id=1, source_target_pairs={{0,24},{1,25},{2,26},{3,27},{4,28},{5,29},{6,30},{7,31},{8,16},{9,... | collective-permute-start | bytes 2899976 | tf_op jit(solution)/shard_map/ppermute | solution.py:55
  287.8 25.7 %collective-permute-start.45 = (bf16[4,944,128]{2,1,0:T(8,128)(2,1)}, bf16[4,944,128]{2,1,0:T(8,128)(2,1)}, u32[]{:S(2)}, u32[]{:S(2)}) collective-permute-start(bf16[4,944,128]{2,1,0:T(8,128)(2,1)} %get-tuple-element.300), channel_id=1, source_target_pairs={{0,8},{1,9},{2,10},{3,11},{4,12},{5,13},{6,14},{7,15},{8,0},{9,1},... | collective-permute-start | bytes 2899976 | tf_op jit(solution)/shard_map/ppermute | solution.py:55
  287.8 25.7 %collective-permute-start.46 = (bf16[4,864,128]{2,1,0:T(8,128)(2,1)}, bf16[4,864,128]{2,1,0:T(8,128)(2,1)}, u32[]{:S(2)}, u32[]{:S(2)}) collective-permute-start(bf16[4,864,128]{2,1,0:T(8,128)(2,1)} %get-tuple-element.301), channel_id=1, source_target_pairs={{0,96},{1,97},{2,98},{3,99},{4,100},{5,101},{6,102},{7,103},{8,104... | collective-permute-start | bytes 2654216 | tf_op jit(solution)/shard_map/ppermute | solution.py:55
  289.2 24.3 %collective-permute-start.47 = (bf16[4,864,128]{2,1,0:T(8,128)(2,1)}, bf16[4,864,128]{2,1,0:T(8,128)(2,1)}, u32[]{:S(2)}, u32[]{:S(2)}) collective-permute-start(bf16[4,864,128]{2,1,0:T(8,128)(2,1)} %get-tuple-element.302), channel_id=1, source_target_pairs={{0,32},{1,33},{2,34},{3,35},{4,36},{5,37},{6,38},{7,39},{8,40},{9,... | collective-permute-start | bytes 2654216 | tf_op jit(solution)/shard_map/ppermute | solution.py:55
  311.0 18.1 %collective-permute-start.56 = (bf16[64,2688]{1,0:T(8,128)(2,1)S(1)}, bf16[64,2688]{1,0:T(8,128)(2,1)S(1)}, u32[]{:S(2)}, u32[]{:S(2)}) collective-permute-start(bf16[64,2688]{1,0:T(8,128)(2,1)S(1)} %get-tuple-element.320), channel_id=1, source_target_pairs={{0,4},{1,5},{2,6},{3,7},{4,0},{5,1},{6,2},{7,3},{8,12},{9,13},{10,... | collective-permute-start | bytes 1032200 | tf_op jit(solution)/shard_map/ppermute | solution.py:55
  322.4 19.4 %collective-permute-start.49 = (bf16[944,128]{1,0:T(8,128)(2,1)S(1)}, bf16[944,128]{1,0:T(8,128)(2,1)S(1)}, u32[]{:S(2)}, u32[]{:S(2)}) collective-permute-start(bf16[944,128]{1,0:T(8,128)(2,1)S(1)} %get-tuple-element.309), channel_id=1, source_target_pairs={{0,32},{1,33},{2,34},{3,35},{4,36},{5,37},{6,38},{7,39},{8,40},{9,... | collective-permute-start | bytes 725000 | tf_op jit(solution)/shard_map/ppermute | solution.py:55
  323.0 18.8 %collective-permute-start.50 = (bf16[944,128]{1,0:T(8,128)(2,1)}, bf16[944,128]{1,0:T(8,128)(2,1)S(1)}, u32[]{:S(2)}, u32[]{:S(2)}) collective-permute-start(bf16[944,128]{1,0:T(8,128)(2,1)} %get-tuple-element.310), channel_id=1, source_target_pairs={{0,64},{1,65},{2,66},{3,67},{4,68},{5,69},{6,70},{7,71},{8,72},{9,... | collective-permute-start | bytes 725000 | tf_op jit(solution)/shard_map/ppermute | solution.py:55
  325.1 16.7 %collective-permute-start.51 = (bf16[944,128]{1,0:T(8,128)(2,1)}, bf16[944,128]{1,0:T(8,128)(2,1)S(1)}, u32[]{:S(2)}, u32[]{:S(2)}) collective-permute-start(bf16[944,128]{1,0:T(8,128)(2,1)} %get-tuple-element.311), channel_id=1, source_target_pairs={{0,96},{1,97},{2,98},{3,99},{4,100},{5,101},{6,102},{7,103},{8,104... | collective-permute-start | bytes 725000 | tf_op jit(solution)/shard_map/ppermute | solution.py:55
  (90 other events, 820.8 us)
Sparse Core Ops, SparseCore 0:
  21.0 37.1 all-gather.2
  70.9 77.7 all-gather.4
  194.9 90.3 reduce-scatter.2
  287.7 42.9 reduce-scatter.4

commit v5 on v4

--- a/solution.py
+++ b/solution.py
@@ -113,7 +113,7 @@
         in_specs=[ANY] * 8,
         scratch_shapes=[pltpu.VMEM(w.shape, bf16) for w in (*mixer, *feed)]
         + [pltpu.SemaphoreType.DMA((8,))],
-        compiler_params=params(63),
+        compiler_params=params(58),
     )(*mixer, *feed)
 
 
@@ -217,7 +217,7 @@
         out_specs=(ANY,) * 4,
         scratch_shapes=[pltpu.VMEM(v.shape, bf16) for v in more * 2] + [pltpu.SemaphoreType.DMA((4, 3))],
         input_output_aliases={i: i for i in range(4)},
-        compiler_params=params(63),
+        compiler_params=params(58),
     )(*values, *more)
 
 
@@ -241,20 +241,21 @@
         out_shape=tuple(jax.ShapeDtypeStruct(shape, bf16) for shape in outs),
         in_specs=blocks,
         out_specs=tuple(pl.BlockSpec(shape, lambda i: (0, 0)) for shape in outs),
-        compiler_params=params(32),
+        compiler_params=params(58),
     )(*a, *b)
     return out[:4], out[4:]
 
 
 def feed_kernel(
-    w_ref, x0_ref, x1_ref, g0_ref, g1_ref, hidden_ref, grads_ref, keep_ref, send_ref,
+    w_ref, x0_ref, x1_ref, x2_ref, x3_ref, g0_ref, g1_ref, hidden_ref, grads_ref, keep_ref, send_ref,
     held_ref, x_ref, grad_ref, sems,
 ):
     wide = hidden_ref.shape[0]
-    half = x0_ref.shape[0]
+    part = x0_ref.shape[0]
+    half = 2 * part
     given = [
-        pltpu.make_async_copy(x0_ref, x_ref.at[pl.ds(0, half), :], sems.at[48]),
-        pltpu.make_async_copy(x1_ref, x_ref.at[pl.ds(half, half), :], sems.at[49]),
+        pltpu.make_async_copy(ref, x_ref.at[pl.ds(i * part, part), :], sems.at[48 + i])
+        for i, ref in enumerate((x0_ref, x1_ref, x2_ref, x3_ref))
     ]
     weights = [
         [
@@ -268,8 +269,8 @@
         for i in range(3)
     ]
     grads = [
-        pltpu.make_async_copy(g0_ref, grad_ref.at[pl.ds(0, half), :], sems.at[50]),
-        pltpu.make_async_copy(g1_ref, grad_ref.at[pl.ds(half, half), :], sems.at[51]),
+        pltpu.make_async_copy(g0_ref, grad_ref.at[pl.ds(0, half), :], sems.at[52]),
+        pltpu.make_async_copy(g1_ref, grad_ref.at[pl.ds(half, half), :], sems.at[53]),
     ]
     for copy in given + weights[0] + weights[1] + grads + weights[2]:
         copy.start()
@@ -293,8 +294,8 @@
         out_ref[...] = dot(grads_ref[:, rows], held_ref[: 2 * wide, :], TN).astype(out_ref.dtype)
 
 
-def feed_forward_back(w, x0, x1, g0, g1):
-    half, width = x0.shape
+def feed_forward_back(w, x, g0, g1):
+    half, width = g0.shape
     wide = w.shape[0] // 48
     return pl.pallas_call(
         feed_kernel,
@@ -304,29 +305,30 @@
             jax.ShapeDtypeStruct((half, width), f32),
             jax.ShapeDtypeStruct((half, width), bf16),
         ),
-        in_specs=[ANY] * 5,
+        in_specs=[ANY] * 7,
         scratch_shapes=[
             pltpu.VMEM((3 * wide, width), bf16),
             pltpu.VMEM((2 * half, width), bf16),
             pltpu.VMEM((2 * half, width), bf16),
-            pltpu.SemaphoreType.DMA((52,)),
+            pltpu.SemaphoreType.DMA((54,)),
         ],
         cost_estimate=cost(20 * half * wide * width, 10 * wide * width),
-        compiler_params=params(63),
-    )(w, x0, x1, g0, g1)
+        compiler_params=params(58),
+    )(w, *x, g0, g1)
 
 
 def early_kernel(
-    hidden_ref, grads_ref, x0_ref, x1_ref, g0_ref, g1_ref, w_ref, out_ref, keep_ref, send_ref, turn_ref
+    hidden_ref, grads_ref, x0_ref, x1_ref, x2_ref, x3_ref, g0_ref, g1_ref, w_ref,
+    out_ref, keep_ref, send_ref, turn_ref,
 ):
     wide = hidden_ref.shape[0]
-    half = x0_ref.shape[0]
+    half = g0_ref.shape[0]
 
     @pl.when(pl.program_id(0) == 0)
     def _():
         turn_ref[...] = hidden_ref[...].T
 
-    up = dot(grads_ref[...], stacked(x0_ref[...], x1_ref[...])).astype(bf16)
+    up = dot(grads_ref[...], stacked(x0_ref[...], x1_ref[...], x2_ref[...], x3_ref[...])).astype(bf16)
     down = dot(hidden_ref[...], stacked(g0_ref[...], g1_ref[...])).astype(bf16)
     for i in range(4):
         lanes = slice(128 * i, 128 * i + 128)
@@ -337,9 +339,9 @@
     send_ref[...] = dot(turn_ref[half:, :], w).astype(bf16)
 
 
-def early_gradients(hidden, grads, x0, x1, g0, g1, w):
+def early_gradients(hidden, grads, x, g0, g1, w):
     wide, rows = hidden.shape
-    half, width = x0.shape
+    half, width = g0.shape
     block = pl.BlockSpec((half, 512), lambda i: (0, i))
     return pl.pallas_call(
         early_kernel,
@@ -352,26 +354,21 @@
         in_specs=[
             pl.BlockSpec((wide, rows), lambda i: (0, 0)),
             pl.BlockSpec((2 * wide, rows), lambda i: (0, 0)),
-            block,
-            block,
-            block,
-            block,
-            pl.BlockSpec((4, wide, 128), lambda i: (i, 2, 0)),
-        ],
+        ]
+        + [pl.BlockSpec((half // 2, 512), lambda i: (0, i))] * 4
+        + [block, block, pl.BlockSpec((4, wide, 128), lambda i: (i, 2, 0))],
         out_specs=(pl.BlockSpec((4, 3 * wide, 128), lambda i: (i, 0, 0)), block, block),
         scratch_shapes=[pltpu.VMEM((rows, wide), bf16)],
         cost_estimate=cost(14 * half * wide * width, 10 * wide * width),
-        compiler_params=params(63),
-    )(hidden, grads, x0, x1, g0, g1, w.reshape(16, 3 * wide, 128))
-
-
-def parts_kernel(steps, g_in, o_in, x_in, *refs):
-    m_in, refs = refs[:4], refs[4:]
+        compiler_params=params(58),
+    )(hidden, grads, *x, g0, g1, w.reshape(16, 3 * wide, 128))
+
+
+def parts_kernel(steps, g_in, o_in, x_in, m_in, *refs):
     outs, (g_ref, o_ref, x_ref, m_ref, sems) = refs[:-5], refs[-5:]
     plane = lax.axis_index("dp") // 2
     wide = o_ref.shape[0]
     keys = g_ref.shape[0] - 2 * wide
-    size = m_in[0].shape[0]
 
     def lanes(dx, dz):
         return pl.ds(pl.multiple_of(jnp.bitwise_xor(4 * dx + dz, plane) * 128, 128), 128)
@@ -383,7 +380,7 @@
     ]
     waits = []
     for n, d in enumerate(steps):
-        base = 3 + 24 * n
+        base = 3 + 12 * n
         copies = [[], [], []]
         for i in range(4):
             here = pl.ds(128 * i, 128)
@@ -393,14 +390,11 @@
                         x_in.at[:, at], x_ref.at[2 * n + k, :, here], sems.at[base + 4 * k + i]
                     )
                 )
-            for k, m in enumerate(m_in):
-                copies[2].append(
-                    pltpu.make_async_copy(
-                        m.at[:, lanes(i, d)],
-                        m_ref.at[n, pl.ds(k * size, size), here],
-                        sems.at[base + 8 + 4 * i + k],
-                    )
+            copies[2].append(
+                pltpu.make_async_copy(
+                    m_in.at[:, lanes(i, d)], m_ref.at[n, :, here], sems.at[base + 8 + i]
                 )
+            )
         if n == 0:
             for k in range(3):
                 copies[k].append(fixed[k])
@@ -440,18 +434,18 @@
         functools.partial(parts_kernel, steps),
         grid=(1,),
         out_shape=tuple(jax.ShapeDtypeStruct(shape, bf16) for shape in shapes),
-        in_specs=[ANY] * 7,
+        in_specs=[ANY] * 4,
         out_specs=tuple(pl.BlockSpec(shape, lambda i: (0, 0, 0)) for shape in shapes),
         scratch_shapes=[
             pltpu.VMEM(g.shape, bf16),
             pltpu.VMEM(o.shape, bf16),
             pltpu.VMEM((2 * len(steps), rows, 512), bf16),
             pltpu.VMEM((len(steps), rows, 512), bf16),
-            pltpu.SemaphoreType.DMA((3 + 24 * len(steps),)),
+            pltpu.SemaphoreType.DMA((3 + 12 * len(steps),)),
         ],
         cost_estimate=cost(rows * 512 * (ra + rb) * 2 * len(steps), 6 * rows * 2048),
-        compiler_params=params(63),
-    )(g, o, x, *m)
+        compiler_params=params(58),
+    )(g, o, x, m)
 
 
 def early_out_kernel(sum_ref, keep_ref, send_ref):
@@ -580,20 +574,20 @@
         out_specs=(ANY, pl.BlockSpec((1, width), lambda i: (0, 0))),
         scratch_shapes=[pltpu.VMEM((half, width), bf16), pltpu.SemaphoreType.DMA((4,))],
         cost_estimate=cost(2 * size * total * width, 10 * total * width),
-        compiler_params=params(63),
+        compiler_params=params(58),
     )(g, w, x)
 
 
 def gather_line_first(own, *beside):
-    r1, r3, *beside = tie(move(own, Y1), move(own, Y3), *beside)
-    mine = stacked(own, r1)
+    r1, r3, core, *beside = tie(move(own, Y1), move(own, Y3), move(own, C1), *beside)
     half = own.shape[0] // 2
-    return (mine, move(mine, C1)), (move(r3[:half], Y1), move(r1[half:], Y3), r3), beside
-
-
-def gather_line_last(r2p, r2q, r3):
-    other = stacked(r2p, r2q, r3)
-    return other, move(other, C1)
+    left = move(r3[:half], Y1), move(r1[half:], Y3), r3, move(r3, C1)
+    return (own, r1, core, move(r1, C1)), left, beside
+
+
+def gather_line_last(r2p, r2q, r3, core):
+    r2 = stacked(r2p, r2q)
+    return r2, r3, move(r2, C1), core
 
 
 def scatter_line(keep_m, send_m, keep_o, send_o):
@@ -610,8 +604,8 @@
 
 
 def gather_pair(own):
-    mine = stacked(own, move(own, Y1))
-    return mine, move(mine, C1)
+    far, core = tie(move(own, Y1), move(own, C1))
+    return own, far, core, move(far, C1)
 
 
 def scatter_pair(keep, send, *beside):
@@ -747,22 +741,24 @@
             pltpu.SemaphoreType.DMA((42,)),
         ],
         cost_estimate=cost(2 * size * total * width, 16 * total * width),
-        compiler_params=params(63),
+        compiler_params=params(58),
     )(*blocks, line, decay, gain)
 
 
 def mixer_back_kernel(
-    g0_ref, g1_ref, w_ref, q_ref, k_ref, v_ref, gate_ref, decay_ref, gain_ref, retained_ref, *refs
+    group, g0_ref, g1_ref, g2_ref, g3_ref, w_ref, q_ref, k_ref, v_ref, gate_ref, decay_ref, gain_ref,
+    retained_ref, *refs,
 ):
-    out_ref, gain_out_ref, grad_ref, wo_ref, sems = refs[-5:]
+    out_ref, gain_out_ref, all_ref, grad_ref, wo_ref, sems = refs[-6:]
     kwide, wide = q_ref.shape[1], v_ref.shape[1]
     keys = 2 * kwide
-    half = g0_ref.shape[0]
-    copies = [
-        pltpu.make_async_copy(w_ref.at[pl.ds(0, wide), :], wo_ref, sems.at[2]),
-        pltpu.make_async_copy(g0_ref, grad_ref.at[pl.ds(0, half), :], sems.at[0]),
-        pltpu.make_async_copy(g1_ref, grad_ref.at[pl.ds(half, half), :], sems.at[1]),
+    part = g0_ref.shape[0]
+    rows = 4 * part
+    copies = [pltpu.make_async_copy(w_ref.at[pl.ds(0, wide), :], wo_ref, sems.at[4])] + [
+        pltpu.make_async_copy(ref, grad_ref.at[pl.ds(i * part, part), :], sems.at[i])
+        for i, ref in enumerate((g0_ref, g1_ref, g2_ref, g3_ref))
     ]
+    back_copy = pltpu.make_async_copy(grad_ref, all_ref.at[pl.ds(group * rows, rows), :], sems.at[5])
     for copy in copies:
         copy.start()
     q, k, v, decay = q_ref[...], k_ref[...], v_ref[...], decay_ref[...]
@@ -777,6 +773,7 @@
     silu = gate * sig
     for copy in copies:
         copy.wait()
+    back_copy.start()
     grad = dot(grad_ref[...], wo_ref[...], NT)
     grad_normed = grad * normed
     out_ref[keys + wide :, :] = (grad_normed * gain * (sig * (1.0 + gate * (1.0 - sig)))).astype(bf16).T
@@ -792,36 +789,37 @@
     out_ref[keys : keys + wide, :] = dot(back, weights, TN).astype(bf16)
     out_ref[kwide:keys, :] = dot(q, grad_scores, TN).astype(bf16)
     out_ref[:kwide, :] = dot(grad_scores, k).astype(bf16).T
-
-
-def mixer_backward(group, grads, w, q, k, v, gate, decay, gain, retained, before=None):
+    back_copy.wait()
+
+
+def mixer_backward(group, grads, w, q, k, v, gate, decay, gain, retained, before=()):
     kwide, wide = q.shape[1], v.shape[1]
     rows = decay.shape[0]
     slim = pl.BlockSpec((rows, kwide), lambda i: (group, 0))
     whole = pl.BlockSpec((rows, wide), lambda i: (group, 0))
     line = pl.BlockSpec((1, wide), lambda i: (0, 0))
     size = 2 * kwide + 2 * wide
-    given = [] if before is None else [before]
     return pl.pallas_call(
-        mixer_back_kernel,
+        functools.partial(mixer_back_kernel, group),
         grid=(1,),
         out_shape=(
             jax.ShapeDtypeStruct((size, q.shape[0]), bf16),
             jax.ShapeDtypeStruct((1, wide), f32),
+            jax.ShapeDtypeStruct((q.shape[0], w.shape[1]), bf16),
         ),
-        in_specs=[ANY] * 3
+        in_specs=[ANY] * 5
         + [slim, slim, whole, whole, pl.BlockSpec((rows, rows), lambda i: (0, 0)), line, whole]
-        + [ANY] * len(given),
-        out_specs=(pl.BlockSpec((size, rows), lambda i: (0, group)), line),
-        input_output_aliases={10: 0} if given else {},
+        + [ANY] * len(before),
+        out_specs=(pl.BlockSpec((size, rows), lambda i: (0, group)), line, ANY),
+        input_output_aliases={12: 0, 13: 2} if before else {},
         scratch_shapes=[
             pltpu.VMEM((rows, w.shape[1]), bf16),
             pltpu.VMEM((wide, w.shape[1]), bf16),
-            pltpu.SemaphoreType.DMA((3,)),
+            pltpu.SemaphoreType.DMA((6,)),
         ],
         cost_estimate=cost(2 * rows * (size + wide) * 1024, 8 * rows * 2048),
-        compiler_params=params(63),
-    )(*grads, w, q, k, v, gate, decay, gain, retained, *given)
+        compiler_params=params(58),
+    )(*grads, w, q, k, v, gate, decay, gain, retained, *before)
 
 
 def shards(
@@ -890,9 +888,9 @@
     r2 = lax.rsqrt(jnp.mean(middle * middle, axis=-1, keepdims=True) + norm_eps)
     normed_mid = (middle * r2 * feed_gain).astype(bf16)
     mid = gather_pair(normed_mid)
-    hidden, grads, keep, send = feed_forward_back(second, *mid, *grad_feed)
+    hidden, grads, keep, send = feed_forward_back(second, mid, *grad_feed)
     early, feed_keep, feed_send = early_gradients(
-        hidden, grads, *mid, *grad_feed, second
+        hidden, grads, mid, *grad_feed, second
     )
     grad_normed_mid, early, feed_keep, feed_send = scatter_pair(keep, send, early, feed_keep, feed_send)
     early_sum = lax.psum_scatter(
@@ -912,21 +910,17 @@
         feed_keep[:rows].astype(f32) + feed_got[:rows].astype(f32),
         add_low(feed_keep[rows:], feed_got[rows:]),
     )
-    grads, gain_m = mixer_backward(
+    grads, gain_m, grad_mixer = mixer_backward(
         0, grad_mixer_m, w_mixer, q, k, v, gate, decay, group_own, retained
     )
-    left, grads, feed_send = tie(left, grads, feed_send)
+    left, grads, grad_mixer, feed_send = tie(left, grads, grad_mixer, feed_send)
     grad_mixer_o = gather_line_last(*left)
-    grads, gain_o = mixer_backward(
-        1, grad_mixer_o, w_mixer, q, k, v, gate, decay, group_own, retained, grads
+    grads, gain_o, grad_mixer = mixer_backward(
+        1, grad_mixer_o, w_mixer, q, k, v, gate, decay, group_own, retained, (grads, grad_mixer)
     )
     part_group_gain = (gain_m + gain_o).reshape(-1)
-    grad_mixer = *grad_mixer_m, *grad_mixer_o
-    *sent, grads, feed_far, group_far = tie(
-        *gradient_parts((2,), 2, grads, mixed, normed_group, grad_mixer),
-        grads,
-        move(feed_send, Y1),
-        move(part_group_gain, Y2),
+    *sent, grads, feed_far = tie(
+        *gradient_parts((2,), 2, grads, mixed, normed_group, grad_mixer), grads, move(feed_send, Y1)
     )
 
     moved = [move(part, pairs) for part, pairs in zip(sent, (Z1, Z3, X1, X3))]
@@ -945,34 +939,35 @@
     moved = move(a3, Z3), move(a1, Z1), move(b3, X3), move(b1, X1)
     a0, b0 = gradient_parts((0,), 1, grads, mixed, normed_group, grad_mixer)
     result = (middle + valid_rows * (feed_keep + feed_far.astype(f32))).astype(bf16)
-    gains = gains + move(gains, Y2)
+    gains = jnp.concatenate([gains, part_group_gain])
+    far = move(gains, Y2)
+    group_far = far[2 * width :]
     gains = jnp.concatenate(
         [
-            gains,
+            gains[: 2 * width] + far[: 2 * width],
             jnp.where(is_low, part_group_gain, group_far),
             jnp.where(is_low, group_far, part_group_gain),
         ]
     )
-    back, early_sum, _ = tie(back, early_sum, a3)
+    back, early_sum, _ = tie(back, early_sum, a0)
     grad_normed_in = lax.psum_scatter(
         back, AXES, axis_index_groups=LINES, scatter_dimension=0, tiled=True
     ).astype(f32)
-    gains, a0, b0, result = tie(gains, a0, b0, result)
-    r3, r1_, s3, s1, gains = tie(*moved, gains + move(gains, X1))
-    a, b = tie(*add_blocks((a0, r3, r1_), (b0, s3, s1)))
+    r3, r1_, s3, s1, gains, a0, b0 = tie(*moved, gains, a0, b0)
+    a, b, gains = tie(*add_blocks((a0, r3, r1_), (b0, s3, s1)), gains + move(gains, X1))
+    *moved, gains, g_gelu, g_linear, g_down, result = tie(
+        *(move(a[i], (X1, X2, X3)[i - 1]) for i in (1, 2, 3)),
+        *(move(b[i], (Z1, Z2, Z3)[i - 1]) for i in (1, 2, 3)),
+        gains + move(gains, X2),
+        *settle_early(early_sum),
+        result,
+    )
+    for pairs in (Z1, Z2):
+        gains = gains + move(gains, pairs)
     z1 = grad_normed_in * mixer_gain
     grad_tokens = (
         grad_middle + r1 * z1 - token_float * (r1 * r1 * r1) * jnp.mean(z1 * token_float, axis=-1, keepdims=True)
     ).astype(bf16)
-    *moved, gains, g_gelu, g_linear, g_down, grad_tokens = tie(
-        *(move(a[i], (X1, X2, X3)[i - 1]) for i in (1, 2, 3)),
-        *(move(b[i], (Z1, Z2, Z3)[i - 1]) for i in (1, 2, 3)),
-        gains + move(gains, X2),
-        *settle_early(early_sum),
-        grad_tokens,
-    )
-    for pairs in (Z1, Z2):
-        gains = gains + move(gains, pairs)
     sum_a, sum_b = (a[0], *moved[:3]), (b[0], *moved[3:])
     g_output, g_query, g_key, g_value, g_swish = settle_late(
         sum_a, sum_b, (wide, kwide, kwide, wide, wide)

time: 366 us -> 360 us (0.984)
  local copies, waits for them, and re-layouts: 25.4 us -> 11 us
  waiting for transfers between devices: 104 us -> 111 us
  starting transfers between devices: 72 us -> 77 us
  other arithmetic: 27.9 us -> 23.9 us
    unnamed x104 -> x98, local copies, waits for them, and re-layouts: 20.1 us -> 8.15 us
    reduce_scatter x1, waiting for transfers between devices: 0.91 us -> 7.74 us  [shards(): lax.psum_scatter(early.reshape(-1, 128), AXES, axis_index_groups=PLANES,...]
    ppermute x60 -> x62, starting transfers between devices: 71.6 us -> 76.7 us  [move(): return lax.ppermute(value, AXES, pairs)]
    ppermute x60 -> x62, waiting for transfers between devices: 103 us -> 104 us  [move(): return lax.ppermute(value, AXES, pairs)]
  transfers between devices with their start and end apart: 64 -> 66, of which waited for: 26 -> 25; matrix products, arithmetic and copies ran while one was open for 10% -> 6% of each run, Pallas kernels for 26% -> 27%
where the time goes in v5:
time: 360 us; the launch traced here: 354 us
  Pallas kernels  114 us (32%)
  waiting for transfers between devices  111 us (31%)
  starting transfers between devices  77 us (21%)
  other arithmetic  23.9 us (7%)
  between operations  16.8 us (5%)
  local copies, waits for them, and re-layouts  11 us (3%)
    ppermute x62, waiting for transfers between devices, move(): return lax.ppermute(value, AXES, pairs)  104 us
    ppermute x62, starting transfers between devices, move(): return lax.ppermute(value, AXES, pairs)  76.7 us
    pallas_call x1, Pallas kernels, mixer_forward(): pl.pallas_call(mixer_kernel, grid=(2,), out_shape=(jax.ShapeDtypeStruct((...  19.7 us
    pallas_call x3, Pallas kernels, gradient_parts(): pl.pallas_call(functools.partial(parts_kernel, steps), grid=(1,), out_sha...  19.1 us
    pallas_call x2, Pallas kernels, mixer_backward(): pl.pallas_call(functools.partial(mixer_back_kernel, group), grid=(1,), ou...  17 us
    pallas_call x1, Pallas kernels, feed_forward_back(): pl.pallas_call(feed_kernel, out_shape=(jax.ShapeDtypeStruct((wide, 2 * ha...  15 us
    pallas_call x1, Pallas kernels, input_gradients(): pl.pallas_call(back_kernel, grid=(2,), out_shape=(jax.ShapeDtypeStruct((t...  14.5 us
    pallas_call x1, Pallas kernels, early_gradients(): pl.pallas_call(early_kernel, grid=(4,), out_shape=(jax.ShapeDtypeStruct((...  12.9 us
  transfers between devices with their start and end apart: 66, of which 25 were waited for; matrix products, arithmetic and copies ran while one was open for 6% of the time, Pallas kernels for 27%

profile of v5, /device:TPU:0, one launch (start us, length us, event | category | flops | bytes accessed | tf_op | source)
XLA Modules:
  0.0 354.3 jit_solution(15150299236353904577)
XLA Ops:
  9.6 3.4 collective-permute-start
  31.5 7.4 %collective-permute-done.4 = bf16[864,128]{1,0:T(8,128)(2,1)S(1)} collective-permute-done((bf16[864,128]{1,0:T(8,128)(2,1)S(1)}, bf16[864,128]{1,0:T(8,128)(2,1)S(1)}, u32[]{:S(2)}, u32[]{:S(2)}) %collective-permute-start.4) | collective-permute-done | bytes 221216 | tf_op jit(solution)/shard_map/ppermute | solution.py:55
  51.6 8.6 %collective-permute-done.11.got_ref = bf16[64,2688]{1,0:T(8,128)(2,1)S(1)} collective-permute-done((bf16[64,2688]{1,0:T(8,128)(2,1)S(1)}, bf16[64,2688]{1,0:T(8,128)(2,1)S(1)}, u32[]{:S(2)}, u32[]{:S(2)}) %collective-permute-start.11) | collective-permute-done | bytes 344096 | tf_op jit(solution)/shard_map/ppermute | solution.py:55
  75.9 7.5 %collective-permute-done.14.refs_7_ = bf16[2,864,128]{2,1,0:T(8,128)(2,1)S(1)} collective-permute-done((bf16[2,864,128]{2,1,0:T(8,128)(2,1)}, bf16[2,864,128]{2,1,0:T(8,128)(2,1)S(1)}, u32[]{:S(2)}, u32[]{:S(2)}) %collective-permute-start.14) | collective-permute-done | bytes 442400 | tf_op jit(solution)/shard_map/ppermute | solution.py:55
  88.5 19.7 %shard_map.249 = (bf16[1808,2048]{1,0:T(8,128)(2,1)}, bf16[1024,2048]{1,0:T(8,128)(2,1)}, bf16[1024,256]{1,0:T(8,128)(2,1)}, bf16[1024,256]{1,0:T(8,128)(2,1)}, ...) custom-call(bf16[4,944,128]{2,1,0:T(8,128)(2,1)} %pad_maximum_fusion, ...), custom_call_target="tpu_custom_call" | custom-call | flops 7583301632 | bytes 33554432 | tf_op jit(solution)/shard_map/pallas_call | solution.py:705
  113.8 3.1 collective-permute-start.21
  117.3 4.4 %collective-permute-done.20 = bf16[64,2048]{1,0:T(8,128)(2,1)S(1)} collective-permute-done((bf16[64,2048]{1,0:T(8,128)(2,1)S(1)}, bf16[64,2048]{1,0:T(8,128)(2,1)S(1)}, u32[]{:S(2)}, u32[]{:S(2)}) %collective-permute-start.20) | collective-permute-done | bytes 262176 | tf_op jit(solution)/shard_map/ppermute | solution.py:55
  126.8 11.4 %collective-permute-done.22 = bf16[128,2048]{1,0:T(8,128)(2,1)S(1)} collective-permute-done((bf16[128,2048]{1,0:T(8,128)(2,1)S(1)}, bf16[128,2048]{1,0:T(8,128)(2,1)S(1)}, u32[]{:S(2)}, u32[]{:S(2)}) %collective-permute-start.22) | collective-permute-done | bytes 524320 | tf_op jit(solution)/shard_map/ppermute | solution.py:55
  140.7 11.8 %collective-permute-done.24.x1_ref = bf16[128,2048]{1,0:T(8,128)(2,1)S(1)} collective-permute-done((bf16[128,2048]{1,0:T(8,128)(2,1)S(1)}, bf16[128,2048]{1,0:T(8,128)(2,1)S(1)}, u32[]{:S(2)}, u32[]{:S(2)}) %collective-permute-start.24) | collective-permute-done | bytes 524320 | tf_op jit(solution)/shard_map/ppermute | solution.py:55
  154.8 15.0 %shard_map.251 = (bf16[864,512]{1,0:T(8,128)(2,1)}, bf16[1728,512]{1,0:T(8,128)(2,1)}, f32[256,2048]{1,0:T(8,128)}, bf16[256,2048]{1,0:T(8,128)(2,1)}) custom-call(bf16[41472,128]{1,0:T(8,128)(2,1)} %all-gather.5.cloned.1.call-done.w_ref, bf16[128,2048]{1,0:T(8,128)(2,1)} %copy-done.28, bf16[128,2048]{1,0:T(8,128)(2,1)} %copy-done.42, ...), custom_call_target="tpu_custom_call" | custom-call | flops 9059696640 | bytes 17694720 | tf_op jit(solution)/shard_map/pallas_call | solution.py:300
  176.7 12.9 %shard_map.252 = (bf16[16,2592,128]{2,1,0:T(8,128)(2,1)}, bf16[256,2048]{1,0:T(8,128)(2,1)}, bf16[256,2048]{1,0:T(8,128)(2,1)}) custom-call(bf16[864,512]{1,0:T(8,128)(2,1)} %get-tuple-element.245.hidden_ref, bf16[1728,512]{1,0:T(8,128)(2,1)} %get-tuple-element.246.grads_ref, bf16[128,2048]{1,0:T(8,128)(2,1)} %copy-done.28, bf16[128,2048]{1,0:T(8,128)(2,1)} %copy-done.42, ...), custom_call_target="tpu_custom_call" | custom-call | flops 6341787648 | bytes 17694720 | tf_op jit(solution)/shard_map/pallas_call | solution.py:346
  197.8 10.4 %collective-permute-done.29.g1_ref = bf16[128,2048]{1,0:T(8,128)(2,1)S(1)} collective-permute-done((bf16[128,2048]{1,0:T(8,128)(2,1)S(1)}, bf16[128,2048]{1,0:T(8,128)(2,1)S(1)}, u32[]{:S(2)}, u32[]{:S(2)}) %collective-permute-start.29) | collective-permute-done | bytes 524320 | tf_op jit(solution)/shard_map/ppermute | solution.py:55
  213.3 8.4 %shard_map.253 = (bf16[1376,1024]{1,0:T(8,128)(2,1)}, f32[1,432]{1,0:T(1,128)}, bf16[1024,2048]{1,0:T(8,128)(2,1)}) custom-call(bf16[128,2048]{1,0:T(8,128)(2,1)} %copy-done.17, bf16[128,2048]{1,0:T(8,128)(2,1)} %copy-done.20, bf16[128,2048]{1,0:T(8,128)(2,1)} %copy-done.25, bf16[128,2048]{1,0:T(8,128)(2,1)} %copy-done.26, ...), custom_call_target="tpu_custom_call" | custom-call | flops 1895825408 | bytes 8388608 | tf_op jit(solution)/shard_map/pallas_call | solution.py:802
  224.6 8.7 %shard_map.254 = (bf16[1376,1024]{1,0:T(8,128)(2,1)}, f32[1,432]{1,0:T(1,128)}, bf16[1024,2048]{1,0:T(8,128)(2,1)}) custom-call(bf16[128,2048]{1,0:T(8,128)(2,1)} %copy-done.21, bf16[128,2048]{1,0:T(8,128)(2,1)} %copy-done.19, bf16[128,2048]{1,0:T(8,128)(2,1)} %copy-done.27, ...), custom_call_target="tpu_custom_call", output_to_operand_aliasing={{0}: (12, {}), {2}: (13, {})} | custom-call | flops 1895825408 | bytes 8388608 | tf_op jit(solution)/shard_map/pallas_call | solution.py:802
  233.2 5.5 %shard_map.255 = (bf16[2,944,128]{2,1,0:T(8,128)(2,1)}, bf16[2,944,128]{2,1,0:T(8,128)(2,1)}, bf16[2,864,128]{2,1,0:T(8,128)(2,1)}, bf16[2,864,128]{2,1,0:T(8,128)(2,1)}) custom-call(bf16[1376,1024]{1,0:T(8,128)(2,1)} %get-tuple-element.315.g_in.g_ref, bf16[432,1024]{1,0:T(8,128)(2,1)} %get-tuple-element.274.o_in, ...), custom_call_target="tpu_custom_call" | custom-call | flops 1895825408 | bytes 12582912 | tf_op jit(solution)/shard_map/pallas_call | solution.py:433
  242.4 14.5 %shard_map.256 = (bf16[1024,2048]{1,0:T(8,128)(2,1)}, f32[1,2048]{1,0:T(1,128)}) custom-call(bf16[1376,1024]{1,0:T(8,128)(2,1)} %get-tuple-element.315.g_in.g_ref, bf16[1808,2048]{1,0:T(8,128)(2,1)} %get-tuple-element.258.w_ref, bf16[1024,2048]{1,0:T(8,128)(2,1)} %get-tuple-element.275.x_in.x_ref), custom_call_target="tpu_custom_call" | custom-call | flops 5771362304 | bytes 20971520 | tf_op jit(solution)/shard_map/pallas_call | solution.py:562
  257.6 8.2 %shard_map.257 = (bf16[4,944,128]{2,1,0:T(8,128)(2,1)}, bf16[4,864,128]{2,1,0:T(8,128)(2,1)}, bf16[4,944,128]{2,1,0:T(8,128)(2,1)}, bf16[4,864,128]{2,1,0:T(8,128)(2,1)}) custom-call(bf16[1376,1024]{1,0:T(8,128)(2,1)} %get-tuple-element.315.g_in.g_ref, bf16[432,1024]{1,0:T(8,128)(2,1)} %get-tuple-element.274.o_in, ...), custom_call_target="tpu_custom_call" | custom-call | flops 3791650816 | bytes 12582912 | tf_op jit(solution)/shard_map/pallas_call | solution.py:433
  270.2 5.4 %shard_map.259 = (bf16[4,944,128]{2,1,0:T(8,128)(2,1)}, bf16[4,864,128]{2,1,0:T(8,128)(2,1)}) custom-call(bf16[1376,1024]{1,0:T(8,128)(2,1)} %get-tuple-element.315.g_in.g_ref, bf16[432,1024]{1,0:T(8,128)(2,1)} %get-tuple-element.274.o_in, bf16[1024,2048]{1,0:T(8,128)(2,1)} %get-tuple-element.275.x_in.x_ref, bf16[1024,2048]{1,0:T(8,128)(2,1)} %get-tuple-element.276.m_in), custom_call_target="tpu_custom_call" | custom-call | flops 1895825408 | bytes 12582912 | tf_op jit(solution)/shard_map/pallas_call | solution.py:433
  275.6 7.7 %reduce-scatter.3.cloned.1.call-done.sum_ref = bf16[2592,128]{1,0:T(8,128)(2,1)} async-done(((bf16[41472,128]{1,0:T(8,128)(2,1)}), bf16[2592,128]{1,0:T(8,128)(2,1)}) %reduce-scatter.3.cloned.1.call-update) | async-done | bytes 663568 | tf_op jit(solution)/shard_map/reduce_scatter | solution.py:896
  293.1 3.1 collective-permute-start.58
  296.3 11.1 %collective-permute-done.47.refs_4_ = bf16[4,864,128]{2,1,0:T(8,128)(2,1)} collective-permute-done((bf16[4,864,128]{2,1,0:T(8,128)(2,1)}, bf16[4,864,128]{2,1,0:T(8,128)(2,1)}, u32[]{:S(2)}, u32[]{:S(2)}) %collective-permute-start.47) | collective-permute-done | bytes 884768 | tf_op jit(solution)/shard_map/ppermute | solution.py:55
  308.3 5.0 %shard_map.260 = (bf16[944,128]{1,0:T(8,128)(2,1)}, bf16[944,128]{1,0:T(8,128)(2,1)}, bf16[944,128]{1,0:T(8,128)(2,1)}, bf16[944,128]{1,0:T(8,128)(2,1)}, bf16[8...) custom-call(bf16[4,944,128]{2,1,0:T(8,128)(2,1)} %get-tuple-element.318.refs, ...), custom_call_target="tpu_custom_call" | custom-call | tf_op jit(solution)/shard_map/pallas_call | solution.py:238
  314.4 3.2 collective-permute-start.57
  333.3 3.1 collective-permute-start.61
  (280 shorter events, 138.0 us)
Async XLA Ops:
  7.2 81.3 %all-gather.3.cloned.1.call-start = ((), (), s32[]{:S(2)}) async-start(), calls=%async_computation.2 | async-start | bytes 4718592 | tf_op jit(solution)/shard_map/all_gather | solution.py:875
  20.3 134.4 %all-gather.5.cloned.1.call-start = ((), (), s32[]{:S(2)}) async-start(), calls=%async_computation.3 | async-start | bytes 11280384 | tf_op jit(solution)/shard_map/all_gather | solution.py:879
  22.6 16.2 %collective-permute-start.1 = (bf16[944,128]{1,0:T(8,128)(2,1)S(1)}, bf16[944,128]{1,0:T(8,128)(2,1)S(1)}, u32[]{:S(2)}, u32[]{:S(2)}) collective-permute-start(bf16[944,128]{1,0:T(8,128)(2,1)S(1)} %get-tuple-element.195), channel_id=1, source_target_pairs={{0,32},{1,33},{2,34},{3,35},{4,36},{5,37},{6,38},{7,39},{8,40},{9,... | collective-permute-start | bytes 725000 | tf_op jit(solution)/shard_map/ppermute | solution.py:55
  41.0 23.2 %collective-permute-start.7 = (bf16[4,944,128]{2,1,0:T(8,128)(2,1)}, bf16[4,944,128]{2,1,0:T(8,128)(2,1)S(1)}, u32[]{:S(2)}, u32[]{:S(2)}) collective-permute-start(bf16[4,944,128]{2,1,0:T(8,128)(2,1)} %pad_maximum_fusion.refs_0_), channel_id=1, source_target_pairs={{0,8},{1,9},{2,10},{3,11},{4,12},{5,13},{6,14},{7,15},{8,0},{9,1},... | collective-permute-start | bytes 2899976 | tf_op jit(solution)/shard_map/ppermute | solution.py:55
  41.6 22.7 %collective-permute-start.8 = (bf16[4,944,128]{2,1,0:T(8,128)(2,1)}, bf16[4,944,128]{2,1,0:T(8,128)(2,1)S(1)}, u32[]{:S(2)}, u32[]{:S(2)}) collective-permute-start(bf16[4,944,128]{2,1,0:T(8,128)(2,1)} %pad_maximum_fusion.refs_0_), channel_id=1, source_target_pairs={{0,24},{1,25},{2,26},{3,27},{4,28},{5,29},{6,30},{7,31},{8,16},{9,... | collective-permute-start | bytes 2899976 | tf_op jit(solution)/shard_map/ppermute | solution.py:55
  43.9 19.0 %collective-permute-start.9 = (bf16[4,864,128]{2,1,0:T(8,128)(2,1)}, bf16[4,864,128]{2,1,0:T(8,128)(2,1)S(1)}, u32[]{:S(2)}, u32[]{:S(2)}) collective-permute-start(bf16[4,864,128]{2,1,0:T(8,128)(2,1)} %pad_maximum_fusion.1.refs_5_), channel_id=1, source_target_pairs={{0,32},{1,33},{2,34},{3,35},{4,36},{5,37},{6,38},{7,39},{8,40},{9,... | collective-permute-start | bytes 2654216 | tf_op jit(solution)/shard_map/ppermute | solution.py:55
  45.2 19.1 %collective-permute-start.10 = (bf16[4,864,128]{2,1,0:T(8,128)(2,1)}, bf16[4,864,128]{2,1,0:T(8,128)(2,1)}, u32[]{:S(2)}, u32[]{:S(2)}) collective-permute-start(bf16[4,864,128]{2,1,0:T(8,128)(2,1)} %pad_maximum_fusion.1.refs_5_), channel_id=1, source_target_pairs={{0,96},{1,97},{2,98},{3,99},{4,100},{5,101},{6,102},{7,103},{8,104... | collective-permute-start | bytes 2654216 | tf_op jit(solution)/shard_map/ppermute | solution.py:55
  70.2 213.2 %reduce-scatter.3.cloned.1.call-start = ((), (), s32[]{:S(2)}) async-start(), calls=%async_computation.4 | async-start | bytes 11280384 | tf_op jit(solution)/shard_map/reduce_scatter | solution.py:896
  70.2 16.2 %collective-permute-start.16 = (bf16[128,2048]{1,0:T(8,128)(2,1)}, bf16[128,2048]{1,0:T(8,128)(2,1)S(1)}, u32[]{:S(2)}, u32[]{:S(2)}) collective-permute-start(bf16[128,2048]{1,0:T(8,128)(2,1)} %fusion), channel_id=1, source_target_pairs={{0,2},{1,3},{2,0},{3,1},{4,6},{5,7},{6,4},{7,5},{8,10},{9,11},{10,... | collective-permute-start | bytes 1572872 | tf_op jit(solution)/shard_map/ppermute | solution.py:55
  70.8 15.6 %collective-permute-start.12 = (bf16[2,944,128]{2,1,0:T(8,128)(2,1)}, bf16[2,944,128]{2,1,0:T(8,128)(2,1)S(1)}, u32[]{:S(2)}, u32[]{:S(2)}) collective-permute-start(bf16[2,944,128]{2,1,0:T(8,128)(2,1)} %copy-done.9), channel_id=1, source_target_pairs={{0,8},{1,9},{2,10},{3,11},{4,12},{5,13},{6,14},{7,15},{8,0},{9,1},... | collective-permute-start | bytes 1449992 | tf_op jit(solution)/shard_map/ppermute | solution.py:55
  70.8 15.6 %collective-permute-start.13 = (bf16[2,944,128]{2,1,0:T(8,128)(2,1)}, bf16[2,944,128]{2,1,0:T(8,128)(2,1)S(1)}, u32[]{:S(2)}, u32[]{:S(2)}) collective-permute-start(bf16[2,944,128]{2,1,0:T(8,128)(2,1)} %copy-done.8), channel_id=1, source_target_pairs={{0,24},{1,25},{2,26},{3,27},{4,28},{5,29},{6,30},{7,31},{8,16},{9,... | collective-permute-start | bytes 1449992 | tf_op jit(solution)/shard_map/ppermute | solution.py:55
  87.2 21.0 %collective-permute-start.17 = (bf16[256,2048]{1,0:T(8,128)(2,1)S(1)}, bf16[256,2048]{1,0:T(8,128)(2,1)S(1)}, u32[]{:S(2)}, u32[]{:S(2)}) collective-permute-start(bf16[256,2048]{1,0:T(8,128)(2,1)S(1)} %constant_dynamic-update-slice_fusion.g0_ref), channel_id=1, source_target_pairs={{0,1},{1,0},{2,3},{3,2},{4,5},{5,4},{6,7},{7,6},{8,9},{9,8},{10,11... | collective-permute-start | bytes 3145736 | tf_op jit(solution)/shard_map/ppermute | solution.py:55
  190.1 154.0 %reduce-scatter.5.cloned.1.call-start = ((), (), s32[]{:S(2)}) async-start(), calls=%async_computation.5 | async-start | bytes 4718592 | tf_op jit(solution)/shard_map/reduce_scatter | solution.py:953
  194.8 15.2 %collective-permute-start.30 = (bf16[128,2048]{1,0:T(8,128)(2,1)S(1)}, bf16[128,2048]{1,0:T(8,128)(2,1)S(1)}, u32[]{:S(2)}, u32[]{:S(2)}) collective-permute-start(bf16[128,2048]{1,0:T(8,128)(2,1)S(1)} %get-tuple-element.252.g0_ref), channel_id=1, source_target_pairs={{0,6},{1,7},{2,4},{3,5},{4,2},{5,3},{6,0},{7,1},{8,14},{9,15},{10,... | collective-permute-start | bytes 1572872 | tf_op jit(solution)/shard_map/ppermute | solution.py:55
  221.9 16.9 %collective-permute-start.38 = (bf16[128,2048]{1,0:T(8,128)(2,1)S(1)}, bf16[128,2048]{1,0:T(8,128)(2,1)S(1)}, u32[]{:S(2)}, u32[]{:S(2)}) collective-permute-start(bf16[128,2048]{1,0:T(8,128)(2,1)S(1)} %get-tuple-element.281), channel_id=1, source_target_pairs={{0,2},{1,3},{2,0},{3,1},{4,6},{5,7},{6,4},{7,5},{8,10},{9,11},{10,... | collective-permute-start | bytes 1572872 | tf_op jit(solution)/shard_map/ppermute | solution.py:55
  238.8 27.0 %collective-permute-start.39 = (bf16[2,944,128]{2,1,0:T(8,128)(2,1)}, bf16[2,944,128]{2,1,0:T(8,128)(2,1)S(1)}, u32[]{:S(2)}, u32[]{:S(2)}) collective-permute-start(bf16[2,944,128]{2,1,0:T(8,128)(2,1)} %get-tuple-element.282), channel_id=1, source_target_pairs={{0,8},{1,9},{2,10},{3,11},{4,12},{5,13},{6,14},{7,15},{8,0},{9,1},... | collective-permute-start | bytes 1449992 | tf_op jit(solution)/shard_map/ppermute | solution.py:55
  238.9 27.0 %collective-permute-start.40 = (bf16[2,944,128]{2,1,0:T(8,128)(2,1)}, bf16[2,944,128]{2,1,0:T(8,128)(2,1)S(1)}, u32[]{:S(2)}, u32[]{:S(2)}) collective-permute-start(bf16[2,944,128]{2,1,0:T(8,128)(2,1)} %get-tuple-element.283), channel_id=1, source_target_pairs={{0,24},{1,25},{2,26},{3,27},{4,28},{5,29},{6,30},{7,31},{8,16},{9,... | collective-permute-start | bytes 1449992 | tf_op jit(solution)/shard_map/ppermute | solution.py:55
  240.3 25.5 %collective-permute-start.41 = (bf16[2,864,128]{2,1,0:T(8,128)(2,1)}, bf16[2,864,128]{2,1,0:T(8,128)(2,1)S(1)}, u32[]{:S(2)}, u32[]{:S(2)}) collective-permute-start(bf16[2,864,128]{2,1,0:T(8,128)(2,1)} %get-tuple-element.284), channel_id=1, source_target_pairs={{0,32},{1,33},{2,34},{3,35},{4,36},{5,37},{6,38},{7,39},{8,40},{9,... | collective-permute-start | bytes 1327112 | tf_op jit(solution)/shard_map/ppermute | solution.py:55
  240.7 25.1 %collective-permute-start.42 = (bf16[2,864,128]{2,1,0:T(8,128)(2,1)}, bf16[2,864,128]{2,1,0:T(8,128)(2,1)}, u32[]{:S(2)}, u32[]{:S(2)}) collective-permute-start(bf16[2,864,128]{2,1,0:T(8,128)(2,1)} %get-tuple-element.285), channel_id=1, source_target_pairs={{0,96},{1,97},{2,98},{3,99},{4,100},{5,101},{6,102},{7,103},{8,104... | collective-permute-start | bytes 1327112 | tf_op jit(solution)/shard_map/ppermute | solution.py:55
  283.4 24.0 %collective-permute-start.45 = (bf16[4,944,128]{2,1,0:T(8,128)(2,1)}, bf16[4,944,128]{2,1,0:T(8,128)(2,1)}, u32[]{:S(2)}, u32[]{:S(2)}) collective-permute-start(bf16[4,944,128]{2,1,0:T(8,128)(2,1)} %get-tuple-element.308), channel_id=1, source_target_pairs={{0,24},{1,25},{2,26},{3,27},{4,28},{5,29},{6,30},{7,31},{8,16},{9,... | collective-permute-start | bytes 2899976 | tf_op jit(solution)/shard_map/ppermute | solution.py:55
  285.8 22.1 %collective-permute-start.46 = (bf16[4,944,128]{2,1,0:T(8,128)(2,1)}, bf16[4,944,128]{2,1,0:T(8,128)(2,1)}, u32[]{:S(2)}, u32[]{:S(2)}) collective-permute-start(bf16[4,944,128]{2,1,0:T(8,128)(2,1)} %get-tuple-element.309), channel_id=1, source_target_pairs={{0,8},{1,9},{2,10},{3,11},{4,12},{5,13},{6,14},{7,15},{8,0},{9,1},... | collective-permute-start | bytes 2899976 | tf_op jit(solution)/shard_map/ppermute | solution.py:55
  285.9 21.5 %collective-permute-start.47 = (bf16[4,864,128]{2,1,0:T(8,128)(2,1)}, bf16[4,864,128]{2,1,0:T(8,128)(2,1)}, u32[]{:S(2)}, u32[]{:S(2)}) collective-permute-start(bf16[4,864,128]{2,1,0:T(8,128)(2,1)} %get-tuple-element.310), channel_id=1, source_target_pairs={{0,96},{1,97},{2,98},{3,99},{4,100},{5,101},{6,102},{7,103},{8,104... | collective-permute-start | bytes 2654216 | tf_op jit(solution)/shard_map/ppermute | solution.py:55
  287.2 20.2 %collective-permute-start.48 = (bf16[4,864,128]{2,1,0:T(8,128)(2,1)}, bf16[4,864,128]{2,1,0:T(8,128)(2,1)}, u32[]{:S(2)}, u32[]{:S(2)}) collective-permute-start(bf16[4,864,128]{2,1,0:T(8,128)(2,1)} %get-tuple-element.311), channel_id=1, source_target_pairs={{0,32},{1,33},{2,34},{3,35},{4,36},{5,37},{6,38},{7,39},{8,40},{9,... | collective-permute-start | bytes 2654216 | tf_op jit(solution)/shard_map/ppermute | solution.py:55
  293.1 30.9 %collective-permute-start.58 = (bf16[64,2688]{1,0:T(8,128)(2,1)S(1)}, bf16[64,2688]{1,0:T(8,128)(2,1)S(1)}, u32[]{:S(2)}, u32[]{:S(2)}) collective-permute-start(bf16[64,2688]{1,0:T(8,128)(2,1)S(1)} %get-tuple-element.344), channel_id=1, source_target_pairs={{0,4},{1,5},{2,6},{3,7},{4,0},{5,1},{6,2},{7,3},{8,12},{9,13},{10,... | collective-permute-start | bytes 1032200 | tf_op jit(solution)/shard_map/ppermute | solution.py:55
  (90 other events, 760.3 us)
Sparse Core Ops, SparseCore 0:
  20.5 38.2 all-gather.2
  70.3 78.3 all-gather.4
  190.2 93.1 reduce-scatter.2
  285.7 41.6 reduce-scatter.4

commit v6 on v5

--- a/solution.py
+++ b/solution.py
@@ -217,7 +217,7 @@
         out_specs=(ANY,) * 4,
         scratch_shapes=[pltpu.VMEM(v.shape, bf16) for v in more * 2] + [pltpu.SemaphoreType.DMA((4, 3))],
         input_output_aliases={i: i for i in range(4)},
-        compiler_params=params(58),
+        compiler_params=params(50),
     )(*values, *more)
 
 
@@ -241,7 +241,7 @@
         out_shape=tuple(jax.ShapeDtypeStruct(shape, bf16) for shape in outs),
         in_specs=blocks,
         out_specs=tuple(pl.BlockSpec(shape, lambda i: (0, 0)) for shape in outs),
-        compiler_params=params(58),
+        compiler_params=params(50),
     )(*a, *b)
     return out[:4], out[4:]
 
@@ -313,7 +313,7 @@
             pltpu.SemaphoreType.DMA((54,)),
         ],
         cost_estimate=cost(20 * half * wide * width, 10 * wide * width),
-        compiler_params=params(58),
+        compiler_params=params(50),
     )(w, *x, g0, g1)
 
 
@@ -360,7 +360,7 @@
         out_specs=(pl.BlockSpec((4, 3 * wide, 128), lambda i: (i, 0, 0)), block, block),
         scratch_shapes=[pltpu.VMEM((rows, wide), bf16)],
         cost_estimate=cost(14 * half * wide * width, 10 * wide * width),
-        compiler_params=params(58),
+        compiler_params=params(50),
     )(hidden, grads, *x, g0, g1, w.reshape(16, 3 * wide, 128))
 
 
@@ -444,7 +444,7 @@
             pltpu.SemaphoreType.DMA((3 + 12 * len(steps),)),
         ],
         cost_estimate=cost(rows * 512 * (ra + rb) * 2 * len(steps), 6 * rows * 2048),
-        compiler_params=params(58),
+        compiler_params=params(50),
     )(g, o, x, m)
 
 
@@ -574,7 +574,7 @@
         out_specs=(ANY, pl.BlockSpec((1, width), lambda i: (0, 0))),
         scratch_shapes=[pltpu.VMEM((half, width), bf16), pltpu.SemaphoreType.DMA((4,))],
         cost_estimate=cost(2 * size * total * width, 10 * total * width),
-        compiler_params=params(58),
+        compiler_params=params(50),
     )(g, w, x)
 
 
@@ -741,7 +741,7 @@
             pltpu.SemaphoreType.DMA((42,)),
         ],
         cost_estimate=cost(2 * size * total * width, 16 * total * width),
-        compiler_params=params(58),
+        compiler_params=params(50),
     )(*blocks, line, decay, gain)
 
 
@@ -818,7 +818,7 @@
             pltpu.SemaphoreType.DMA((6,)),
         ],
         cost_estimate=cost(2 * rows * (size + wide) * 1024, 8 * rows * 2048),
-        compiler_params=params(58),
+        compiler_params=params(50),
     )(*grads, w, q, k, v, gate, decay, gain, retained, *before)
 
 

time: 360 us -> 357 us (level)
  Pallas kernels: 114 us -> 107 us
  local copies, waits for them, and re-layouts: 11 us -> 17.6 us
    unnamed x98 -> x90, local copies, waits for them, and re-layouts: 8.15 us -> 13.9 us
  transfers between devices with their start and end apart: 66 -> 66, of which waited for: 25 -> 28; matrix products, arithmetic and copies ran while one was open for 6% -> 7% of each run, Pallas kernels for 27% -> 26%
where the time goes in v6:
time: 357 us; the launch traced here: 351 us
  waiting for transfers between devices  110 us (31%)
  Pallas kernels  107 us (30%)
  starting transfers between devices  75.6 us (21%)
  other arithmetic  24.5 us (7%)
  local copies, waits for them, and re-layouts  17.6 us (5%)
  between operations  16.7 us (5%)
    ppermute x62, waiting for transfers between devices, move(): return lax.ppermute(value, AXES, pairs)  102 us
    ppermute x62, starting transfers between devices, move(): return lax.ppermute(value, AXES, pairs)  75.3 us
    pallas_call x1, Pallas kernels, mixer_forward(): pl.pallas_call(mixer_kernel, grid=(2,), out_shape=(jax.ShapeDtypeStruct((...  18.9 us
    pallas_call x3, Pallas kernels, gradient_parts(): pl.pallas_call(functools.partial(parts_kernel, steps), grid=(1,), out_sha...  17.1 us
    pallas_call x2, Pallas kernels, mixer_backward(): pl.pallas_call(functools.partial(mixer_back_kernel, group), grid=(1,), ou...  15.3 us
    pallas_call x1, Pallas kernels, feed_forward_back(): pl.pallas_call(feed_kernel, out_shape=(jax.ShapeDtypeStruct((wide, 2 * ha...  14.7 us
    unnamed x90, local copies, waits for them, and re-layouts  13.9 us
    pallas_call x1, Pallas kernels, input_gradients(): pl.pallas_call(back_kernel, grid=(2,), out_shape=(jax.ShapeDtypeStruct((t...  13.5 us
  transfers between devices with their start and end apart: 66, of which 28 were waited for; matrix products, arithmetic and copies ran while one was open for 7% of the time, Pallas kernels for 26%

profile of v6, /device:TPU:0, one launch (start us, length us, event | category | flops | bytes accessed | tf_op | source)
XLA Modules:
  0.0 350.8 jit_solution(13306228840912234698)
XLA Ops:
  9.6 3.4 collective-permute-start
  31.5 7.4 %collective-permute-done.4 = bf16[864,128]{1,0:T(8,128)(2,1)S(1)} collective-permute-done((bf16[864,128]{1,0:T(8,128)(2,1)S(1)}, bf16[864,128]{1,0:T(8,128)(2,1)S(1)}, u32[]{:S(2)}, u32[]{:S(2)}) %collective-permute-start.4) | collective-permute-done | bytes 221216 | tf_op jit(solution)/shard_map/ppermute | solution.py:55
  51.6 8.6 %collective-permute-done.11.got_ref = bf16[64,2688]{1,0:T(8,128)(2,1)S(1)} collective-permute-done((bf16[64,2688]{1,0:T(8,128)(2,1)S(1)}, bf16[64,2688]{1,0:T(8,128)(2,1)S(1)}, u32[]{:S(2)}, u32[]{:S(2)}) %collective-permute-start.11) | collective-permute-done | bytes 344096 | tf_op jit(solution)/shard_map/ppermute | solution.py:55
  76.8 6.8 %collective-permute-done.14.refs_7_ = bf16[2,864,128]{2,1,0:T(8,128)(2,1)S(1)} collective-permute-done((bf16[2,864,128]{2,1,0:T(8,128)(2,1)}, bf16[2,864,128]{2,1,0:T(8,128)(2,1)S(1)}, u32[]{:S(2)}, u32[]{:S(2)}) %collective-permute-start.14) | collective-permute-done | bytes 442400 | tf_op jit(solution)/shard_map/ppermute | solution.py:55
  88.0 18.9 %shard_map.249 = (bf16[1808,2048]{1,0:T(8,128)(2,1)}, bf16[1024,2048]{1,0:T(8,128)(2,1)}, bf16[1024,256]{1,0:T(8,128)(2,1)S(1)}, bf16[1024,256]{1,0:T(8,128)(2,1...) custom-call(bf16[4,944,128]{2,1,0:T(8,128)(2,1)} %pad_maximum_fusion, ...), custom_call_target="tpu_custom_call" | custom-call | flops 7583301632 | bytes 33554432 | tf_op jit(solution)/shard_map/pallas_call | solution.py:705
  116.1 4.4 %collective-permute-done.20 = bf16[64,2048]{1,0:T(8,128)(2,1)S(1)} collective-permute-done((bf16[64,2048]{1,0:T(8,128)(2,1)S(1)}, bf16[64,2048]{1,0:T(8,128)(2,1)S(1)}, u32[]{:S(2)}, u32[]{:S(2)}) %collective-permute-start.20) | collective-permute-done | bytes 262176 | tf_op jit(solution)/shard_map/ppermute | solution.py:55
  125.5 11.3 %collective-permute-done.22 = bf16[128,2048]{1,0:T(8,128)(2,1)S(1)} collective-permute-done((bf16[128,2048]{1,0:T(8,128)(2,1)S(1)}, bf16[128,2048]{1,0:T(8,128)(2,1)S(1)}, u32[]{:S(2)}, u32[]{:S(2)}) %collective-permute-start.22) | collective-permute-done | bytes 524320 | tf_op jit(solution)/shard_map/ppermute | solution.py:55
  140.1 11.8 %collective-permute-done.24.x1_ref = bf16[128,2048]{1,0:T(8,128)(2,1)S(1)} collective-permute-done((bf16[128,2048]{1,0:T(8,128)(2,1)S(1)}, bf16[128,2048]{1,0:T(8,128)(2,1)S(1)}, u32[]{:S(2)}, u32[]{:S(2)}) %collective-permute-start.24) | collective-permute-done | bytes 524320 | tf_op jit(solution)/shard_map/ppermute | solution.py:55
  154.0 14.7 %shard_map.251 = (bf16[864,512]{1,0:T(8,128)(2,1)S(1)}, bf16[1728,512]{1,0:T(8,128)(2,1)}, f32[256,2048]{1,0:T(8,128)}, bf16[256,2048]{1,0:T(8,128)(2,1)S(1)}) custom-call(bf16[41472,128]{1,0:T(8,128)(2,1)} %all-gather.5.cloned.1.call-done.w_ref, bf16[128,2048]{1,0:T(8,128)(2,1)S(1)} %multiply_convert_fusion.1.x0_ref, ...), custom_call_target="tpu_custom_call" | custom-call | flops 9059696640 | bytes 17694720 | tf_op jit(solution)/shard_map/pallas_call | solution.py:300
  174.3 12.2 %shard_map.252 = (bf16[16,2592,128]{2,1,0:T(8,128)(2,1)}, bf16[256,2048]{1,0:T(8,128)(2,1)S(1)}, bf16[256,2048]{1,0:T(8,128)(2,1)}) custom-call(bf16[864,512]{1,0:T(8,128)(2,1)S(1)} %get-tuple-element.245.hidden_ref, bf16[1728,512]{1,0:T(8,128)(2,1)} %get-tuple-element.246.grads_ref, bf16[128,2048]{1,0:T(8,128)(2,1)S(1)} %multiply_convert_fusion.1.x0_ref, ...), custom_call_target="tpu_custom_call" | custom-call | flops 6341787648 | bytes 17694720 | tf_op jit(solution)/shard_map/pallas_call | solution.py:346
  198.4 10.4 %collective-permute-done.29.g1_ref = bf16[128,2048]{1,0:T(8,128)(2,1)S(1)} collective-permute-done((bf16[128,2048]{1,0:T(8,128)(2,1)S(1)}, bf16[128,2048]{1,0:T(8,128)(2,1)S(1)}, u32[]{:S(2)}, u32[]{:S(2)}) %collective-permute-start.29) | collective-permute-done | bytes 524320 | tf_op jit(solution)/shard_map/ppermute | solution.py:55
  212.7 7.6 %shard_map.253 = (bf16[1376,1024]{1,0:T(8,128)(2,1)}, f32[1,432]{1,0:T(1,128)S(1)}, bf16[1024,2048]{1,0:T(8,128)(2,1)}) custom-call(bf16[128,2048]{1,0:T(8,128)(2,1)S(1)} %get-tuple-element.252.g0_ref, bf16[128,2048]{1,0:T(8,128)(2,1)S(1)} %collective-permute-done.29.g1_ref, bf16[128,2048]{1,0:T(8,128)(2,1)S(1)} %collective-permute-done.31.g2_ref, ...), custom_call_target="tpu_custom_call" | custom-call | flops 1895825408 | bytes 8388608 | tf_op jit(solution)/shard_map/pallas_call | solution.py:802
  222.5 7.7 %shard_map.254 = (bf16[1376,1024]{1,0:T(8,128)(2,1)}, f32[1,432]{1,0:T(1,128)S(1)}, bf16[1024,2048]{1,0:T(8,128)(2,1)}) custom-call(bf16[128,2048]{1,0:T(8,128)(2,1)S(1)} %constant_dynamic-update-slice_fusion.2.g0_ref, bf16[128,2048]{1,0:T(8,128)(2,1)S(1)} %collective-permute-done.30.g1_ref, ...), custom_call_target="tpu_custom_call", output_to_operand_aliasing={{0}: (12, {}), {2}: (13, {})} | custom-call | flops 1895825408 | bytes 8388608 | tf_op jit(solution)/shard_map/pallas_call | solution.py:802
  230.1 4.8 %shard_map.255 = (bf16[2,944,128]{2,1,0:T(8,128)(2,1)S(1)}, bf16[2,944,128]{2,1,0:T(8,128)(2,1)S(1)}, bf16[2,864,128]{2,1,0:T(8,128)(2,1)}, bf16[2,864,128]{2,1,0:T(8,128)(2,1)S(1)}) custom-call(bf16[1376,1024]{1,0:T(8,128)(2,1)} %get-tuple-element.315.g_in.g_ref, bf16[432,1024]{1,0:T(8,128)(2,1)S(1)} %copy-done.2, ...), custom_call_target="tpu_custom_call" | custom-call | flops 1895825408 | bytes 12582912 | tf_op jit(solution)/shard_map/pallas_call | solution.py:433
  239.2 13.5 %shard_map.256 = (bf16[1024,2048]{1,0:T(8,128)(2,1)}, f32[1,2048]{1,0:T(1,128)S(1)}) custom-call(bf16[1376,1024]{1,0:T(8,128)(2,1)S(1)} %copy-done, bf16[1808,2048]{1,0:T(8,128)(2,1)} %get-tuple-element.258.w_ref, bf16[1024,2048]{1,0:T(8,128)(2,1)} %get-tuple-element.275.x_in.x_ref), custom_call_target="tpu_custom_call" | custom-call | flops 5771362304 | bytes 20971520 | tf_op jit(solution)/shard_map/pallas_call | solution.py:562
  254.1 7.9 %shard_map.257 = (bf16[4,944,128]{2,1,0:T(8,128)(2,1)S(1)}, bf16[4,864,128]{2,1,0:T(8,128)(2,1)S(1)}, bf16[4,944,128]{2,1,0:T(8,128)(2,1)}, bf16[4,864,128]{2,1,0:T(8,128)(2,1)S(1)}) custom-call(bf16[1376,1024]{1,0:T(8,128)(2,1)} %get-tuple-element.315.g_in.g_ref, bf16[432,1024]{1,0:T(8,128)(2,1)S(1)} %copy-done.3, ...), custom_call_target="tpu_custom_call" | custom-call | flops 3791650816 | bytes 12582912 | tf_op jit(solution)/shard_map/pallas_call | solution.py:433
  268.6 4.4 %shard_map.259 = (bf16[4,944,128]{2,1,0:T(8,128)(2,1)S(1)}, bf16[4,864,128]{2,1,0:T(8,128)(2,1)S(1)}) custom-call(bf16[1376,1024]{1,0:T(8,128)(2,1)} %get-tuple-element.315.g_in.g_ref, bf16[432,1024]{1,0:T(8,128)(2,1)S(1)} %copy-done.4, bf16[1024,2048]{1,0:T(8,128)(2,1)} %get-tuple-element.275.x_in.x_ref, bf16[1024,2048]{1,0:T(8,128)(2,1)} %get-tuple-element.276.m_in), custom_call_target="tpu_custom_call" | custom-call | flops 1895825408 | bytes 12582912 | tf_op jit(solution)/shard_map/pallas_call | solution.py:433
  273.9 7.7 %reduce-scatter.3.cloned.1.call-done.sum_ref = bf16[2592,128]{1,0:T(8,128)(2,1)} async-done(((bf16[41472,128]{1,0:T(8,128)(2,1)}), bf16[2592,128]{1,0:T(8,128)(2,1)}) %reduce-scatter.3.cloned.1.call-update) | async-done | bytes 663568 | tf_op jit(solution)/shard_map/reduce_scatter | solution.py:896
  285.7 3.2 collective-permute-start.49
  292.8 3.1 collective-permute-start.58
  296.0 9.6 %collective-permute-done.47.refs_4_ = bf16[4,864,128]{2,1,0:T(8,128)(2,1)S(1)} collective-permute-done((bf16[4,864,128]{2,1,0:T(8,128)(2,1)}, bf16[4,864,128]{2,1,0:T(8,128)(2,1)S(1)}, u32[]{:S(2)}, u32[]{:S(2)}) %collective-permute-start.47) | collective-permute-done | bytes 884768 | tf_op jit(solution)/shard_map/ppermute | solution.py:55
  306.5 3.6 %shard_map.260 = (bf16[944,128]{1,0:T(8,128)(2,1)S(1)}, bf16[944,128]{1,0:T(8,128)(2,1)S(1)}, bf16[944,128]{1,0:T(8,128)(2,1)S(1)}, bf16[944,128]{1,0:T(8,128)(2...) custom-call(bf16[4,944,128]{2,1,0:T(8,128)(2,1)} %copy-done.7, ...), custom_call_target="tpu_custom_call" | custom-call | tf_op jit(solution)/shard_map/pallas_call | solution.py:238
  329.9 3.1 collective-permute-start.61
  335.3 3.1 collective-permute-done.60
  (272 shorter events, 145.2 us)
Async XLA Ops:
  7.2 80.8 %all-gather.3.cloned.1.call-start = ((), (), s32[]{:S(2)}) async-start(), calls=%async_computation.2 | async-start | bytes 4718592 | tf_op jit(solution)/shard_map/all_gather | solution.py:875
  20.4 133.6 %all-gather.5.cloned.1.call-start = ((), (), s32[]{:S(2)}) async-start(), calls=%async_computation.3 | async-start | bytes 11280384 | tf_op jit(solution)/shard_map/all_gather | solution.py:879
  22.6 16.2 %collective-permute-start.1 = (bf16[944,128]{1,0:T(8,128)(2,1)S(1)}, bf16[944,128]{1,0:T(8,128)(2,1)S(1)}, u32[]{:S(2)}, u32[]{:S(2)}) collective-permute-start(bf16[944,128]{1,0:T(8,128)(2,1)S(1)} %get-tuple-element.195), channel_id=1, source_target_pairs={{0,32},{1,33},{2,34},{3,35},{4,36},{5,37},{6,38},{7,39},{8,40},{9,... | collective-permute-start | bytes 725000 | tf_op jit(solution)/shard_map/ppermute | solution.py:55
  24.1 14.7 %collective-permute-start.2 = (bf16[944,128]{1,0:T(8,128)(2,1)S(1)}, bf16[944,128]{1,0:T(8,128)(2,1)S(1)}, u32[]{:S(2)}, u32[]{:S(2)}) collective-permute-start(bf16[944,128]{1,0:T(8,128)(2,1)S(1)} %get-tuple-element.195), channel_id=1, source_target_pairs={{0,96},{1,97},{2,98},{3,99},{4,100},{5,101},{6,102},{7,103},{8,104... | collective-permute-start | bytes 725000 | tf_op jit(solution)/shard_map/ppermute | solution.py:55
  41.0 23.2 %collective-permute-start.7 = (bf16[4,944,128]{2,1,0:T(8,128)(2,1)}, bf16[4,944,128]{2,1,0:T(8,128)(2,1)S(1)}, u32[]{:S(2)}, u32[]{:S(2)}) collective-permute-start(bf16[4,944,128]{2,1,0:T(8,128)(2,1)} %pad_maximum_fusion.refs_0_), channel_id=1, source_target_pairs={{0,8},{1,9},{2,10},{3,11},{4,12},{5,13},{6,14},{7,15},{8,0},{9,1},... | collective-permute-start | bytes 2899976 | tf_op jit(solution)/shard_map/ppermute | solution.py:55
  41.6 22.7 %collective-permute-start.8 = (bf16[4,944,128]{2,1,0:T(8,128)(2,1)}, bf16[4,944,128]{2,1,0:T(8,128)(2,1)S(1)}, u32[]{:S(2)}, u32[]{:S(2)}) collective-permute-start(bf16[4,944,128]{2,1,0:T(8,128)(2,1)} %pad_maximum_fusion.refs_0_), channel_id=1, source_target_pairs={{0,24},{1,25},{2,26},{3,27},{4,28},{5,29},{6,30},{7,31},{8,16},{9,... | collective-permute-start | bytes 2899976 | tf_op jit(solution)/shard_map/ppermute | solution.py:55
  44.0 19.0 %collective-permute-start.9 = (bf16[4,864,128]{2,1,0:T(8,128)(2,1)}, bf16[4,864,128]{2,1,0:T(8,128)(2,1)S(1)}, u32[]{:S(2)}, u32[]{:S(2)}) collective-permute-start(bf16[4,864,128]{2,1,0:T(8,128)(2,1)} %pad_maximum_fusion.1.refs_5_), channel_id=1, source_target_pairs={{0,32},{1,33},{2,34},{3,35},{4,36},{5,37},{6,38},{7,39},{8,40},{9,... | collective-permute-start | bytes 2654216 | tf_op jit(solution)/shard_map/ppermute | solution.py:55
  45.2 19.1 %collective-permute-start.10 = (bf16[4,864,128]{2,1,0:T(8,128)(2,1)}, bf16[4,864,128]{2,1,0:T(8,128)(2,1)}, u32[]{:S(2)}, u32[]{:S(2)}) collective-permute-start(bf16[4,864,128]{2,1,0:T(8,128)(2,1)} %pad_maximum_fusion.1.refs_5_), channel_id=1, source_target_pairs={{0,96},{1,97},{2,98},{3,99},{4,100},{5,101},{6,102},{7,103},{8,104... | collective-permute-start | bytes 2654216 | tf_op jit(solution)/shard_map/ppermute | solution.py:55
  70.3 211.4 %reduce-scatter.3.cloned.1.call-start = ((), (), s32[]{:S(2)}) async-start(), calls=%async_computation.4 | async-start | bytes 11280384 | tf_op jit(solution)/shard_map/reduce_scatter | solution.py:896
  70.3 16.1 %collective-permute-start.16 = (bf16[128,2048]{1,0:T(8,128)(2,1)}, bf16[128,2048]{1,0:T(8,128)(2,1)S(1)}, u32[]{:S(2)}, u32[]{:S(2)}) collective-permute-start(bf16[128,2048]{1,0:T(8,128)(2,1)} %fusion), channel_id=1, source_target_pairs={{0,2},{1,3},{2,0},{3,1},{4,6},{5,7},{6,4},{7,5},{8,10},{9,11},{10,... | collective-permute-start | bytes 1572872 | tf_op jit(solution)/shard_map/ppermute | solution.py:55
  70.9 15.5 %collective-permute-start.12 = (bf16[2,944,128]{2,1,0:T(8,128)(2,1)}, bf16[2,944,128]{2,1,0:T(8,128)(2,1)S(1)}, u32[]{:S(2)}, u32[]{:S(2)}) collective-permute-start(bf16[2,944,128]{2,1,0:T(8,128)(2,1)} %copy-done.23), channel_id=1, source_target_pairs={{0,8},{1,9},{2,10},{3,11},{4,12},{5,13},{6,14},{7,15},{8,0},{9,1},... | collective-permute-start | bytes 1449992 | tf_op jit(solution)/shard_map/ppermute | solution.py:55
  71.0 15.5 %collective-permute-start.13 = (bf16[2,944,128]{2,1,0:T(8,128)(2,1)}, bf16[2,944,128]{2,1,0:T(8,128)(2,1)S(1)}, u32[]{:S(2)}, u32[]{:S(2)}) collective-permute-start(bf16[2,944,128]{2,1,0:T(8,128)(2,1)} %copy-done.22), channel_id=1, source_target_pairs={{0,24},{1,25},{2,26},{3,27},{4,28},{5,29},{6,30},{7,31},{8,16},{9,... | collective-permute-start | bytes 1449992 | tf_op jit(solution)/shard_map/ppermute | solution.py:55
  87.4 19.6 %collective-permute-start.17 = (bf16[256,2048]{1,0:T(8,128)(2,1)}, bf16[256,2048]{1,0:T(8,128)(2,1)}, u32[]{:S(2)}, u32[]{:S(2)}) collective-permute-start(bf16[256,2048]{1,0:T(8,128)(2,1)} %constant_dynamic-update-slice_fusion.g0_ref), channel_id=1, source_target_pairs={{0,1},{1,0},{2,3},{3,2},{4,5},{5,4},{6,7},{7,6},{8,9},{9,8},{10,11... | collective-permute-start | bytes 3145736 | tf_op jit(solution)/shard_map/ppermute | solution.py:55
  188.5 152.1 %reduce-scatter.5.cloned.1.call-start = ((), (), s32[]{:S(2)}) async-start(), calls=%async_computation.5 | async-start | bytes 4718592 | tf_op jit(solution)/shard_map/reduce_scatter | solution.py:953
  195.0 15.3 %collective-permute-start.30 = (bf16[128,2048]{1,0:T(8,128)(2,1)S(1)}, bf16[128,2048]{1,0:T(8,128)(2,1)S(1)}, u32[]{:S(2)}, u32[]{:S(2)}) collective-permute-start(bf16[128,2048]{1,0:T(8,128)(2,1)S(1)} %get-tuple-element.252.g0_ref), channel_id=1, source_target_pairs={{0,6},{1,7},{2,4},{3,5},{4,2},{5,3},{6,0},{7,1},{8,14},{9,15},{10,... | collective-permute-start | bytes 1572872 | tf_op jit(solution)/shard_map/ppermute | solution.py:55
  235.0 28.0 %collective-permute-start.39 = (bf16[2,944,128]{2,1,0:T(8,128)(2,1)S(1)}, bf16[2,944,128]{2,1,0:T(8,128)(2,1)S(1)}, u32[]{:S(2)}, u32[]{:S(2)}) collective-permute-start(bf16[2,944,128]{2,1,0:T(8,128)(2,1)S(1)} %get-tuple-element.282), channel_id=1, source_target_pairs={{0,8},{1,9},{2,10},{3,11},{4,12},{5,13},{6,14},{7,15},{8,0},{9,1},... | collective-permute-start | bytes 1449992 | tf_op jit(solution)/shard_map/ppermute | solution.py:55
  235.8 27.2 %collective-permute-start.40 = (bf16[2,944,128]{2,1,0:T(8,128)(2,1)S(1)}, bf16[2,944,128]{2,1,0:T(8,128)(2,1)S(1)}, u32[]{:S(2)}, u32[]{:S(2)}) collective-permute-start(bf16[2,944,128]{2,1,0:T(8,128)(2,1)S(1)} %get-tuple-element.283), channel_id=1, source_target_pairs={{0,24},{1,25},{2,26},{3,27},{4,28},{5,29},{6,30},{7,31},{8,16},{9,... | collective-permute-start | bytes 1449992 | tf_op jit(solution)/shard_map/ppermute | solution.py:55
  237.6 25.3 %collective-permute-start.41 = (bf16[2,864,128]{2,1,0:T(8,128)(2,1)}, bf16[2,864,128]{2,1,0:T(8,128)(2,1)S(1)}, u32[]{:S(2)}, u32[]{:S(2)}) collective-permute-start(bf16[2,864,128]{2,1,0:T(8,128)(2,1)} %get-tuple-element.284), channel_id=1, source_target_pairs={{0,32},{1,33},{2,34},{3,35},{4,36},{5,37},{6,38},{7,39},{8,40},{9,... | collective-permute-start | bytes 1327112 | tf_op jit(solution)/shard_map/ppermute | solution.py:55
  237.9 25.0 %collective-permute-start.42 = (bf16[2,864,128]{2,1,0:T(8,128)(2,1)S(1)}, bf16[2,864,128]{2,1,0:T(8,128)(2,1)S(1)}, u32[]{:S(2)}, u32[]{:S(2)}) collective-permute-start(bf16[2,864,128]{2,1,0:T(8,128)(2,1)S(1)} %get-tuple-element.285), channel_id=1, source_target_pairs={{0,96},{1,97},{2,98},{3,99},{4,100},{5,101},{6,102},{7,103},{8,104... | collective-permute-start | bytes 1327112 | tf_op jit(solution)/shard_map/ppermute | solution.py:55
  281.7 24.0 %collective-permute-start.45 = (bf16[4,944,128]{2,1,0:T(8,128)(2,1)}, bf16[4,944,128]{2,1,0:T(8,128)(2,1)}, u32[]{:S(2)}, u32[]{:S(2)}) collective-permute-start(bf16[4,944,128]{2,1,0:T(8,128)(2,1)} %get-tuple-element.308), channel_id=1, source_target_pairs={{0,24},{1,25},{2,26},{3,27},{4,28},{5,29},{6,30},{7,31},{8,16},{9,... | collective-permute-start | bytes 2899976 | tf_op jit(solution)/shard_map/ppermute | solution.py:55
  284.1 21.8 %collective-permute-start.46 = (bf16[4,944,128]{2,1,0:T(8,128)(2,1)S(1)}, bf16[4,944,128]{2,1,0:T(8,128)(2,1)}, u32[]{:S(2)}, u32[]{:S(2)}) collective-permute-start(bf16[4,944,128]{2,1,0:T(8,128)(2,1)S(1)} %copy-done.9), channel_id=1, source_target_pairs={{0,8},{1,9},{2,10},{3,11},{4,12},{5,13},{6,14},{7,15},{8,0},{9,1},... | collective-permute-start | bytes 2899976 | tf_op jit(solution)/shard_map/ppermute | solution.py:55
  284.1 21.4 %collective-permute-start.47 = (bf16[4,864,128]{2,1,0:T(8,128)(2,1)}, bf16[4,864,128]{2,1,0:T(8,128)(2,1)S(1)}, u32[]{:S(2)}, u32[]{:S(2)}) collective-permute-start(bf16[4,864,128]{2,1,0:T(8,128)(2,1)} %copy-done.12), channel_id=1, source_target_pairs={{0,96},{1,97},{2,98},{3,99},{4,100},{5,101},{6,102},{7,103},{8,104... | collective-permute-start | bytes 2654216 | tf_op jit(solution)/shard_map/ppermute | solution.py:55
  285.5 20.0 %collective-permute-start.48 = (bf16[4,864,128]{2,1,0:T(8,128)(2,1)}, bf16[4,864,128]{2,1,0:T(8,128)(2,1)}, u32[]{:S(2)}, u32[]{:S(2)}) collective-permute-start(bf16[4,864,128]{2,1,0:T(8,128)(2,1)} %copy-done.11), channel_id=1, source_target_pairs={{0,32},{1,33},{2,34},{3,35},{4,36},{5,37},{6,38},{7,39},{8,40},{9,... | collective-permute-start | bytes 2654216 | tf_op jit(solution)/shard_map/ppermute | solution.py:55
  292.8 27.9 %collective-permute-start.58 = (bf16[64,2688]{1,0:T(8,128)(2,1)}, bf16[64,2688]{1,0:T(8,128)(2,1)S(1)}, u32[]{:S(2)}, u32[]{:S(2)}) collective-permute-start(bf16[64,2688]{1,0:T(8,128)(2,1)} %get-tuple-element.344), channel_id=1, source_target_pairs={{0,4},{1,5},{2,6},{3,7},{4,0},{5,1},{6,2},{7,3},{8,12},{9,13},{10,... | collective-permute-start | bytes 1032200 | tf_op jit(solution)/shard_map/ppermute | solution.py:55
  (86 other events, 720.8 us)
Sparse Core Ops, SparseCore 0:
  20.5 38.1 all-gather.2
  70.4 78.2 all-gather.4
  188.6 92.9 reduce-scatter.2
  284.0 42.1 reduce-scatter.4
